TPU v7x, 128 devices: a whole 4x4x4 slice. The times are simulated.
128 devices in a mesh: row: 16 (over x, y), col: 8 (over z, core).
Axes of the slice: x: 4, y: 4, z: 4, core: 2. Of those that a mesh axis runs over, the one named last changes fastest.
Arguments:
- inputs: bfloat16 [512, 10240], P('col', 'row'), may hold values from -6 to 6
- cotangent: bfloat16 [512, 10240], P('col', 'row'), may hold values from -1.5 to 1.5
- w_in: bfloat16 [10240, 40960], P('row', 'col'), may hold values from -0.0625 to 0.0625
- w_out: bfloat16 [40960, 10240], P('col', 'row'), may hold values from -0.03125 to 0.03125
Outputs:
- grad_inputs: bfloat16 [512, 10240], P('col', 'row')
- grad_w_in: bfloat16 [10240, 40960], P('row', 'col')
- grad_w_out: bfloat16 [40960, 10240], P('col', 'row')
All inputs are finite; a program needn't handle non-finite values.
Results may differ from a plain program's by a relative error of at most 0.028.
Values may be sent and summed in bfloat16 or wider, within the bound.
No kernel may reach another device: no remote copies, remote signals or barrier semaphores. Data moves between devices by JAX's collectives and lax.ppermute only.
A program may use at most 128 MiB of HBM per device.

v0:
```python
import math

import jax
import jax.numpy as jnp
from jax import lax
from jax.sharding import PartitionSpec as P


def gelu_parts(hidden):
    normal_cdf = 0.5 * (1.0 + jax.scipy.special.erf(hidden / math.sqrt(2.0)))
    density = jnp.exp(-0.5 * hidden * hidden) / math.sqrt(2.0 * math.pi)
    return (hidden * normal_cdf, normal_cdf + hidden * density)


def shards(inputs, cotangent, w_in, w_out):
    inputs_all, cotangent_all = (
        lax.all_gather(inputs, "col", axis=0, tiled=True),
        lax.all_gather(cotangent, "col", axis=0, tiled=True),
    )
    hidden = lax.psum_scatter(
        jnp.dot(inputs_all, w_in, preferred_element_type=jnp.float32).astype(jnp.bfloat16),
        "row",
        scatter_dimension=0,
        tiled=True,
    ).astype(jnp.float32)
    rows_grad = cotangent_all
    grad_act = lax.psum_scatter(
        lax.dot_general(
            rows_grad, w_out, (((1,), (1,)), ((), ())), preferred_element_type=jnp.float32
        ).astype(jnp.bfloat16),
        "row",
        scatter_dimension=0,
        tiled=True,
    ).astype(jnp.float32)
    activated, derivative = gelu_parts(hidden)
    activated_local = activated.astype(jnp.bfloat16)
    grad_hidden_local = (grad_act * derivative).astype(jnp.bfloat16)
    rows_grad = cotangent_all
    weight_total = lax.dot_general(
        lax.all_gather(activated_local, "row", axis=0, tiled=True),
        rows_grad,
        (((0,), (0,)), ((), ())),
        preferred_element_type=jnp.float32,
    )
    grad_w_out = weight_total.astype(jnp.bfloat16)
    grad_hidden_all = lax.all_gather(grad_hidden_local, "row", axis=0, tiled=True)
    grad_w_in = lax.dot_general(
        inputs_all, grad_hidden_all, (((0,), (0,)), ((), ())), preferred_element_type=jnp.float32
    ).astype(jnp.bfloat16)
    grad_inputs = lax.psum_scatter(
        lax.dot_general(
            grad_hidden_all, w_in, (((1,), (1,)), ((), ())), preferred_element_type=jnp.float32
        ).astype(jnp.bfloat16),
        "col",
        scatter_dimension=0,
        tiled=True,
    )
    return (grad_inputs, grad_w_in, grad_w_out)


def solution(mesh):
    in_specs = (P("col", "row"), P("col", "row"), P("row", "col"), P("col", "row"))
    out_specs = (P("col", "row"), P("row", "col"), P("col", "row"))
    return jax.shard_map(shards, mesh=mesh, in_specs=in_specs, out_specs=out_specs, check_vma=False)
```

profile of v0, /device:TPU:0, one launch (start us, length us, event | category | flops | bytes accessed | tf_op | source)
XLA Modules:
  0.0 350.2 jit_solution(8418654854700780503)
XLA Ops:
  7.2 0.0 reduce-scatter.4.cloned.1.call-start
  7.2 14.7 %all_gather.12 = bf16[512,640]{1,0:T(8,128)(2,1)S(1)} all-gather(bf16[64,640]{1,0:T(8,128)(2,1)} %param.5), channel_id=1, replica_groups=mesh['row'=16,'col'=8] {'col'}, dimensions={0}, use_global_device_ids=true | all-gather | bytes 737280 | tf_op jit(solution)/shard_map/all_gather | solution.py:18
  22.0 0.0 copy-start
  22.0 8.9 %convolution_convert_fusion.3 = bf16[512,5120]{1,0:T(8,128)(2,1)} fusion(bf16[512,640]{1,0:T(8,128)(2,1)S(1)} %all_gather.12, bf16[5120,640]{1,0:T(8,128)(2,1)} %param.7), kind=kOutput, calls=%fused_computation.3 | convolution fusion | flops 3358064640 | bytes 12451840 | tf_op jit(solution)/shard_map/dot_general | solution.py:28
  30.8 0.0 reduce-scatter.4.cloned.1.call-update
  30.8 0.0 reduce-scatter.6.cloned.1.call-start
  30.9 0.0 copy-done
  30.9 13.2 %all_gather.13 = bf16[512,640]{1,0:T(8,128)(2,1)S(1)} all-gather(bf16[64,640]{1,0:T(8,128)(2,1)S(1)} %copy-done), channel_id=1, replica_groups=mesh['row'=16,'col'=8] {'col'}, dimensions={0}, use_global_device_ids=true | all-gather | bytes 737280 | tf_op jit(solution)/shard_map/all_gather | solution.py:17
  44.2 8.8 %convolution_convert_fusion.2 = bf16[512,5120]{1,0:T(8,128)(2,1)} fusion(bf16[512,640]{1,0:T(8,128)(2,1)S(1)} %all_gather.13, bf16[640,5120]{1,0:T(8,128)(2,1)} %param.6), kind=kOutput, calls=%fused_computation.2 | convolution fusion | flops 3358064640 | bytes 12451840 | tf_op jit(solution)/shard_map/dot_general | solution.py:21
  52.9 0.0 reduce-scatter.6.cloned.1.call-update
  53.0 0.0 all-gather.3.cloned.1.call-start
  53.0 58.0 %reduce-scatter.4.cloned.1.call-done = bf16[32,5120]{1,0:T(8,128)(2,1)} async-done(((bf16[512,5120]{1,0:T(8,128)(2,1)}), bf16[32,5120]{1,0:T(8,128)(2,1)}) %reduce-scatter.4.cloned.1.call-update) | async-done | bytes 327696 | tf_op jit(solution)/shard_map/reduce_scatter | solution.py:27
  111.0 82.2 %reduce-scatter.6.cloned.1.call-done = bf16[32,5120]{1,0:T(8,128)(2,1)} async-done(((bf16[512,5120]{1,0:T(8,128)(2,1)}), bf16[32,5120]{1,0:T(8,128)(2,1)}) %reduce-scatter.6.cloned.1.call-update) | async-done | bytes 327696 | tf_op jit(solution)/shard_map/reduce_scatter | solution.py:20
  193.2 2.2 fusion.9
  195.5 0.0 all-gather.3.cloned.1.call-update
  195.5 0.0 all-gather.5.cloned.1.call-start
  195.5 0.5 all-gather.5.cloned.1.call-update
  196.1 0.2 reduce-scatter.8.cloned.1.call-start
  196.3 55.4 %all-gather.3.cloned.1.call-done = bf16[512,5120]{1,0:T(8,128)(2,1)} async-done(((bf16[32,5120]{1,0:T(8,128)(2,1)}), bf16[512,5120]{1,0:T(8,128)(2,1)}) %all-gather.3.cloned.1.call-update) | async-done | bytes 5242896 | tf_op jit(solution)/shard_map/all_gather | solution.py:46
  251.7 9.5 %convolution_convert_fusion.4 = bf16[512,640]{1,0:T(8,128)(2,1)} fusion(bf16[512,5120]{1,0:T(8,128)(2,1)} %all-gather.3.cloned.1.call-done, bf16[640,5120]{1,0:T(8,128)(2,1)} %param.6), kind=kOutput, calls=%fused_computation.5 | convolution fusion | flops 3355770880 | bytes 12451840 | tf_op jit(solution)/shard_map/dot_general | solution.py:51
  261.2 0.0 reduce-scatter.8.cloned.1.call-update
  261.2 9.8 %fusion = bf16[640,5120]{0,1:T(8,128)(2,1)} fusion(bf16[512,5120]{1,0:T(8,128)(2,1)} %all-gather.3.cloned.1.call-done, bf16[512,640]{1,0:T(8,128)(2,1)S(1)} %all_gather.13), kind=kOutput, calls=%fused_computation.4 | convolution fusion | flops 3358720000 | bytes 12451840 | tf_op jit(solution)/shard_map/dot_general | solution.py:47
  271.0 9.6 %copy.7 = bf16[640,5120]{1,0:T(8,128)(2,1)} copy(bf16[640,5120]{0,1:T(8,128)(2,1)} %fusion) | data formatting | bytes 13107200
  280.6 29.2 %all-gather.5.cloned.1.call-done = bf16[512,5120]{1,0:T(8,128)(2,1)} async-done(((bf16[32,5120]{1,0:T(8,128)(2,1)}), bf16[512,5120]{1,0:T(8,128)(2,1)}) %all-gather.5.cloned.1.call-update) | async-done | bytes 5242896 | tf_op jit(solution)/shard_map/all_gather | solution.py:40
  309.7 9.6 %convolution_convert_fusion = bf16[5120,640]{1,0:T(8,128)(2,1)} fusion(bf16[512,5120]{1,0:T(8,128)(2,1)} %all-gather.5.cloned.1.call-done, bf16[512,640]{1,0:T(8,128)(2,1)S(1)} %all_gather.12), kind=kOutput, calls=%fused_computation | convolution fusion | flops 3358720000 | bytes 12451840 | tf_op jit(solution)/shard_map/dot_general | solution.py:39
  319.3 24.4 %reduce-scatter.8.cloned.1.call-done = bf16[64,640]{1,0:T(8,128)(2,1)} async-done(((bf16[512,640]{1,0:T(8,128)(2,1)}), bf16[64,640]{1,0:T(8,128)(2,1)}) %reduce-scatter.8.cloned.1.call-update) | async-done | bytes 81936 | tf_op jit(solution)/shard_map/reduce_scatter | solution.py:50
Async XLA Ops:
  7.2 103.9 %reduce-scatter.4.cloned.1.call-start = ((), (), s32[]{:S(2)}) async-start(), calls=%async_computation.3 | async-start | bytes 5570560 | tf_op jit(solution)/shard_map/reduce_scatter | solution.py:27
  22.0 8.9 %copy-start = (bf16[64,640]{1,0:T(8,128)(2,1)S(1)}, bf16[64,640]{1,0:T(8,128)(2,1)}, u32[]{:S(2)}) copy-start(bf16[64,640]{1,0:T(8,128)(2,1)} %param.4) | copy-start | bytes 245764
  30.8 162.4 %reduce-scatter.6.cloned.1.call-start = ((), (), s32[]{:S(2)}) async-start(), calls=%async_computation.4 | async-start | bytes 5570560 | tf_op jit(solution)/shard_map/reduce_scatter | solution.py:20
  53.0 198.7 %all-gather.3.cloned.1.call-start = ((), (), s32[]{:S(2)}) async-start(), calls=%async_computation.5 | async-start | bytes 5570560 | tf_op jit(solution)/shard_map/all_gather | solution.py:46
  195.5 114.2 %all-gather.5.cloned.1.call-start = ((), (), s32[]{:S(2)}) async-start(), calls=%async_computation.7 | async-start | bytes 5570560 | tf_op jit(solution)/shard_map/all_gather | solution.py:40
  196.1 147.6 %reduce-scatter.8.cloned.1.call-start = ((), (), s32[]{:S(2)}) async-start(), calls=%async_computation.6 | async-start | bytes 737280 | tf_op jit(solution)/shard_map/reduce_scatter | solution.py:50
Sparse Core Ops, SparseCore 0:
  31.0 80.0 reduce-scatter.3
  115.0 78.2 reduce-scatter.5
  196.0 55.6 all-gather.2
  253.7 55.9 all-gather.4
  312.5 31.0 reduce-scatter.7
where the time goes:
time: 351 us; the launch traced here: 350 us
  waiting for transfers between devices  250 us (71%)
  matrix products  46.5 us (13%)
  blocking collectives  28 us (8%)
  between operations  13.8 us (4%)
  local copies, waits for them, and re-layouts  9.57 us (3%)
    reduce_scatter x1, waiting for transfers between devices, shards(): lax.psum_scatter(jnp.dot(inputs_all, w_in, preferred_element_type=jnp.flo...  82.2 us
    reduce_scatter x1, waiting for transfers between devices, shards(): lax.psum_scatter(lax.dot_general(rows_grad, w_out, (((1,), (1,)), ((), ()...  58 us
    all_gather x1, waiting for transfers between devices, shards(): lax.all_gather(grad_hidden_local, 'row', axis=0, tiled=True)  55.4 us
    all_gather x1, waiting for transfers between devices, shards(): lax.all_gather(activated_local, 'row', axis=0, tiled=True)  29.2 us
    reduce_scatter x1, waiting for transfers between devices, shards(): lax.psum_scatter(lax.dot_general(grad_hidden_all, w_in, (((1,), (1,)), ((...  24.4 us
    all_gather x1, blocking collectives, shards(): lax.all_gather(cotangent, 'col', axis=0, tiled=True)  14.7 us
    all_gather x1, blocking collectives, shards(): lax.all_gather(inputs, 'col', axis=0, tiled=True)  13.2 us
    dot_general x1, matrix products, shards(): lax.dot_general(inputs_all, grad_hidden_all, (((0,), (0,)), ((), ())), pr...  9.76 us
  transfers between devices with their start and end apart: 5, of which 5 were waited for; matrix products, arithmetic and copies ran while one was open for 13% of the time, Pallas kernels for 0%

commit v1 on v0

v1 whole, which is shorter than its diff:
```python
import functools
import math

import jax
import jax.numpy as jnp
from jax import lax
from jax.experimental import pallas as pl
from jax.experimental.pallas import tpu as pltpu
from jax.sharding import PartitionSpec as P

N_X, N_Y, N_Z, N_C = 4, 4, 4, 2
TOK, WID, FFL = 512, 640, 5120
CHUNKS = (2560, 2560)
TILE = 512
AXES = ("row", "col")
F32, BF16 = jnp.float32, jnp.bfloat16


def neighbours(step, first):
    pairs = []
    for x in range(N_X):
        for y in range(N_Y):
            for z in range(N_Z):
                for c in range(N_C):
                    along_x = (c == 0) == first
                    nx = (x + step * along_x) % N_X
                    ny = (y + step * (not along_x)) % N_Y
                    here, there = ((a * N_Y + b) * N_Z + z for a, b in ((x, y), (nx, ny)))
                    pairs.append((here * N_C + c, there * N_C + c))
    return pairs


def hop(value, step, first):
    return lax.ppermute(value, AXES, neighbours(step, first))


def add(*terms):
    total = terms[0].astype(F32)
    for term in terms[1:]:
        total = total + term.astype(F32)
    return total


def gelu_parts(hidden):
    normal_cdf = 0.5 * (1.0 + jax.scipy.special.erf(hidden / math.sqrt(2.0)))
    density = jnp.exp(-0.5 * hidden * hidden) / math.sqrt(2.0 * math.pi)
    return (hidden * normal_cdf, normal_cdf + hidden * density)


def to_relative(order_ref, source_ref, target_ref):
    for block in range(16):
        start = pl.multiple_of(order_ref[block] * 32, 32)
        target_ref[block * 32 : (block + 1) * 32, :] = source_ref[pl.ds(start, 32), :]


def partial_kernel(order_ref, x_ref, c_ref, wi_ref, wo_ref, h2_ref, g2_ref, p1_ref, p3_ref, p0_ref, xs, cs):
    @pl.when(pl.program_id(0) == 0)
    def _():
        to_relative(order_ref, x_ref, xs)
        to_relative(order_ref, c_ref, cs)

    hidden = jnp.dot(xs[...], wi_ref[...], preferred_element_type=F32).astype(BF16)
    grad = lax.dot_general(
        cs[...], wo_ref[...], (((1,), (1,)), ((), ())), preferred_element_type=F32
    ).astype(BF16)
    p0_ref[0], p0_ref[1] = hidden[0:128], grad[0:128]
    p1_ref[0], p1_ref[1] = hidden[128:256], grad[128:256]
    h2_ref[...], g2_ref[...] = hidden[256:384], grad[256:384]
    p3_ref[0], p3_ref[1] = hidden[384:512], grad[384:512]


def partials(order, x_all, c_all, w_in, w_out, start, size):
    tiles, base = size // TILE, start // TILE
    pair = jax.ShapeDtypeStruct((2, 128, size), BF16)
    one = jax.ShapeDtypeStruct((128, size), BF16)
    pair_spec = pl.BlockSpec((2, 128, TILE), lambda i: (0, 0, i))
    one_spec = pl.BlockSpec((128, TILE), lambda i: (0, i))
    whole = pl.BlockSpec((TOK, WID), lambda i: (0, 0))
    return pl.pallas_call(
        partial_kernel,
        grid=(tiles,),
        out_shape=(one, one, pair, pair, pair),
        in_specs=[
            pl.BlockSpec(memory_space=pltpu.SMEM),
            whole,
            whole,
            pl.BlockSpec((WID, TILE), lambda i: (0, base + i)),
            pl.BlockSpec((TILE, WID), lambda i: (base + i, 0)),
        ],
        out_specs=(one_spec, one_spec, pair_spec, pair_spec, pair_spec),
        scratch_shapes=[pltpu.VMEM((TOK, WID), BF16), pltpu.VMEM((TOK, WID), BF16)],
        compiler_params=pltpu.CompilerParams(vmem_limit_bytes=32 * 2**20),
        cost_estimate=pl.CostEstimate(
            flops=4 * TOK * WID * size, bytes_accessed=4 * (TOK + WID) * size, transcendentals=0
        ),
        name="partials",
    )(order, x_all, c_all, w_in, w_out)


def grads_kernel(last, order_ref, x_ref, c_ref, wi_ref, o0_ref, o1_ref, o3_ref, a2_ref, b2_ref, *rest):
    gi_ref, gwi_ref, gwo_ref, xt, cs, total = rest[-6:]
    tile = pl.program_id(0)

    @pl.when(tile == 0)
    def _():
        to_relative(order_ref, c_ref, cs)
        to_relative(order_ref, x_ref, xt)
        total[...] = rest[0][...] if len(rest) > 6 else jnp.zeros_like(total)

    act = jnp.concatenate([o0_ref[0], o1_ref[0], a2_ref[...], o3_ref[0]], axis=0)
    grad = jnp.concatenate([o0_ref[1], o1_ref[1], b2_ref[...], o3_ref[1]], axis=0)
    total[...] += lax.dot_general(grad, wi_ref[...], (((1,), (1,)), ((), ())), preferred_element_type=F32)
    gwi_ref[...] = lax.dot_general(
        xt[...], grad, (((0,), (0,)), ((), ())), preferred_element_type=F32
    ).astype(BF16)
    gwo_ref[...] = lax.dot_general(
        act, cs[...], (((0,), (0,)), ((), ())), preferred_element_type=F32
    ).astype(BF16)

    @pl.when(tile == pl.num_programs(0) - 1)
    def _():
        if last:
            for block in range(16):
                start = pl.multiple_of(order_ref[block] * 32, 32)
                gi_ref[pl.ds(start, 32), :] = total[block * 32 : (block + 1) * 32, :].astype(BF16)
        else:
            gi_ref[...] = total[...]


def grads(order, x_all, c_all, w_in, gathered, before, start, size, last):
    tiles, base = size // TILE, start // TILE
    o0, o1, o3, a2, b2 = gathered
    pair_spec = pl.BlockSpec((2, 128, TILE), lambda i: (0, 0, i))
    one_spec = pl.BlockSpec((128, TILE), lambda i: (0, i))
    whole = pl.BlockSpec((TOK, WID), lambda i: (0, 0))
    any_spec = pl.BlockSpec(memory_space=pl.ANY)
    return pl.pallas_call(
        functools.partial(grads_kernel, last),
        grid=(tiles,),
        out_shape=(
            jax.ShapeDtypeStruct((TOK, WID), BF16 if last else F32),
            jax.ShapeDtypeStruct((WID, FFL), BF16),
            jax.ShapeDtypeStruct((FFL, WID), BF16),
        ),
        in_specs=[
            pl.BlockSpec(memory_space=pltpu.SMEM),
            whole,
            whole,
            pl.BlockSpec((WID, TILE), lambda i: (0, base + i)),
            pair_spec,
            pair_spec,
            pair_spec,
            one_spec,
            one_spec,
        ]
        + [whole, any_spec, any_spec][: len(before)],
        out_specs=(
            whole,
            pl.BlockSpec((WID, TILE), lambda i: (0, base + i)),
            pl.BlockSpec((TILE, WID), lambda i: (base + i, 0)),
        ),
        scratch_shapes=[
            pltpu.VMEM((TOK, WID), BF16),
            pltpu.VMEM((TOK, WID), BF16),
            pltpu.VMEM((TOK, WID), F32),
        ],
        input_output_aliases={10: 1, 11: 2} if before else {},
        compiler_params=pltpu.CompilerParams(vmem_limit_bytes=40 * 2**20),
        cost_estimate=pl.CostEstimate(
            flops=6 * TOK * WID * size, bytes_accessed=(4 * TOK + 6 * WID) * size, transcendentals=0
        ),
        name="grads",
    )(order, x_all, c_all, w_in, o0, o1, o3, a2, b2, *before)


def reduce_ring(h2, g2, p1, p3, p0, first):
    from_left = hop(h2, 1, first)
    from_right = hop(g2, -1, first)
    right = jnp.stack([add(p1[0], from_left).astype(BF16), p1[1]])
    left = jnp.stack([p3[0], add(p3[1], from_right).astype(BF16)])
    return add(p0, hop(right, 1, first), hop(left, -1, first))


def gather_ring(own, first):
    from_left = hop(own, 1, first)
    from_right = hop(own, -1, first)
    act = hop(from_left[0], 1, first)
    grad = hop(from_right[1], -1, first)
    return own, from_right, act, grad, from_left


def shards(inputs, cotangent, w_in, w_out):
    row, col = lax.axis_index("row"), lax.axis_index("col")
    x, y, core = row // N_Y, row % N_Y, col % N_C
    o = jnp.arange(16, dtype=jnp.int32)
    ox = jnp.where(core == 0, o // 4, o % 4)
    oy = jnp.where(core == 0, o % 4, o // 4)
    order = ((x + ox) % N_X) * N_Y + (y + oy) % N_Y

    x_all = lax.all_gather(inputs, "col", axis=0, tiled=True)
    c_all = lax.all_gather(cotangent, "col", axis=0, tiled=True)

    gathered = []
    start = 0
    for size in CHUNKS:
        h2, g2, p1, p3, p0 = partials(order, x_all, c_all, w_in, w_out, start, size)
        q = reduce_ring(h2, g2, p1, p3, p0, True).astype(BF16)
        b = [q[:, 32 * i : 32 * (i + 1)] for i in range(4)]
        hidden, grad_act = reduce_ring(b[2][0], b[2][1], b[1], b[3], b[0], False)
        activated, derivative = gelu_parts(hidden)
        own = jnp.stack([activated.astype(BF16), (grad_act * derivative).astype(BF16)])
        b0, b1, act, grad, b3 = gather_ring(own, False)
        quarter = jnp.concatenate([b0, b1, jnp.stack([act, grad]), b3], axis=1)
        o0, o1, act, grad, o3 = gather_ring(quarter, True)
        gathered.append((o0, o1, o3, act, grad))
        start += size

    before = ()
    start = 0
    for i, size in enumerate(CHUNKS):
        before = grads(
            order, x_all, c_all, w_in, gathered[i], before, start, size, i == len(CHUNKS) - 1
        )
        start += size
    gi, gwi, gwo = before
    parts = lax.all_to_all(gi.reshape(8, 64, WID), "col", 0, 0)
    gi = jnp.sum(parts.astype(F32), axis=0).astype(BF16)
    return gi, gwi, gwo


def solution(mesh):
    in_specs = (P("col", "row"), P("col", "row"), P("row", "col"), P("col", "row"))
    out_specs = (P("col", "row"), P("row", "col"), P("col", "row"))
    return jax.shard_map(shards, mesh=mesh, in_specs=in_specs, out_specs=out_specs, check_vma=False)
```

time: 351 us -> 207 us (0.59)
  waiting for transfers between devices: 250 us -> 65 us
  starting transfers between devices: 0.38 us -> 53.6 us
  matrix products: 46.5 us -> 0 us
  Pallas kernels: 0 us -> 31.8 us
  blocking collectives: 28 us -> 43.9 us
  between operations: 13.8 us -> 1.01 us
    reduce_scatter x3 -> x0, waiting for transfers between devices: 165 us -> none  [the longest x1 82.2 us: shards(): lax.psum_scatter(jnp.dot(inputs_all, w_in, preferred_element_type=jnp.flo...]
    all_gather x2 -> x0, waiting for transfers between devices: 84.6 us -> none  [the longest x1 55.4 us: shards(): lax.all_gather(grad_hidden_local, 'row', axis=0, tiled=True)]
    ppermute x0 -> x32, waiting for transfers between devices: none -> 65 us  [hop(): return lax.ppermute(value, AXES, neighbours(step, first))]
    ppermute x0 -> x32, starting transfers between devices: none -> 53.6 us  [hop(): return lax.ppermute(value, AXES, neighbours(step, first))]
    dot_general x5 -> x0, matrix products: 46.5 us -> none  [the longest x1 9.76 us: shards(): lax.dot_general(inputs_all, grad_hidden_all, (((0,), (0,)), ((), ())), pr...]
    pallas_call x0 -> x4, Pallas kernels: none -> 31.8 us  [the longest x2 19.2 us: grads(): pl.pallas_call(functools.partial(grads_kernel, last), grid=(tiles,), out_...]
    all_to_all x0 -> x1, blocking collectives: none -> 15.7 us  [shards(): parts = lax.all_to_all(gi.reshape(8, 64, WID), 'col', 0, 0)]
    unnamed x3 -> x8, local copies, waits for them, and re-layouts: 9.57 us -> 5.72 us
  transfers between devices with their start and end apart: 5 -> 32, of which waited for: 5 -> 19; matrix products, arithmetic and copies ran while one was open for 13% -> 2% of each run, Pallas kernels for 0% -> 8%
where the time goes in v1:
time: 207 us; the launch traced here: 205 us
  waiting for transfers between devices  65 us (31%)
  starting transfers between devices  53.6 us (26%)
  blocking collectives  43.9 us (21%)
  Pallas kernels  31.8 us (15%)
  local copies, waits for them, and re-layouts  6.21 us (3%)
  other arithmetic  3.86 us (2%)
    ppermute x32, waiting for transfers between devices, hop(): return lax.ppermute(value, AXES, neighbours(step, first))  65 us
    ppermute x32, starting transfers between devices, hop(): return lax.ppermute(value, AXES, neighbours(step, first))  53.6 us
    pallas_call x2, Pallas kernels, grads(): pl.pallas_call(functools.partial(grads_kernel, last), grid=(tiles,), out_...  19.2 us
    all_to_all x1, blocking collectives, shards(): parts = lax.all_to_all(gi.reshape(8, 64, WID), 'col', 0, 0)  15.7 us
    all_gather x1, blocking collectives, shards(): x_all = lax.all_gather(inputs, 'col', axis=0, tiled=True)  14.7 us
    all_gather x1, blocking collectives, shards(): c_all = lax.all_gather(cotangent, 'col', axis=0, tiled=True)  13.4 us
    pallas_call x2, Pallas kernels, partials(): pl.pallas_call(partial_kernel, grid=(tiles,), out_shape=(one, one, pair,...  12.6 us
    unnamed x8, local copies, waits for them, and re-layouts  5.72 us
  transfers between devices with their start and end apart: 32, of which 19 were waited for; matrix products, arithmetic and copies ran while one was open for 2% of the time, Pallas kernels for 8%

profile of v1, /device:TPU:0, one launch (start us, length us, event | category | flops | bytes accessed | tf_op | source)
XLA Modules:
  0.0 205.3 jit_solution(9537049919955137865)
XLA Ops:
  0.7 14.7 %all_gather.6.x_ref = bf16[512,640]{1,0:T(8,128)(2,1)S(1)} all-gather(bf16[64,640]{1,0:T(8,128)(2,1)} %param.4), channel_id=1, replica_groups=mesh['row'=16,'col'=8] {'col'}, dimensions={0}, use_global_device_ids=true | all-gather | bytes 737280 | tf_op jit(solution)/shard_map/all_gather | solution.py:200
  15.4 13.4 %all_gather.7.c_ref = bf16[512,640]{1,0:T(8,128)(2,1)S(1)} all-gather(bf16[64,640]{1,0:T(8,128)(2,1)} %param.5), channel_id=1, replica_groups=mesh['row'=16,'col'=8] {'col'}, dimensions={0}, use_global_device_ids=true | all-gather | bytes 737280 | tf_op jit(solution)/shard_map/all_gather | solution.py:201
  28.9 2.9 %copy-done = bf16[640,5120]{1,0:T(8,128)(2,1)S(1)} copy-done((bf16[640,5120]{1,0:T(8,128)(2,1)S(1)}, bf16[640,5120]{1,0:T(8,128)(2,1)}, u32[]{:S(2)}) %copy-start) | copy-done | bytes 6553624
  31.7 2.9 %copy-done.1 = bf16[5120,640]{1,0:T(8,128)(2,1)S(1)} copy-done((bf16[5120,640]{1,0:T(8,128)(2,1)S(1)}, bf16[5120,640]{1,0:T(8,128)(2,1)}, u32[]{:S(2)}) %copy-start.1) | copy-done | bytes 6553624
  34.6 6.3 %partials.3 = (bf16[128,2560]{1,0:T(8,128)(2,1)S(1)}, bf16[128,2560]{1,0:T(8,128)(2,1)S(1)}, bf16[2,128,2560]{2,1,0:T(8,128)(2,1)S(1)}, bf16[2,128,2560]{2,1,0:T(8,128)(2,1)S(1)}, bf16[2,128,2560]{2,1,0:T(8,128)(2,1)S(1)}) custom-call(s32[16]{0:T(128)S(1)} %fusion.28.order_ref, bf16[512,640]{1,0:T(8,128)(2,1)S(1)} %all_gather.6.x_ref, ...), custom_call_target="tpu_custom_call" | custom-call | flops 3355443200 | bytes 11796480 | tf_op jit(solution)/shard_map/partials/pallas_call | solution.py:79
  40.9 2.8 %collective-permute-start.18 = (bf16[128,2560]{1,0:T(8,128)(2,1)S(1)}, bf16[128,2560]{1,0:T(8,128)(2,1)S(1)}, u32[]{:S(2)}, u32[]{:S(2)}) collective-permute-start(bf16[128,2560]{1,0:T(8,128)(2,1)S(1)} %get-tuple-element.28), channel_id=1, source_target_pairs={{0,96},{1,25},{2,98},{3,27},{4,100},{5,29},{6,102},{7,31},{8,104},... | collective-permute-start | bytes 1966088 | tf_op jit(solution)/shard_map/ppermute | solution.py:34
  43.7 6.3 %partials.2 = (bf16[128,2560]{1,0:T(8,128)(2,1)S(1)}, bf16[128,2560]{1,0:T(8,128)(2,1)S(1)}, bf16[2,128,2560]{2,1,0:T(8,128)(2,1)S(1)}, bf16[2,128,2560]{2,1,0:T(8,128)(2,1)S(1)}, bf16[2,128,2560]{2,1,0:T(8,128)(2,1)S(1)}) custom-call(s32[16]{0:T(128)S(1)} %fusion.28.order_ref, bf16[512,640]{1,0:T(8,128)(2,1)S(1)} %all_gather.6.x_ref, ...), custom_call_target="tpu_custom_call" | custom-call | flops 3355443200 | bytes 11796480 | tf_op jit(solution)/shard_map/partials/pallas_call | solution.py:79
  50.9 2.6 %collective-permute-start.2 = (bf16[128,2560]{1,0:T(8,128)(2,1)S(1)}, bf16[128,2560]{1,0:T(8,128)(2,1)S(1)}, u32[]{:S(2)}, u32[]{:S(2)}) collective-permute-start(bf16[128,2560]{1,0:T(8,128)(2,1)S(1)} %get-tuple-element.23), channel_id=1, source_target_pairs={{0,96},{1,25},{2,98},{3,27},{4,100},{5,29},{6,102},{7,31},{8,104},... | collective-permute-start | bytes 1966088 | tf_op jit(solution)/shard_map/ppermute | solution.py:34
  56.4 5.1 %collective-permute-done.2 = bf16[128,2560]{1,0:T(8,128)(2,1)S(1)} collective-permute-done((bf16[128,2560]{1,0:T(8,128)(2,1)S(1)}, bf16[128,2560]{1,0:T(8,128)(2,1)S(1)}, u32[]{:S(2)}, u32[]{:S(2)}) %collective-permute-start.2) | collective-permute-done | bytes 655392 | tf_op jit(solution)/shard_map/ppermute | solution.py:34
  61.8 3.8 %collective-permute-start.3 = (bf16[2,128,2560]{2,1,0:T(8,128)(2,1)S(1)}, bf16[2,128,2560]{2,1,0:T(8,128)(2,1)S(1)}, u32[]{:S(2)}, u32[]{:S(2)}) collective-permute-start(bf16[2,128,2560]{2,1,0:T(8,128)(2,1)S(1)} %pad_maximum_fusion.1), channel_id=1, source_target_pairs={{0,96},{1,25},{2,98},{3,27},{4,100},{5,29},{6,102},{7,31},{8,104},... | collective-permute-start | bytes 3932168 | tf_op jit(solution)/shard_map/ppermute | solution.py:34
  65.9 9.6 %collective-permute-done.19 = bf16[2,128,2560]{2,1,0:T(8,128)(2,1)S(1)} collective-permute-done((bf16[2,128,2560]{2,1,0:T(8,128)(2,1)S(1)}, bf16[2,128,2560]{2,1,0:T(8,128)(2,1)S(1)}, u32[]{:S(2)}, u32[]{:S(2)}) %collective-permute-start.19) | collective-permute-done | bytes 1310752 | tf_op jit(solution)/shard_map/ppermute | solution.py:34
  80.4 10.9 %collective-permute-done.3 = bf16[2,128,2560]{2,1,0:T(8,128)(2,1)S(1)} collective-permute-done((bf16[2,128,2560]{2,1,0:T(8,128)(2,1)S(1)}, bf16[2,128,2560]{2,1,0:T(8,128)(2,1)S(1)}, u32[]{:S(2)}, u32[]{:S(2)}) %collective-permute-start.3) | collective-permute-done | bytes 1310752 | tf_op jit(solution)/shard_map/ppermute | solution.py:34
  100.0 2.9 %collective-permute-start.7 = (bf16[2,32,2560]{2,1,0:T(8,128)(2,1)S(1)}, bf16[2,32,2560]{2,1,0:T(8,128)(2,1)S(1)}, u32[]{:S(2)}, u32[]{:S(2)}) collective-permute-start(bf16[2,32,2560]{2,1,0:T(8,128)(2,1)S(1)} %pad_maximum_fusion.7), channel_id=1, source_target_pairs={{0,24},{1,97},{2,26},{3,99},{4,28},{5,101},{6,30},{7,103},{8,0},{9... | collective-permute-start | bytes 983048 | tf_op jit(solution)/shard_map/ppermute | solution.py:34
  103.5 3.1 %collective-permute-done.21 = bf16[2,32,2560]{2,1,0:T(8,128)(2,1)S(1)} collective-permute-done((bf16[2,32,2560]{2,1,0:T(8,128)(2,1)S(1)}, bf16[2,32,2560]{2,1,0:T(8,128)(2,1)S(1)}, u32[]{:S(2)}, u32[]{:S(2)}) %collective-permute-start.21) | collective-permute-done | bytes 327712 | tf_op jit(solution)/shard_map/ppermute | solution.py:34
  107.0 3.2 %collective-permute-start.24 = (bf16[2,32,2560]{2,1,0:T(8,128)(2,1)S(1)}, bf16[2,32,2560]{2,1,0:T(8,128)(2,1)S(1)}, u32[]{:S(2)}, u32[]{:S(2)}) collective-permute-start(bf16[2,32,2560]{2,1,0:T(8,128)(2,1)S(1)} %pad_maximum_fusion.11), channel_id=1, source_target_pairs={{0,24},{1,97},{2,26},{3,99},{4,28},{5,101},{6,30},{7,103},{8,0},{9... | collective-permute-start | bytes 983048 | tf_op jit(solution)/shard_map/ppermute | solution.py:34
  111.8 3.5 %collective-permute-done.25 = bf16[2,32,2560]{2,1,0:T(8,128)(2,1)S(1)} collective-permute-done((bf16[2,32,2560]{2,1,0:T(8,128)(2,1)S(1)}, bf16[2,32,2560]{2,1,0:T(8,128)(2,1)S(1)}, u32[]{:S(2)}, u32[]{:S(2)}) %collective-permute-start.25) | collective-permute-done | bytes 327712 | tf_op jit(solution)/shard_map/ppermute | solution.py:34
  115.4 3.3 %collective-permute-start.27 = (bf16[32,2560]{1,0:T(8,128)(2,1)S(1)}, bf16[32,2560]{1,0:T(8,128)(2,1)S(1)}, u32[]{:S(2)}, u32[]{:S(2)}) collective-permute-start(bf16[32,2560]{1,0:T(8,128)(2,1)S(1)} %slice_bitcast_fusion.4), channel_id=1, source_target_pairs={{0,24},{1,97},{2,26},{3,99},{4,28},{5,101},{6,30},{7,103},{8,0},{9... | collective-permute-start | bytes 491528 | tf_op jit(solution)/shard_map/ppermute | solution.py:34
  118.8 3.2 %collective-permute-start.8 = (bf16[2,32,2560]{2,1,0:T(8,128)(2,1)S(1)}, bf16[2,32,2560]{2,1,0:T(8,128)(2,1)S(1)}, u32[]{:S(2)}, u32[]{:S(2)}) collective-permute-start(bf16[2,32,2560]{2,1,0:T(8,128)(2,1)S(1)} %pad_maximum_fusion.8), channel_id=1, source_target_pairs={{0,24},{1,97},{2,26},{3,99},{4,28},{5,101},{6,30},{7,103},{8,0},{9... | collective-permute-start | bytes 983048 | tf_op jit(solution)/shard_map/ppermute | solution.py:34
  122.1 2.4 %collective-permute-start.29 = (bf16[2,128,2560]{2,1,0:T(8,128)(2,1)S(1)}, bf16[2,128,2560]{2,1,0:T(8,128)(2,1)S(1)}, u32[]{:S(2)}, u32[]{:S(2)}) collective-permute-start(bf16[2,128,2560]{2,1,0:T(8,128)(2,1)S(1)} %pad_maximum_fusion.5.o0_ref), channel_id=1, source_target_pairs={{0,32},{1,9},{2,34},{3,11},{4,36},{5,13},{6,38},{7,15},{8,40},{9,1... | collective-permute-start | bytes 3932168 | tf_op jit(solution)/shard_map/ppermute | solution.py:34
  124.6 6.1 %collective-permute-done.9 = bf16[2,32,2560]{2,1,0:T(8,128)(2,1)S(1)} collective-permute-done((bf16[2,32,2560]{2,1,0:T(8,128)(2,1)S(1)}, bf16[2,32,2560]{2,1,0:T(8,128)(2,1)S(1)}, u32[]{:S(2)}, u32[]{:S(2)}) %collective-permute-start.9) | collective-permute-done | bytes 327712 | tf_op jit(solution)/shard_map/ppermute | solution.py:34
  130.8 2.8 %collective-permute-start.28 = (bf16[2,128,2560]{2,1,0:T(8,128)(2,1)S(1)}, bf16[2,128,2560]{2,1,0:T(8,128)(2,1)S(1)}, u32[]{:S(2)}, u32[]{:S(2)}) collective-permute-start(bf16[2,128,2560]{2,1,0:T(8,128)(2,1)S(1)} %pad_maximum_fusion.5.o0_ref), channel_id=1, source_target_pairs={{0,96},{1,25},{2,98},{3,27},{4,100},{5,29},{6,102},{7,31},{8,104},... | collective-permute-start | bytes 3932168 | tf_op jit(solution)/shard_map/ppermute | solution.py:34
  133.5 3.2 %collective-permute-start.11 = (bf16[32,2560]{1,0:T(8,128)(2,1)S(1)}, bf16[32,2560]{1,0:T(8,128)(2,1)S(1)}, u32[]{:S(2)}, u32[]{:S(2)}) collective-permute-start(bf16[32,2560]{1,0:T(8,128)(2,1)S(1)} %slice_bitcast_fusion.10), channel_id=1, source_target_pairs={{0,24},{1,97},{2,26},{3,99},{4,28},{5,101},{6,30},{7,103},{8,0},{9... | collective-permute-start | bytes 491528 | tf_op jit(solution)/shard_map/ppermute | solution.py:34
  136.8 2.3 %collective-permute-done.10 = bf16[32,2560]{1,0:T(8,128)(2,1)S(1)} collective-permute-done((bf16[32,2560]{1,0:T(8,128)(2,1)S(1)}, bf16[32,2560]{1,0:T(8,128)(2,1)S(1)}, u32[]{:S(2)}, u32[]{:S(2)}) %collective-permute-start.10) | collective-permute-done | bytes 163872 | tf_op jit(solution)/shard_map/ppermute | solution.py:34
  139.1 2.3 %collective-permute-done.11 = bf16[32,2560]{1,0:T(8,128)(2,1)S(1)} collective-permute-done((bf16[32,2560]{1,0:T(8,128)(2,1)S(1)}, bf16[32,2560]{1,0:T(8,128)(2,1)S(1)}, u32[]{:S(2)}, u32[]{:S(2)}) %collective-permute-start.11) | collective-permute-done | bytes 163872 | tf_op jit(solution)/shard_map/ppermute | solution.py:34
  141.6 3.2 %collective-permute-start.12 = (bf16[2,128,2560]{2,1,0:T(8,128)(2,1)S(1)}, bf16[2,128,2560]{2,1,0:T(8,128)(2,1)S(1)}, u32[]{:S(2)}, u32[]{:S(2)}) collective-permute-start(bf16[2,128,2560]{2,1,0:T(8,128)(2,1)S(1)} %pad_maximum_fusion.2.o0_ref), channel_id=1, source_target_pairs={{0,96},{1,25},{2,98},{3,27},{4,100},{5,29},{6,102},{7,31},{8,104},... | collective-permute-start | bytes 3932168 | tf_op jit(solution)/shard_map/ppermute | solution.py:34
  144.9 3.7 %collective-permute-done.28.o1_ref = bf16[2,128,2560]{2,1,0:T(8,128)(2,1)S(1)} collective-permute-done((bf16[2,128,2560]{2,1,0:T(8,128)(2,1)S(1)}, bf16[2,128,2560]{2,1,0:T(8,128)(2,1)S(1)}, u32[]{:S(2)}, u32[]{:S(2)}) %collective-permute-start.28) | collective-permute-done | bytes 1310752 | tf_op jit(solution)/shard_map/ppermute | solution.py:34
  148.7 3.8 %collective-permute-start.31 = (bf16[128,2560]{1,0:T(8,128)(2,1)S(1)}, bf16[128,2560]{1,0:T(8,128)(2,1)S(1)}, u32[]{:S(2)}, u32[]{:S(2)}) collective-permute-start(bf16[128,2560]{1,0:T(8,128)(2,1)S(1)} %slice_bitcast_fusion), channel_id=1, source_target_pairs={{0,96},{1,25},{2,98},{3,27},{4,100},{5,29},{6,102},{7,31},{8,104},... | collective-permute-start | bytes 1966088 | tf_op jit(solution)/shard_map/ppermute | solution.py:34
  152.4 7.9 %collective-permute-done.13.o3_ref = bf16[2,128,2560]{2,1,0:T(8,128)(2,1)S(1)} collective-permute-done((bf16[2,128,2560]{2,1,0:T(8,128)(2,1)S(1)}, bf16[2,128,2560]{2,1,0:T(8,128)(2,1)S(1)}, u32[]{:S(2)}, u32[]{:S(2)}) %collective-permute-start.13) | collective-permute-done | bytes 1310752 | tf_op jit(solution)/shard_map/ppermute | solution.py:34
  162.7 3.8 %collective-permute-start.15 = (bf16[128,2560]{1,0:T(8,128)(2,1)S(1)}, bf16[128,2560]{1,0:T(8,128)(2,1)S(1)}, u32[]{:S(2)}, u32[]{:S(2)}) collective-permute-start(bf16[128,2560]{1,0:T(8,128)(2,1)S(1)} %slice_bitcast_fusion.2), channel_id=1, source_target_pairs={{0,96},{1,25},{2,98},{3,27},{4,100},{5,29},{6,102},{7,31},{8,104},... | collective-permute-start | bytes 1966088 | tf_op jit(solution)/shard_map/ppermute | solution.py:34
  169.7 9.4 %grads.2 = (f32[512,640]{1,0:T(8,128)S(1)}, bf16[640,5120]{1,0:T(8,128)(2,1)}, bf16[5120,640]{1,0:T(8,128)(2,1)}) custom-call(s32[16]{0:T(128)S(1)} %fusion.28.order_ref, bf16[512,640]{1,0:T(8,128)(2,1)S(1)} %all_gather.6.x_ref, bf16[512,640]{1,0:T(8,128)(2,1)S(1)} %all_gather.7.c_ref, bf16[640,5120]{1,0:T(8,128)(2,1)S(1)} %bitcast.78, ...), custom_call_target="tpu_custom_call" | custom-call | flops 5033164800 | bytes 15073280 | tf_op jit(solution)/shard_map/grads/pallas_call | solution.py:137
  179.1 9.8 %grads.3 = (bf16[512,640]{1,0:T(8,128)(2,1)S(1)}, bf16[640,5120]{1,0:T(8,128)(2,1)}, bf16[5120,640]{1,0:T(8,128)(2,1)}) custom-call(s32[16]{0:T(128)S(1)} %fusion.28.order_ref, bf16[512,640]{1,0:T(8,128)(2,1)S(1)} %all_gather.6.x_ref, bf16[512,640]{1,0:T(8,128)(2,1)S(1)} %all_gather.7.c_ref, ...), custom_call_target="tpu_custom_call", output_to_operand_aliasing={{1}: (10, {}), {2}: (11, {})} | custom-call | flops 5033164800 | bytes 15073280 | tf_op jit(solution)/shard_map/grads/pallas_call | solution.py:137
  188.9 15.7 %all_to_all.5 = bf16[8,64,640]{2,1,0:T(8,128)(2,1)S(1)} all-to-all(bf16[8,64,640]{2,1,0:T(8,128)(2,1)S(1)} %bitcast.79), channel_id=1, replica_groups=mesh['row'=16,'col'=8] {'col'}, dimensions={0} | all-to-all | bytes 1310720 | tf_op jit(solution)/shard_map/all_to_all | solution.py:226
  (88 shorter events, 27.3 us)
Async XLA Ops:
  40.9 12.7 %collective-permute-start.18 = (bf16[128,2560]{1,0:T(8,128)(2,1)S(1)}, bf16[128,2560]{1,0:T(8,128)(2,1)S(1)}, u32[]{:S(2)}, u32[]{:S(2)}) collective-permute-start(bf16[128,2560]{1,0:T(8,128)(2,1)S(1)} %get-tuple-element.28), channel_id=1, source_target_pairs={{0,96},{1,25},{2,98},{3,27},{4,100},{5,29},{6,102},{7,31},{8,104},... | collective-permute-start | bytes 1966088 | tf_op jit(solution)/shard_map/ppermute | solution.py:34
  43.7 12.2 %collective-permute-start.16 = (bf16[128,2560]{1,0:T(8,128)(2,1)S(1)}, bf16[128,2560]{1,0:T(8,128)(2,1)S(1)}, u32[]{:S(2)}, u32[]{:S(2)}) collective-permute-start(bf16[128,2560]{1,0:T(8,128)(2,1)S(1)} %get-tuple-element.26), channel_id=1, source_target_pairs={{0,32},{1,9},{2,34},{3,11},{4,36},{5,13},{6,38},{7,15},{8,40},{9,1... | collective-permute-start | bytes 1966088 | tf_op jit(solution)/shard_map/ppermute | solution.py:34
  50.0 15.5 %collective-permute-start = (bf16[128,2560]{1,0:T(8,128)(2,1)S(1)}, bf16[128,2560]{1,0:T(8,128)(2,1)S(1)}, u32[]{:S(2)}, u32[]{:S(2)}) collective-permute-start(bf16[128,2560]{1,0:T(8,128)(2,1)S(1)} %get-tuple-element.21), channel_id=1, source_target_pairs={{0,32},{1,9},{2,34},{3,11},{4,36},{5,13},{6,38},{7,15},{8,40},{9,1... | collective-permute-start | bytes 1966088 | tf_op jit(solution)/shard_map/ppermute | solution.py:34
  50.9 10.7 %collective-permute-start.2 = (bf16[128,2560]{1,0:T(8,128)(2,1)S(1)}, bf16[128,2560]{1,0:T(8,128)(2,1)S(1)}, u32[]{:S(2)}, u32[]{:S(2)}) collective-permute-start(bf16[128,2560]{1,0:T(8,128)(2,1)S(1)} %get-tuple-element.23), channel_id=1, source_target_pairs={{0,96},{1,25},{2,98},{3,27},{4,100},{5,29},{6,102},{7,31},{8,104},... | collective-permute-start | bytes 1966088 | tf_op jit(solution)/shard_map/ppermute | solution.py:34
  53.9 21.6 %collective-permute-start.19 = (bf16[2,128,2560]{2,1,0:T(8,128)(2,1)S(1)}, bf16[2,128,2560]{2,1,0:T(8,128)(2,1)S(1)}, u32[]{:S(2)}, u32[]{:S(2)}) collective-permute-start(bf16[2,128,2560]{2,1,0:T(8,128)(2,1)S(1)} %pad_maximum_fusion.4), channel_id=1, source_target_pairs={{0,96},{1,25},{2,98},{3,27},{4,100},{5,29},{6,102},{7,31},{8,104},... | collective-permute-start | bytes 3932168 | tf_op jit(solution)/shard_map/ppermute | solution.py:34
  56.2 20.4 %collective-permute-start.17 = (bf16[2,128,2560]{2,1,0:T(8,128)(2,1)S(1)}, bf16[2,128,2560]{2,1,0:T(8,128)(2,1)S(1)}, u32[]{:S(2)}, u32[]{:S(2)}) collective-permute-start(bf16[2,128,2560]{2,1,0:T(8,128)(2,1)S(1)} %pad_maximum_fusion.3), channel_id=1, source_target_pairs={{0,32},{1,9},{2,34},{3,11},{4,36},{5,13},{6,38},{7,15},{8,40},{9,1... | collective-permute-start | bytes 3932168 | tf_op jit(solution)/shard_map/ppermute | solution.py:34
  61.8 29.6 %collective-permute-start.3 = (bf16[2,128,2560]{2,1,0:T(8,128)(2,1)S(1)}, bf16[2,128,2560]{2,1,0:T(8,128)(2,1)S(1)}, u32[]{:S(2)}, u32[]{:S(2)}) collective-permute-start(bf16[2,128,2560]{2,1,0:T(8,128)(2,1)S(1)} %pad_maximum_fusion.1), channel_id=1, source_target_pairs={{0,96},{1,25},{2,98},{3,27},{4,100},{5,29},{6,102},{7,31},{8,104},... | collective-permute-start | bytes 3932168 | tf_op jit(solution)/shard_map/ppermute | solution.py:34
  65.8 26.5 %collective-permute-start.1 = (bf16[2,128,2560]{2,1,0:T(8,128)(2,1)S(1)}, bf16[2,128,2560]{2,1,0:T(8,128)(2,1)S(1)}, u32[]{:S(2)}, u32[]{:S(2)}) collective-permute-start(bf16[2,128,2560]{2,1,0:T(8,128)(2,1)S(1)} %pad_maximum_fusion), channel_id=1, source_target_pairs={{0,32},{1,9},{2,34},{3,11},{4,36},{5,13},{6,38},{7,15},{8,40},{9,1... | collective-permute-start | bytes 3932168 | tf_op jit(solution)/shard_map/ppermute | solution.py:34
  77.1 19.1 %collective-permute-start.20 = (bf16[32,2560]{1,0:T(8,128)(2,1)S(1)}, bf16[32,2560]{1,0:T(8,128)(2,1)S(1)}, u32[]{:S(2)}, u32[]{:S(2)}) collective-permute-start(bf16[32,2560]{1,0:T(8,128)(2,1)S(1)} %get-tuple-element.37), channel_id=1, source_target_pairs={{0,8},{1,33},{2,10},{3,35},{4,12},{5,37},{6,14},{7,39},{8,16},{9,4... | collective-permute-start | bytes 491528 | tf_op jit(solution)/shard_map/ppermute | solution.py:34
  78.7 17.5 %collective-permute-start.22 = (bf16[32,2560]{1,0:T(8,128)(2,1)S(1)}, bf16[32,2560]{1,0:T(8,128)(2,1)S(1)}, u32[]{:S(2)}, u32[]{:S(2)}) collective-permute-start(bf16[32,2560]{1,0:T(8,128)(2,1)S(1)} %get-tuple-element.38), channel_id=1, source_target_pairs={{0,24},{1,97},{2,26},{3,99},{4,28},{5,101},{6,30},{7,103},{8,0},{9... | collective-permute-start | bytes 491528 | tf_op jit(solution)/shard_map/ppermute | solution.py:34
  92.9 6.6 %collective-permute-start.4 = (bf16[32,2560]{1,0:T(8,128)(2,1)S(1)}, bf16[32,2560]{1,0:T(8,128)(2,1)S(1)}, u32[]{:S(2)}, u32[]{:S(2)}) collective-permute-start(bf16[32,2560]{1,0:T(8,128)(2,1)S(1)} %get-tuple-element.43), channel_id=1, source_target_pairs={{0,8},{1,33},{2,10},{3,35},{4,12},{5,37},{6,14},{7,39},{8,16},{9,4... | collective-permute-start | bytes 491528 | tf_op jit(solution)/shard_map/ppermute | solution.py:34
  94.6 5.3 %collective-permute-start.6 = (bf16[32,2560]{1,0:T(8,128)(2,1)S(1)}, bf16[32,2560]{1,0:T(8,128)(2,1)S(1)}, u32[]{:S(2)}, u32[]{:S(2)}) collective-permute-start(bf16[32,2560]{1,0:T(8,128)(2,1)S(1)} %get-tuple-element.44), channel_id=1, source_target_pairs={{0,24},{1,97},{2,26},{3,99},{4,28},{5,101},{6,30},{7,103},{8,0},{9... | collective-permute-start | bytes 491528 | tf_op jit(solution)/shard_map/ppermute | solution.py:34
  96.3 7.1 %collective-permute-start.23 = (bf16[2,32,2560]{2,1,0:T(8,128)(2,1)S(1)}, bf16[2,32,2560]{2,1,0:T(8,128)(2,1)S(1)}, u32[]{:S(2)}, u32[]{:S(2)}) collective-permute-start(bf16[2,32,2560]{2,1,0:T(8,128)(2,1)S(1)} %pad_maximum_fusion.10), channel_id=1, source_target_pairs={{0,24},{1,97},{2,26},{3,99},{4,28},{5,101},{6,30},{7,103},{8,0},{9... | collective-permute-start | bytes 983048 | tf_op jit(solution)/shard_map/ppermute | solution.py:34
  98.3 8.4 %collective-permute-start.21 = (bf16[2,32,2560]{2,1,0:T(8,128)(2,1)S(1)}, bf16[2,32,2560]{2,1,0:T(8,128)(2,1)S(1)}, u32[]{:S(2)}, u32[]{:S(2)}) collective-permute-start(bf16[2,32,2560]{2,1,0:T(8,128)(2,1)S(1)} %pad_maximum_fusion.9), channel_id=1, source_target_pairs={{0,8},{1,33},{2,10},{3,35},{4,12},{5,37},{6,14},{7,39},{8,16},{9,4... | collective-permute-start | bytes 983048 | tf_op jit(solution)/shard_map/ppermute | solution.py:34
  100.0 10.2 %collective-permute-start.7 = (bf16[2,32,2560]{2,1,0:T(8,128)(2,1)S(1)}, bf16[2,32,2560]{2,1,0:T(8,128)(2,1)S(1)}, u32[]{:S(2)}, u32[]{:S(2)}) collective-permute-start(bf16[2,32,2560]{2,1,0:T(8,128)(2,1)S(1)} %pad_maximum_fusion.7), channel_id=1, source_target_pairs={{0,24},{1,97},{2,26},{3,99},{4,28},{5,101},{6,30},{7,103},{8,0},{9... | collective-permute-start | bytes 983048 | tf_op jit(solution)/shard_map/ppermute | solution.py:34
  103.0 8.5 %collective-permute-start.5 = (bf16[2,32,2560]{2,1,0:T(8,128)(2,1)S(1)}, bf16[2,32,2560]{2,1,0:T(8,128)(2,1)S(1)}, u32[]{:S(2)}, u32[]{:S(2)}) collective-permute-start(bf16[2,32,2560]{2,1,0:T(8,128)(2,1)S(1)} %pad_maximum_fusion.6), channel_id=1, source_target_pairs={{0,8},{1,33},{2,10},{3,35},{4,12},{5,37},{6,14},{7,39},{8,16},{9,4... | collective-permute-start | bytes 983048 | tf_op jit(solution)/shard_map/ppermute | solution.py:34
  106.9 8.4 %collective-permute-start.25 = (bf16[2,32,2560]{2,1,0:T(8,128)(2,1)S(1)}, bf16[2,32,2560]{2,1,0:T(8,128)(2,1)S(1)}, u32[]{:S(2)}, u32[]{:S(2)}) collective-permute-start(bf16[2,32,2560]{2,1,0:T(8,128)(2,1)S(1)} %pad_maximum_fusion.11), channel_id=1, source_target_pairs={{0,8},{1,33},{2,10},{3,35},{4,12},{5,37},{6,14},{7,39},{8,16},{9,4... | collective-permute-start | bytes 983048 | tf_op jit(solution)/shard_map/ppermute | solution.py:34
  107.0 8.4 %collective-permute-start.24 = (bf16[2,32,2560]{2,1,0:T(8,128)(2,1)S(1)}, bf16[2,32,2560]{2,1,0:T(8,128)(2,1)S(1)}, u32[]{:S(2)}, u32[]{:S(2)}) collective-permute-start(bf16[2,32,2560]{2,1,0:T(8,128)(2,1)S(1)} %pad_maximum_fusion.11), channel_id=1, source_target_pairs={{0,24},{1,97},{2,26},{3,99},{4,28},{5,101},{6,30},{7,103},{8,0},{9... | collective-permute-start | bytes 983048 | tf_op jit(solution)/shard_map/ppermute | solution.py:34
  115.3 6.7 %collective-permute-start.26 = (bf16[32,2560]{1,0:T(8,128)(2,1)S(1)}, bf16[32,2560]{1,0:T(8,128)(2,1)S(1)}, u32[]{:S(2)}, u32[]{:S(2)}) collective-permute-start(bf16[32,2560]{1,0:T(8,128)(2,1)S(1)} %slice_bitcast_fusion.5), channel_id=1, source_target_pairs={{0,8},{1,33},{2,10},{3,35},{4,12},{5,37},{6,14},{7,39},{8,16},{9,4... | collective-permute-start | bytes 491528 | tf_op jit(solution)/shard_map/ppermute | solution.py:34
  115.4 6.6 %collective-permute-start.27 = (bf16[32,2560]{1,0:T(8,128)(2,1)S(1)}, bf16[32,2560]{1,0:T(8,128)(2,1)S(1)}, u32[]{:S(2)}, u32[]{:S(2)}) collective-permute-start(bf16[32,2560]{1,0:T(8,128)(2,1)S(1)} %slice_bitcast_fusion.4), channel_id=1, source_target_pairs={{0,24},{1,97},{2,26},{3,99},{4,28},{5,101},{6,30},{7,103},{8,0},{9... | collective-permute-start | bytes 491528 | tf_op jit(solution)/shard_map/ppermute | solution.py:34
  118.7 11.9 %collective-permute-start.9 = (bf16[2,32,2560]{2,1,0:T(8,128)(2,1)S(1)}, bf16[2,32,2560]{2,1,0:T(8,128)(2,1)S(1)}, u32[]{:S(2)}, u32[]{:S(2)}) collective-permute-start(bf16[2,32,2560]{2,1,0:T(8,128)(2,1)S(1)} %pad_maximum_fusion.8), channel_id=1, source_target_pairs={{0,8},{1,33},{2,10},{3,35},{4,12},{5,37},{6,14},{7,39},{8,16},{9,4... | collective-permute-start | bytes 983048 | tf_op jit(solution)/shard_map/ppermute | solution.py:34
  118.8 14.7 %collective-permute-start.8 = (bf16[2,32,2560]{2,1,0:T(8,128)(2,1)S(1)}, bf16[2,32,2560]{2,1,0:T(8,128)(2,1)S(1)}, u32[]{:S(2)}, u32[]{:S(2)}) collective-permute-start(bf16[2,32,2560]{2,1,0:T(8,128)(2,1)S(1)} %pad_maximum_fusion.8), channel_id=1, source_target_pairs={{0,24},{1,97},{2,26},{3,99},{4,28},{5,101},{6,30},{7,103},{8,0},{9... | collective-permute-start | bytes 983048 | tf_op jit(solution)/shard_map/ppermute | solution.py:34
  122.1 22.7 %collective-permute-start.29 = (bf16[2,128,2560]{2,1,0:T(8,128)(2,1)S(1)}, bf16[2,128,2560]{2,1,0:T(8,128)(2,1)S(1)}, u32[]{:S(2)}, u32[]{:S(2)}) collective-permute-start(bf16[2,128,2560]{2,1,0:T(8,128)(2,1)S(1)} %pad_maximum_fusion.5.o0_ref), channel_id=1, source_target_pairs={{0,32},{1,9},{2,34},{3,11},{4,36},{5,13},{6,38},{7,15},{8,40},{9,1... | collective-permute-start | bytes 3932168 | tf_op jit(solution)/shard_map/ppermute | solution.py:34
  130.7 8.4 %collective-permute-start.10 = (bf16[32,2560]{1,0:T(8,128)(2,1)S(1)}, bf16[32,2560]{1,0:T(8,128)(2,1)S(1)}, u32[]{:S(2)}, u32[]{:S(2)}) collective-permute-start(bf16[32,2560]{1,0:T(8,128)(2,1)S(1)} %slice_bitcast_fusion.11), channel_id=1, source_target_pairs={{0,8},{1,33},{2,10},{3,35},{4,12},{5,37},{6,14},{7,39},{8,16},{9,4... | collective-permute-start | bytes 491528 | tf_op jit(solution)/shard_map/ppermute | solution.py:34
  130.8 17.9 %collective-permute-start.28 = (bf16[2,128,2560]{2,1,0:T(8,128)(2,1)S(1)}, bf16[2,128,2560]{2,1,0:T(8,128)(2,1)S(1)}, u32[]{:S(2)}, u32[]{:S(2)}) collective-permute-start(bf16[2,128,2560]{2,1,0:T(8,128)(2,1)S(1)} %pad_maximum_fusion.5.o0_ref), channel_id=1, source_target_pairs={{0,96},{1,25},{2,98},{3,27},{4,100},{5,29},{6,102},{7,31},{8,104},... | collective-permute-start | bytes 3932168 | tf_op jit(solution)/shard_map/ppermute | solution.py:34
  133.5 7.9 %collective-permute-start.11 = (bf16[32,2560]{1,0:T(8,128)(2,1)S(1)}, bf16[32,2560]{1,0:T(8,128)(2,1)S(1)}, u32[]{:S(2)}, u32[]{:S(2)}) collective-permute-start(bf16[32,2560]{1,0:T(8,128)(2,1)S(1)} %slice_bitcast_fusion.10), channel_id=1, source_target_pairs={{0,24},{1,97},{2,26},{3,99},{4,28},{5,101},{6,30},{7,103},{8,0},{9... | collective-permute-start | bytes 491528 | tf_op jit(solution)/shard_map/ppermute | solution.py:34
  141.5 18.9 %collective-permute-start.13 = (bf16[2,128,2560]{2,1,0:T(8,128)(2,1)S(1)}, bf16[2,128,2560]{2,1,0:T(8,128)(2,1)S(1)}, u32[]{:S(2)}, u32[]{:S(2)}) collective-permute-start(bf16[2,128,2560]{2,1,0:T(8,128)(2,1)S(1)} %pad_maximum_fusion.2.o0_ref), channel_id=1, source_target_pairs={{0,32},{1,9},{2,34},{3,11},{4,36},{5,13},{6,38},{7,15},{8,40},{9,1... | collective-permute-start | bytes 3932168 | tf_op jit(solution)/shard_map/ppermute | solution.py:34
  141.6 21.1 %collective-permute-start.12 = (bf16[2,128,2560]{2,1,0:T(8,128)(2,1)S(1)}, bf16[2,128,2560]{2,1,0:T(8,128)(2,1)S(1)}, u32[]{:S(2)}, u32[]{:S(2)}) collective-permute-start(bf16[2,128,2560]{2,1,0:T(8,128)(2,1)S(1)} %pad_maximum_fusion.2.o0_ref), channel_id=1, source_target_pairs={{0,96},{1,25},{2,98},{3,27},{4,100},{5,29},{6,102},{7,31},{8,104},... | collective-permute-start | bytes 3932168 | tf_op jit(solution)/shard_map/ppermute | solution.py:34
  144.9 22.6 %collective-permute-start.30 = (bf16[128,2560]{1,0:T(8,128)(2,1)S(1)}, bf16[128,2560]{1,0:T(8,128)(2,1)S(1)}, u32[]{:S(2)}, u32[]{:S(2)}) collective-permute-start(bf16[128,2560]{1,0:T(8,128)(2,1)S(1)} %slice_bitcast_fusion.1), channel_id=1, source_target_pairs={{0,32},{1,9},{2,34},{3,11},{4,36},{5,13},{6,38},{7,15},{8,40},{9,1... | collective-permute-start | bytes 1966088 | tf_op jit(solution)/shard_map/ppermute | solution.py:34
  148.7 21.0 %collective-permute-start.31 = (bf16[128,2560]{1,0:T(8,128)(2,1)S(1)}, bf16[128,2560]{1,0:T(8,128)(2,1)S(1)}, u32[]{:S(2)}, u32[]{:S(2)}) collective-permute-start(bf16[128,2560]{1,0:T(8,128)(2,1)S(1)} %slice_bitcast_fusion), channel_id=1, source_target_pairs={{0,96},{1,25},{2,98},{3,27},{4,100},{5,29},{6,102},{7,31},{8,104},... | collective-permute-start | bytes 1966088 | tf_op jit(solution)/shard_map/ppermute | solution.py:34
  160.4 18.7 %collective-permute-start.14 = (bf16[128,2560]{1,0:T(8,128)(2,1)S(1)}, bf16[128,2560]{1,0:T(8,128)(2,1)S(1)}, u32[]{:S(2)}, u32[]{:S(2)}) collective-permute-start(bf16[128,2560]{1,0:T(8,128)(2,1)S(1)} %slice_bitcast_fusion.3), channel_id=1, source_target_pairs={{0,32},{1,9},{2,34},{3,11},{4,36},{5,13},{6,38},{7,15},{8,40},{9,1... | collective-permute-start | bytes 1966088 | tf_op jit(solution)/shard_map/ppermute | solution.py:34
  162.7 16.4 %collective-permute-start.15 = (bf16[128,2560]{1,0:T(8,128)(2,1)S(1)}, bf16[128,2560]{1,0:T(8,128)(2,1)S(1)}, u32[]{:S(2)}, u32[]{:S(2)}) collective-permute-start(bf16[128,2560]{1,0:T(8,128)(2,1)S(1)} %slice_bitcast_fusion.2), channel_id=1, source_target_pairs={{0,96},{1,25},{2,98},{3,27},{4,100},{5,29},{6,102},{7,31},{8,104},... | collective-permute-start | bytes 1966088 | tf_op jit(solution)/shard_map/ppermute | solution.py:34
  (4 other events, 88.3 us)

commit v2 on v0

v2 whole, which is shorter than its diff:
```python
import functools
import math

import jax
import jax.numpy as jnp
from jax import lax
from jax.experimental import pallas as pl
from jax.experimental.pallas import tpu as pltpu
from jax.sharding import PartitionSpec as P

N_X, N_Y, N_Z, N_C = 4, 4, 4, 2
TOK, WID, FFL = 512, 640, 5120
HALF = FFL // 2
TILE = 1280
TILES = FFL // TILE
AXES = ("row", "col")
F32, BF16 = jnp.float32, jnp.bfloat16
LIMIT = 24 * 2**20
STEPS = (
    ("h", "gather_z"),
    ("g", "gather_z"),
    ("h", "gather_core"),
    ("h", "partials"),
    ("g", "gather_core"),
    ("h", "send_far"),
    ("g", "partials"),
    ("h", "send_near"),
    ("g", "send_far"),
    ("g", "send_near"),
    ("h", "send_second"),
    ("g", "send_second"),
    ("h", "sum_second"),
    ("g", "sum_second"),
    ("", "activate"),
    ("g", "gather_near"),
    ("h", "gather_near"),
    ("g", "gather_far"),
    ("", "near_input_grads"),
    ("h", "gather_far"),
    ("", "far_input_grads"),
    ("", "grad_w_out"),
    ("", "sum_cores"),
    ("", "grad_w_in"),
    ("", "sum_z"),
)


def neighbours(move):
    pairs = []
    for x in range(N_X):
        for y in range(N_Y):
            for z in range(N_Z):
                for c in range(N_C):
                    nx, ny, nz, nc = move(x, y, z, c)
                    here = ((x * N_Y + y) * N_Z + z) * N_C + c
                    there = (((nx % N_X) * N_Y + ny % N_Y) * N_Z + nz % N_Z) * N_C + nc % N_C
                    pairs.append((here, there))
    return pairs


def hop(value, step, first):
    def move(x, y, z, c):
        return (x + step, y, z, c) if (c == 0) == first else (x, y + step, z, c)

    return lax.ppermute(value, AXES, neighbours(move))


def hop_z(value, step):
    return lax.ppermute(value, AXES, neighbours(lambda x, y, z, c: (x, y, z + step, c)))


def swap_core(value):
    return lax.ppermute(value, AXES, neighbours(lambda x, y, z, c: (x, y, z, c + 1)))


def add(*terms):
    total = terms[0].astype(F32)
    for term in terms[1:]:
        total = total + term.astype(F32)
    return total


def gelu_parts(hidden):
    normal_cdf = 0.5 * (1.0 + jax.scipy.special.erf(hidden / math.sqrt(2.0)))
    density = jnp.exp(-0.5 * hidden * hidden) / math.sqrt(2.0 * math.pi)
    return (hidden * normal_cdf, normal_cdf + hidden * density)


def store_partials(term, far_left_ref, far_right_ref, p1_ref, p3_ref, p0_ref):
    tile = pl.program_id(0)
    p0_ref[...] = term[0:128]
    p1_ref[...] = term[128:256]
    p3_ref[...] = term[384:512]

    @pl.when(tile < TILES // 2)
    def _():
        far_left_ref[...] = term[256:384]

    @pl.when(tile >= TILES // 2)
    def _():
        far_right_ref[...] = term[256:384]


def partial_kernel(hidden, order_ref, all_ref, w_ref, rows_ref, *outs):
    @pl.when(pl.program_id(0) == 0)
    def _():
        for block in range(16):
            start = pl.multiple_of(order_ref[block] * 32, 32)
            rows_ref[block * 32 : (block + 1) * 32, :] = all_ref[pl.ds(start, 32), :]

    sides = (((1,), (0 if hidden else 1,)), ((), ()))
    term = lax.dot_general(rows_ref[...], w_ref[...], sides, preferred_element_type=F32)
    store_partials(term.astype(BF16), *outs)


def partials(hidden, order, tokens, weight):
    whole = pl.BlockSpec((TOK, WID), lambda i: (0, 0))
    rows = jax.ShapeDtypeStruct((TOK, WID), BF16)
    half = jax.ShapeDtypeStruct((128, HALF), BF16)
    block = jax.ShapeDtypeStruct((128, FFL), BF16)
    spec = pl.BlockSpec((128, TILE), lambda i: (0, i))
    left = pl.BlockSpec((128, TILE), lambda i: (0, jnp.minimum(i, TILES // 2 - 1)))
    right = pl.BlockSpec((128, TILE), lambda i: (0, jnp.maximum(i - TILES // 2, 0)))
    return pl.pallas_call(
        functools.partial(partial_kernel, hidden),
        grid=(TILES,),
        out_shape=(rows, half, half, block, block, block),
        in_specs=[
            pl.BlockSpec(memory_space=pltpu.SMEM),
            whole,
            pl.BlockSpec((WID, TILE), lambda i: (0, i))
            if hidden
            else pl.BlockSpec((TILE, WID), lambda i: (i, 0)),
        ],
        out_specs=(whole, left, right, spec, spec, spec),
        compiler_params=pltpu.CompilerParams(vmem_limit_bytes=LIMIT),
        cost_estimate=pl.CostEstimate(
            flops=2 * TOK * WID * FFL, bytes_accessed=2 * (TOK + WID) * FFL, transcendentals=0
        ),
        name="hidden_partials" if hidden else "grad_partials",
    )(order, tokens, weight)


def near_input_grads_kernel(wi_ref, b0_ref, b1_ref, b3_ref, out_ref):
    @pl.when(pl.program_id(0) == 0)
    def _():
        out_ref[...] = jnp.zeros_like(out_ref)

    grad = jnp.concatenate([b0_ref[...], b1_ref[...], b3_ref[...]], axis=0)
    out_ref[...] += lax.dot_general(grad, wi_ref[...], (((1,), (1,)), ((), ())), preferred_element_type=F32)


def far_input_grads_kernel(order_ref, wi_ref, b2_ref, near_ref, out_ref, total):
    @pl.when(pl.program_id(0) == 0)
    def _():
        total[...] = jnp.zeros_like(total)

    total[...] += lax.dot_general(
        b2_ref[...], wi_ref[...], (((1,), (1,)), ((), ())), preferred_element_type=F32
    )

    @pl.when(pl.program_id(0) == pl.num_programs(0) - 1)
    def _():
        for block in range(16):
            rows = pl.ds(pl.multiple_of(order_ref[block] * 32, 32), 32)
            low = (block % 4) * 32
            if block // 4 == 2:
                term = total[low : low + 32, :]
            else:
                low += (0, 128, 0, 256)[block // 4]
                term = near_ref[low : low + 32, :]
            out_ref[rows, :] = term.astype(BF16)


def input_grads(w_in, blocks, near=None, order=None):
    last = near is not None
    whole = lambda rows: pl.BlockSpec((rows, WID), lambda i: (0, 0))
    return pl.pallas_call(
        far_input_grads_kernel if last else near_input_grads_kernel,
        grid=(TILES,),
        out_shape=jax.ShapeDtypeStruct((TOK, WID), BF16) if last else jax.ShapeDtypeStruct((384, WID), F32),
        in_specs=([pl.BlockSpec(memory_space=pltpu.SMEM)] if last else [])
        + [pl.BlockSpec((WID, TILE), lambda i: (0, i))]
        + [pl.BlockSpec((128, TILE), lambda i: (0, i)) for _ in blocks]
        + ([whole(384)] if last else []),
        out_specs=whole(TOK if last else 384),
        scratch_shapes=[pltpu.VMEM((128, WID), F32)] if last else [],
        compiler_params=pltpu.CompilerParams(vmem_limit_bytes=LIMIT),
        cost_estimate=pl.CostEstimate(
            flops=2 * 128 * len(blocks) * WID * FFL, bytes_accessed=2 * (TOK + WID) * FFL, transcendentals=0
        ),
        name="far_input_grads" if last else "near_input_grads",
    )(*((order,) if last else ()), w_in, *blocks, *((near,) if last else ()))


def w_out_kernel(c_ref, b0_ref, b1_ref, b2_ref, b3_ref, out_ref):
    act = jnp.concatenate([b0_ref[...], b1_ref[...], b2_ref[...], b3_ref[...]], axis=0)
    out_ref[...] = lax.dot_general(
        act, c_ref[...], (((0,), (0,)), ((), ())), preferred_element_type=F32
    ).astype(BF16)


def w_in_kernel(x_ref, b0_ref, b1_ref, b2_ref, b3_ref, out_ref):
    grad = jnp.concatenate([b0_ref[...], b1_ref[...], b2_ref[...], b3_ref[...]], axis=0)
    out_ref[...] = lax.dot_general(
        x_ref[...], grad, (((0,), (0,)), ((), ())), preferred_element_type=F32
    ).astype(BF16)


def weight_grads(outer, rows, blocks):
    return pl.pallas_call(
        w_out_kernel if outer else w_in_kernel,
        grid=(TILES,),
        out_shape=jax.ShapeDtypeStruct((FFL, WID) if outer else (WID, FFL), BF16),
        in_specs=[pl.BlockSpec((TOK, WID), lambda i: (0, 0))]
        + [pl.BlockSpec((128, TILE), lambda i: (0, i))] * 4,
        out_specs=(
            pl.BlockSpec((TILE, WID), lambda i: (i, 0))
            if outer
            else pl.BlockSpec((WID, TILE), lambda i: (0, i))
        ),
        compiler_params=pltpu.CompilerParams(vmem_limit_bytes=LIMIT),
        cost_estimate=pl.CostEstimate(
            flops=2 * TOK * WID, bytes_accessed=2 * (TOK + WID), transcendentals=0
        ),
        name="grad_w_out" if outer else "grad_w_in",
    )(rows, *blocks)


class Stream:
    def __init__(self, hidden, tokens, weight):
        self.hidden, self.own, self.weight = hidden, tokens, weight

    def gather_z(self, env):
        self.came = tuple(hop_z(self.own, step) for step in (2, 1, -1))
        return ()

    def gather_core(self, env):
        far, left, right = env.after(self.came)
        self.own = jnp.concatenate([self.own, right, far, left], axis=0)
        self.came = swap_core(self.own)
        return (self.own,)

    def partials(self, env):
        tokens = jnp.concatenate([self.own, env.after(self.came)], axis=0)
        self.rows, *parts = partials(self.hidden, env.order, tokens, self.weight)
        self.far_left, self.far_right, self.p1, self.p3, self.p0 = parts
        return parts

    def send_far(self, env):
        left, right = env.after((self.far_left, self.far_right))
        self.came = hop(left, 1, True), hop(right, -1, True)

    def send_near(self, env):
        from_left, from_right = env.after(self.came)
        right = jnp.concatenate([add(self.p1[:, :HALF], from_left).astype(BF16), self.p1[:, HALF:]], axis=1)
        left = jnp.concatenate([self.p3[:, :HALF], add(self.p3[:, HALF:], from_right).astype(BF16)], axis=1)
        self.came = hop(right, 1, True), hop(left, -1, True)
        return right, left

    def send_second(self, env):
        from_left, from_right = env.after(self.came)
        q = add(self.p0, from_left, from_right).astype(BF16)
        blocks = [q[32 * i : 32 * (i + 1)] for i in range(4)]
        self.own = blocks[0]
        self.came = tuple(hop(blocks[i], step, False) for i, step in ((2, 2), (1, 1), (3, -1)))
        return (q,)

    def sum_second(self, env):
        self.own = add(self.own, *env.after(self.came))
        return (self.own,)

    def send_own(self):
        self.came = tuple(hop(self.own, step, False) for step in (2, 1, -1))

    def gather_near(self, env):
        far, left, right = env.after(self.came)
        self.quarter = jnp.concatenate([self.own, right, far, left], axis=0)
        self.came = hop(self.quarter, 1, True), hop(self.quarter, -1, True)
        return (self.quarter,)

    def gather_far(self, env):
        self.left, self.right = env.after(self.came)
        halves = self.left[:, :HALF], self.right[:, HALF:]
        self.came = hop(halves[0], 1, True), hop(halves[1], -1, True)
        return halves

    def blocks(self, env):
        far = jnp.concatenate(env.after(self.came), axis=1)
        return self.quarter, self.right, far, self.left


class Env:
    def __init__(self, **given):
        self.__dict__.update(given)
        self.last = ()

    def after(self, values):
        return lax.optimization_barrier((values, self.last))[0] if self.last else values

    def activate(self, env):
        activated, derivative = gelu_parts(self.h.own)
        self.h.own, self.g.own = activated.astype(BF16), (self.g.own * derivative).astype(BF16)
        self.g.send_own()
        self.h.send_own()
        return self.g.own, self.h.own

    def near_input_grads(self, env):
        g = self.g
        self.near = input_grads(self.w_in, env.after((g.quarter, g.right, g.left)))
        return (self.near,)

    def far_input_grads(self, env):
        self.grad_blocks = self.g.blocks(env)
        sums = input_grads(self.w_in, self.grad_blocks[2:3], self.near, self.order)
        self.sums = sums.reshape(2, N_Z, 64, WID)
        self.swapped = swap_core(self.sums[1])
        return (self.sums,)

    def grad_w_in(self, env):
        self.w_in_result = weight_grads(False, env.after(self.h.rows), self.grad_blocks)
        return (self.w_in_result,)

    def sum_cores(self, env):
        total = add(self.sums[0], env.after(self.swapped)).astype(BF16)
        self.kept = total[0]
        self.crossed = tuple(hop_z(total[step % N_Z], step) for step in (2, 1, -1))
        return (total,)

    def grad_w_out(self, env):
        self.w_out_result = weight_grads(True, self.g.rows, self.h.blocks(env))
        return (self.w_out_result,)

    def sum_z(self, env):
        self.inputs_result = add(self.kept, *env.after(self.crossed)).astype(BF16)
        return (self.inputs_result,)


def shards(inputs, cotangent, w_in, w_out):
    row, col = lax.axis_index("row"), lax.axis_index("col")
    x, y, z, core = row // N_Y, row % N_Y, col // N_C, col % N_C
    o = jnp.arange(16, dtype=jnp.int32)
    ox = jnp.where(core == 0, o // 4, o % 4)
    oy = jnp.where(core == 0, o % 4, o // 4)
    block = ((x + ox) % N_X) * N_Y + (y + oy) % N_Y
    other = (block // 2 + core) % N_C
    order = (other * N_Z + (block // 4 - z) % N_Z) * 2 + block % 2

    env = Env(order=order, w_in=w_in, h=Stream(True, inputs, w_in), g=Stream(False, cotangent, w_out))
    for where, step in STEPS:
        env.last = getattr(getattr(env, where) if where else env, step)(env) or env.last
    return env.inputs_result, env.w_in_result, env.w_out_result


def solution(mesh):
    in_specs = (P("col", "row"), P("col", "row"), P("row", "col"), P("col", "row"))
    out_specs = (P("col", "row"), P("row", "col"), P("col", "row"))
    return jax.shard_map(shards, mesh=mesh, in_specs=in_specs, out_specs=out_specs, check_vma=False)
```

time: 351 us -> 182 us (0.52)
  waiting for transfers between devices: 250 us -> 82.9 us
  starting transfers between devices: 0.38 us -> 54.5 us
  matrix products: 46.5 us -> 0 us
  Pallas kernels: 0 us -> 33.4 us
  blocking collectives: 28 us -> 0 us
  between operations: 13.8 us -> 1.06 us
  local copies, waits for them, and re-layouts: 9.57 us -> 5.64 us
    reduce_scatter x3 -> x0, waiting for transfers between devices: 165 us -> none  [the longest x1 82.2 us: shards(): lax.psum_scatter(jnp.dot(inputs_all, w_in, preferred_element_type=jnp.flo...]
    all_gather x2 -> x0, waiting for transfers between devices: 84.6 us -> none  [the longest x1 55.4 us: shards(): lax.all_gather(grad_hidden_local, 'row', axis=0, tiled=True)]
    ppermute x0 -> x40, waiting for transfers between devices: none -> 82.9 us  [the longest x28 79.3 us: hop(): return lax.ppermute(value, AXES, neighbours(move))]
    ppermute x0 -> x40, starting transfers between devices: none -> 54.5 us  [the longest x28 39.8 us: hop(): return lax.ppermute(value, AXES, neighbours(move))]
    dot_general x5 -> x0, matrix products: 46.5 us -> none  [the longest x1 9.76 us: shards(): lax.dot_general(inputs_all, grad_hidden_all, (((0,), (0,)), ((), ())), pr...]
    pallas_call x0 -> x6, Pallas kernels: none -> 33.4 us  [the longest x2 12.6 us: partials(): pl.pallas_call(functools.partial(partial_kernel, hidden), grid=(TILES,),...]
    all_gather x2 -> x0, blocking collectives: 28 us -> none  [the longest x1 14.7 us: shards(): lax.all_gather(cotangent, 'col', axis=0, tiled=True)]
    unnamed x3 -> x16, local copies, waits for them, and re-layouts: 9.57 us -> 4.91 us
  transfers between devices with their start and end apart: 5 -> 40, of which waited for: 5 -> 21; matrix products, arithmetic and copies ran while one was open for 13% -> 3% of each run, Pallas kernels for 0% -> 18%
where the time goes in v2:
time: 182 us
  waiting for transfers between devices  82.9 us (46%)
  starting transfers between devices  54.5 us (30%)
  Pallas kernels  33.4 us (18%)
  local copies, waits for them, and re-layouts  5.64 us (3%)
  other arithmetic  4.17 us (2%)
    ppermute x28, waiting for transfers between devices, hop(): return lax.ppermute(value, AXES, neighbours(move))  79.3 us
    ppermute x28, starting transfers between devices, hop(): return lax.ppermute(value, AXES, neighbours(move))  39.8 us
    ppermute x9, starting transfers between devices, hop_z(): lax.ppermute(value, AXES, neighbours(lambda x, y, z, c: (x, y, z + step,...  14.4 us
    pallas_call x2, Pallas kernels, partials(): pl.pallas_call(functools.partial(partial_kernel, hidden), grid=(TILES,),...  12.6 us
    pallas_call x2, Pallas kernels, weight_grads(): pl.pallas_call(w_out_kernel if outer else w_in_kernel, grid=(TILES,), out...  12.4 us
    pallas_call x2, Pallas kernels, input_grads(): pl.pallas_call(far_input_grads_kernel if last else near_input_grads_kerne...  8.45 us
    unnamed x16, local copies, waits for them, and re-layouts  4.91 us
  transfers between devices with their start and end apart: 40, of which 21 were waited for; matrix products, arithmetic and copies ran while one was open for 3% of the time, Pallas kernels for 18%

profile of v2, /device:TPU:0, one launch (start us, length us, event | category | flops | bytes accessed | tf_op | source)
XLA Modules:
  0.0 181.6 jit_solution(14896054193588461109)
XLA Ops:
  0.6 4.0 %collective-permute-start.4 = (bf16[64,640]{1,0:T(8,128)(2,1)}, bf16[64,640]{1,0:T(8,128)(2,1)S(1)}, u32[]{:S(2)}, u32[]{:S(2)}) collective-permute-start(bf16[64,640]{1,0:T(8,128)(2,1)} %param.4), channel_id=1, source_target_pairs={{0,4},{1,5},{2,6},{3,7},{4,0},{5,1},{6,2},{7,3},{8,12},{9,13},{10,... | collective-permute-start | bytes 245768 | tf_op jit(solution)/shard_map/ppermute | solution.py:69
  11.5 2.7 %collective-permute-start = (bf16[64,640]{1,0:T(8,128)(2,1)}, bf16[64,640]{1,0:T(8,128)(2,1)S(1)}, u32[]{:S(2)}, u32[]{:S(2)}) collective-permute-start(bf16[64,640]{1,0:T(8,128)(2,1)} %param.5), channel_id=1, source_target_pairs={{0,4},{1,5},{2,6},{3,7},{4,0},{5,1},{6,2},{7,3},{8,12},{9,13},{10,... | collective-permute-start | bytes 245768 | tf_op jit(solution)/shard_map/ppermute | solution.py:69
  16.3 2.9 %copy-done = bf16[640,5120]{1,0:T(8,128)(2,1)S(1)} copy-done((bf16[640,5120]{1,0:T(8,128)(2,1)S(1)}, bf16[640,5120]{1,0:T(8,128)(2,1)}, u32[]{:S(2)}) %copy-start) | copy-done | bytes 6553624
  19.2 6.4 %hidden_partials.1 = (bf16[512,640]{1,0:T(8,128)(2,1)S(1)}, bf16[128,2560]{1,0:T(8,128)(2,1)S(1)}, bf16[128,2560]{1,0:T(8,128)(2,1)S(1)}, bf16[128,5120]{1,0:T(8...) custom-call(s32[16]{0:T(128)S(1)} %fusion.12.order_ref, ...), custom_call_target="tpu_custom_call" | custom-call | flops 3355443200 | bytes 11796480 | tf_op jit(solution)/shard_map/hidden_partials/pallas_call | solution.py:124
  29.3 6.2 %grad_partials.1 = (bf16[512,640]{1,0:T(8,128)(2,1)S(1)}, bf16[128,2560]{1,0:T(8,128)(2,1)S(1)}, bf16[128,2560]{1,0:T(8,128)(2,1)S(1)}, bf16[128,5120]{1,0:T(8,1...) custom-call(s32[16]{0:T(128)S(1)} %fusion.12.order_ref, ...), custom_call_target="tpu_custom_call" | custom-call | flops 3355443200 | bytes 11796480 | tf_op jit(solution)/shard_map/grad_partials/pallas_call | solution.py:124
  35.5 2.2 %collective-permute-done.8 = bf16[128,2560]{1,0:T(8,128)(2,1)S(1)} collective-permute-done((bf16[128,2560]{1,0:T(8,128)(2,1)S(1)}, bf16[128,2560]{1,0:T(8,128)(2,1)S(1)}, u32[]{:S(2)}, u32[]{:S(2)}) %collective-permute-start.8) | collective-permute-done | bytes 655392 | tf_op jit(solution)/shard_map/ppermute | solution.py:65
  44.0 6.4 %collective-permute-done.10 = bf16[128,2560]{1,0:T(8,128)(2,1)S(1)} collective-permute-done((bf16[128,2560]{1,0:T(8,128)(2,1)S(1)}, bf16[128,2560]{1,0:T(8,128)(2,1)S(1)}, u32[]{:S(2)}, u32[]{:S(2)}) %collective-permute-start.10) | collective-permute-done | bytes 655392 | tf_op jit(solution)/shard_map/ppermute | solution.py:65
  51.0 3.0 %collective-permute-start.13 = (bf16[128,5120]{1,0:T(8,128)(2,1)S(1)}, bf16[128,5120]{1,0:T(8,128)(2,1)S(1)}, u32[]{:S(2)}, u32[]{:S(2)}) collective-permute-start(bf16[128,5120]{1,0:T(8,128)(2,1)S(1)} %pad_maximum_fusion.3), channel_id=1, source_target_pairs={{0,96},{1,25},{2,98},{3,27},{4,100},{5,29},{6,102},{7,31},{8,104},... | collective-permute-start | bytes 3932168 | tf_op jit(solution)/shard_map/ppermute | solution.py:65
  54.4 10.3 %collective-permute-done.15 = bf16[128,5120]{1,0:T(8,128)(2,1)S(1)} collective-permute-done((bf16[128,5120]{1,0:T(8,128)(2,1)S(1)}, bf16[128,5120]{1,0:T(8,128)(2,1)S(1)}, u32[]{:S(2)}, u32[]{:S(2)}) %collective-permute-start.15) | collective-permute-done | bytes 1310752 | tf_op jit(solution)/shard_map/ppermute | solution.py:65
  65.4 3.1 %collective-permute-start.21 = (bf16[32,5120]{1,0:T(8,128)(2,1)S(1)}, bf16[32,5120]{1,0:T(8,128)(2,1)S(1)}, u32[]{:S(2)}, u32[]{:S(2)}) collective-permute-start(bf16[32,5120]{1,0:T(8,128)(2,1)S(1)} %get-tuple-element.122), channel_id=1, source_target_pairs={{0,24},{1,97},{2,26},{3,99},{4,28},{5,101},{6,30},{7,103},{8,0},{9... | collective-permute-start | bytes 983048 | tf_op jit(solution)/shard_map/ppermute | solution.py:65
  68.5 2.2 %collective-permute-start.19 = (bf16[32,5120]{1,0:T(8,128)(2,1)S(1)}, bf16[32,5120]{1,0:T(8,128)(2,1)S(1)}, u32[]{:S(2)}, u32[]{:S(2)}) collective-permute-start(bf16[32,5120]{1,0:T(8,128)(2,1)S(1)} %get-tuple-element.124), channel_id=1, source_target_pairs={{0,16},{1,65},{2,18},{3,67},{4,20},{5,69},{6,22},{7,71},{8,24},{9,... | collective-permute-start | bytes 983048 | tf_op jit(solution)/shard_map/ppermute | solution.py:65
  70.7 15.1 %collective-permute-done.13 = bf16[128,5120]{1,0:T(8,128)(2,1)S(1)} collective-permute-done((bf16[128,5120]{1,0:T(8,128)(2,1)S(1)}, bf16[128,5120]{1,0:T(8,128)(2,1)S(1)}, u32[]{:S(2)}, u32[]{:S(2)}) %collective-permute-start.13) | collective-permute-done | bytes 1310752 | tf_op jit(solution)/shard_map/ppermute | solution.py:65
  86.5 3.3 %collective-permute-start.18 = (bf16[32,5120]{1,0:T(8,128)(2,1)S(1)}, bf16[32,5120]{1,0:T(8,128)(2,1)S(1)}, u32[]{:S(2)}, u32[]{:S(2)}) collective-permute-start(bf16[32,5120]{1,0:T(8,128)(2,1)S(1)} %get-tuple-element.119), channel_id=1, source_target_pairs={{0,24},{1,97},{2,26},{3,99},{4,28},{5,101},{6,30},{7,103},{8,0},{9... | collective-permute-start | bytes 983048 | tf_op jit(solution)/shard_map/ppermute | solution.py:65
  89.7 2.2 %collective-permute-start.16 = (bf16[32,5120]{1,0:T(8,128)(2,1)S(1)}, bf16[32,5120]{1,0:T(8,128)(2,1)S(1)}, u32[]{:S(2)}, u32[]{:S(2)}) collective-permute-start(bf16[32,5120]{1,0:T(8,128)(2,1)S(1)} %get-tuple-element.121), channel_id=1, source_target_pairs={{0,16},{1,65},{2,18},{3,67},{4,20},{5,69},{6,22},{7,71},{8,24},{9,... | collective-permute-start | bytes 983048 | tf_op jit(solution)/shard_map/ppermute | solution.py:65
  94.3 7.2 %collective-permute-done.17 = bf16[32,5120]{1,0:T(8,128)(2,1)S(1)} collective-permute-done((bf16[32,5120]{1,0:T(8,128)(2,1)S(1)}, bf16[32,5120]{1,0:T(8,128)(2,1)S(1)}, u32[]{:S(2)}, u32[]{:S(2)}) %collective-permute-start.17) | collective-permute-done | bytes 327712 | tf_op jit(solution)/shard_map/ppermute | solution.py:65
  104.3 2.4 %collective-permute-start.29 = (bf16[32,5120]{1,0:T(8,128)(2,1)S(1)}, bf16[32,5120]{1,0:T(8,128)(2,1)S(1)}, u32[]{:S(2)}, u32[]{:S(2)}) collective-permute-start(bf16[32,5120]{1,0:T(8,128)(2,1)S(1)} %get-tuple-element.117), channel_id=1, source_target_pairs={{0,24},{1,97},{2,26},{3,99},{4,28},{5,101},{6,30},{7,103},{8,0},{9... | collective-permute-start | bytes 983048 | tf_op jit(solution)/shard_map/ppermute | solution.py:65
  106.7 2.4 %collective-permute-done.24 = bf16[32,5120]{1,0:T(8,128)(2,1)S(1)} collective-permute-done((bf16[32,5120]{1,0:T(8,128)(2,1)S(1)}, bf16[32,5120]{1,0:T(8,128)(2,1)S(1)}, u32[]{:S(2)}, u32[]{:S(2)}) %collective-permute-start.24) | collective-permute-done | bytes 327712 | tf_op jit(solution)/shard_map/ppermute | solution.py:65
  109.6 4.3 %collective-permute-done.23 = bf16[32,5120]{1,0:T(8,128)(2,1)S(1)} collective-permute-done((bf16[32,5120]{1,0:T(8,128)(2,1)S(1)}, bf16[32,5120]{1,0:T(8,128)(2,1)S(1)}, u32[]{:S(2)}, u32[]{:S(2)}) %collective-permute-start.23) | collective-permute-done | bytes 327712 | tf_op jit(solution)/shard_map/ppermute | solution.py:65
  114.0 3.0 %collective-permute-start.26 = (bf16[128,5120]{1,0:T(8,128)(2,1)S(1)}, bf16[128,5120]{1,0:T(8,128)(2,1)S(1)}, u32[]{:S(2)}, u32[]{:S(2)}) collective-permute-start(bf16[128,5120]{1,0:T(8,128)(2,1)S(1)} %pad_maximum_fusion.4.b0_ref), channel_id=1, source_target_pairs={{0,96},{1,25},{2,98},{3,27},{4,100},{5,29},{6,102},{7,31},{8,104},... | collective-permute-start | bytes 3932168 | tf_op jit(solution)/shard_map/ppermute | solution.py:65
  117.0 2.5 %collective-permute-done.29 = bf16[32,5120]{1,0:T(8,128)(2,1)S(1)} collective-permute-done((bf16[32,5120]{1,0:T(8,128)(2,1)S(1)}, bf16[32,5120]{1,0:T(8,128)(2,1)S(1)}, u32[]{:S(2)}, u32[]{:S(2)}) %collective-permute-start.29) | collective-permute-done | bytes 327712 | tf_op jit(solution)/shard_map/ppermute | solution.py:65
  119.5 5.7 %collective-permute-done.27 = bf16[32,5120]{1,0:T(8,128)(2,1)S(1)} collective-permute-done((bf16[32,5120]{1,0:T(8,128)(2,1)S(1)}, bf16[32,5120]{1,0:T(8,128)(2,1)S(1)}, u32[]{:S(2)}, u32[]{:S(2)}) %collective-permute-start.27) | collective-permute-done | bytes 327712 | tf_op jit(solution)/shard_map/ppermute | solution.py:65
  125.3 4.8 %collective-permute-start.33 = (bf16[128,5120]{1,0:T(8,128)(2,1)S(1)}, bf16[128,5120]{1,0:T(8,128)(2,1)S(1)}, u32[]{:S(2)}, u32[]{:S(2)}) collective-permute-start(bf16[128,5120]{1,0:T(8,128)(2,1)S(1)} %pad_maximum_fusion.5.b0_ref), channel_id=1, source_target_pairs={{0,96},{1,25},{2,98},{3,27},{4,100},{5,29},{6,102},{7,31},{8,104},... | collective-permute-start | bytes 3932168 | tf_op jit(solution)/shard_map/ppermute | solution.py:65
  132.1 3.7 %collective-permute-done.25.b3_ref = bf16[128,5120]{1,0:T(8,128)(2,1)S(1)} collective-permute-done((bf16[128,5120]{1,0:T(8,128)(2,1)S(1)}, bf16[128,5120]{1,0:T(8,128)(2,1)S(1)}, u32[]{:S(2)}, u32[]{:S(2)}) %collective-permute-start.25) | collective-permute-done | bytes 1310752 | tf_op jit(solution)/shard_map/ppermute | solution.py:65
  138.0 4.7 %near_input_grads.1.near_ref = f32[384,640]{1,0:T(8,128)S(1)} custom-call(bf16[640,5120]{1,0:T(8,128)(2,1)S(1)} %bitcast.15, bf16[128,5120]{1,0:T(8,128)(2,1)S(1)} %pad_maximum_fusion.4.b0_ref, bf16[128,5120]{1,0:T(8,128)(2,1)S(1)} %collective-permute-done.26.b1_ref, bf16[128,5120]{1,0:T(8,128)(2,1)S(1)} %collective-permute-done.25.b3_ref), custom_call_target="tpu_custom_call" | custom-call | flops 2516582400 | bytes 11796480 | tf_op jit(solution)/shard_map/near_input_grads/pallas_call | solution.py:178
  142.8 3.4 %collective-permute-done.33.b1_ref = bf16[128,5120]{1,0:T(8,128)(2,1)S(1)} collective-permute-done((bf16[128,5120]{1,0:T(8,128)(2,1)S(1)}, bf16[128,5120]{1,0:T(8,128)(2,1)S(1)}, u32[]{:S(2)}, u32[]{:S(2)}) %collective-permute-start.33) | collective-permute-done | bytes 1310752 | tf_op jit(solution)/shard_map/ppermute | solution.py:65
  146.2 3.7 %collective-permute-done.32.b3_ref = bf16[128,5120]{1,0:T(8,128)(2,1)S(1)} collective-permute-done((bf16[128,5120]{1,0:T(8,128)(2,1)S(1)}, bf16[128,5120]{1,0:T(8,128)(2,1)S(1)}, u32[]{:S(2)}, u32[]{:S(2)}) %collective-permute-start.32) | collective-permute-done | bytes 1310752 | tf_op jit(solution)/shard_map/ppermute | solution.py:65
  153.2 3.7 %collective-permute-done.30 = bf16[128,2560]{1,0:T(8,128)(2,1)S(1)} collective-permute-done((bf16[128,2560]{1,0:T(8,128)(2,1)S(1)}, bf16[128,2560]{1,0:T(8,128)(2,1)S(1)}, u32[]{:S(2)}, u32[]{:S(2)}) %collective-permute-start.30) | collective-permute-done | bytes 655392 | tf_op jit(solution)/shard_map/ppermute | solution.py:65
  157.0 3.7 %far_input_grads.1 = bf16[512,640]{1,0:T(8,128)(2,1)S(1)} custom-call(s32[16]{0:T(128)S(1)} %fusion.12.order_ref, bf16[640,5120]{1,0:T(8,128)(2,1)S(1)} %bitcast.15, bf16[128,5120]{1,0:T(8,128)(2,1)S(1)} %constant_dynamic-update-slice_fusion.18.b2_ref, f32[384,640]{1,0:T(8,128)S(1)} %near_input_grads.1.near_ref), custom_call_target="tpu_custom_call" | custom-call | flops 838860800 | bytes 11796480 | tf_op jit(solution)/shard_map/far_input_grads/pallas_call | solution.py:178
  160.9 3.0 %collective-permute-done.35 = bf16[128,2560]{1,0:T(8,128)(2,1)S(1)} collective-permute-done((bf16[128,2560]{1,0:T(8,128)(2,1)S(1)}, bf16[128,2560]{1,0:T(8,128)(2,1)S(1)}, u32[]{:S(2)}, u32[]{:S(2)}) %collective-permute-start.35) | collective-permute-done | bytes 655392 | tf_op jit(solution)/shard_map/ppermute | solution.py:65
  164.1 6.5 %grad_w_out.1 = bf16[5120,640]{1,0:T(8,128)(2,1)} custom-call(bf16[512,640]{1,0:T(8,128)(2,1)S(1)} %get-tuple-element.108.c_ref, bf16[128,5120]{1,0:T(8,128)(2,1)S(1)} %pad_maximum_fusion.5.b0_ref, bf16[128,5120]{1,0:T(8,128)(2,1)S(1)} %collective-permute-done.33.b1_ref, bf16[128,5120]{1,0:T(8,128)(2,1)S(1)} %pad_maximum_fusion.6.b2_ref, ...), custom_call_target="tpu_custom_call" | custom-call | flops 655360 | bytes 2304 | tf_op jit(solution)/shard_map/grad_w_out/pallas_call | solution.py:211
  172.8 2.3 %collective-permute-start.37 = (bf16[64,640]{1,0:T(8,128)(2,1)S(1)}, bf16[64,640]{1,0:T(8,128)(2,1)S(1)}, u32[]{:S(2)}, u32[]{:S(2)}) collective-permute-start(bf16[64,640]{1,0:T(8,128)(2,1)S(1)} %get-tuple-element.129), channel_id=1, source_target_pairs={{0,4},{1,5},{2,6},{3,7},{4,0},{5,1},{6,2},{7,3},{8,12},{9,13},{10,... | collective-permute-start | bytes 245768 | tf_op jit(solution)/shard_map/ppermute | solution.py:69
  175.1 5.8 %grad_w_in.1 = bf16[640,5120]{1,0:T(8,128)(2,1)} custom-call(bf16[512,640]{1,0:T(8,128)(2,1)S(1)} %get-tuple-element.113.x_ref, bf16[128,5120]{1,0:T(8,128)(2,1)S(1)} %pad_maximum_fusion.4.b0_ref, bf16[128,5120]{1,0:T(8,128)(2,1)S(1)} %collective-permute-done.26.b1_ref, bf16[128,5120]{1,0:T(8,128)(2,1)S(1)} %constant_dynamic-update-slice_fusion.18.b2_ref, ...), custom_call_target="tpu_custom_call" | custom-call | flops 655360 | bytes 2304 | tf_op jit(solution)/shard_map/grad_w_in/pallas_call | solution.py:211
  (105 shorter events, 37.9 us)
Async XLA Ops:
  11.4 14.2 %collective-permute-start.1 = (bf16[64,640]{1,0:T(8,128)(2,1)}, bf16[64,640]{1,0:T(8,128)(2,1)S(1)}, u32[]{:S(2)}, u32[]{:S(2)}) collective-permute-start(bf16[64,640]{1,0:T(8,128)(2,1)} %param.5), channel_id=1, source_target_pairs={{0,2},{1,3},{2,4},{3,5},{4,6},{5,7},{6,0},{7,1},{8,10},{9,11},{10,... | collective-permute-start | bytes 245768 | tf_op jit(solution)/shard_map/ppermute | solution.py:69
  11.5 14.1 %collective-permute-start = (bf16[64,640]{1,0:T(8,128)(2,1)}, bf16[64,640]{1,0:T(8,128)(2,1)S(1)}, u32[]{:S(2)}, u32[]{:S(2)}) collective-permute-start(bf16[64,640]{1,0:T(8,128)(2,1)} %param.5), channel_id=1, source_target_pairs={{0,4},{1,5},{2,6},{3,7},{4,0},{5,1},{6,2},{7,3},{8,12},{9,13},{10,... | collective-permute-start | bytes 245768 | tf_op jit(solution)/shard_map/ppermute | solution.py:69
  14.2 11.4 %collective-permute-start.2 = (bf16[64,640]{1,0:T(8,128)(2,1)}, bf16[64,640]{1,0:T(8,128)(2,1)S(1)}, u32[]{:S(2)}, u32[]{:S(2)}) collective-permute-start(bf16[64,640]{1,0:T(8,128)(2,1)} %param.5), channel_id=1, source_target_pairs={{0,6},{1,7},{2,0},{3,1},{4,2},{5,3},{6,4},{7,5},{8,14},{9,15},{10,... | collective-permute-start | bytes 245768 | tf_op jit(solution)/shard_map/ppermute | solution.py:69
  25.8 11.9 %collective-permute-start.8 = (bf16[128,2560]{1,0:T(8,128)(2,1)S(1)}, bf16[128,2560]{1,0:T(8,128)(2,1)S(1)}, u32[]{:S(2)}, u32[]{:S(2)}) collective-permute-start(bf16[128,2560]{1,0:T(8,128)(2,1)S(1)} %get-tuple-element.74), channel_id=1, source_target_pairs={{0,32},{1,9},{2,34},{3,11},{4,36},{5,13},{6,38},{7,15},{8,40},{9,1... | collective-permute-start | bytes 1966088 | tf_op jit(solution)/shard_map/ppermute | solution.py:65
  27.3 10.6 %collective-permute-start.9 = (bf16[128,2560]{1,0:T(8,128)(2,1)S(1)}, bf16[128,2560]{1,0:T(8,128)(2,1)S(1)}, u32[]{:S(2)}, u32[]{:S(2)}) collective-permute-start(bf16[128,2560]{1,0:T(8,128)(2,1)S(1)} %get-tuple-element.75), channel_id=1, source_target_pairs={{0,96},{1,25},{2,98},{3,27},{4,100},{5,29},{6,102},{7,31},{8,104},... | collective-permute-start | bytes 1966088 | tf_op jit(solution)/shard_map/ppermute | solution.py:65
  38.5 11.9 %collective-permute-start.10 = (bf16[128,2560]{1,0:T(8,128)(2,1)S(1)}, bf16[128,2560]{1,0:T(8,128)(2,1)S(1)}, u32[]{:S(2)}, u32[]{:S(2)}) collective-permute-start(bf16[128,2560]{1,0:T(8,128)(2,1)S(1)} %get-tuple-element.79), channel_id=1, source_target_pairs={{0,32},{1,9},{2,34},{3,11},{4,36},{5,13},{6,38},{7,15},{8,40},{9,1... | collective-permute-start | bytes 1966088 | tf_op jit(solution)/shard_map/ppermute | solution.py:65
  40.1 10.6 %collective-permute-start.11 = (bf16[128,2560]{1,0:T(8,128)(2,1)S(1)}, bf16[128,2560]{1,0:T(8,128)(2,1)S(1)}, u32[]{:S(2)}, u32[]{:S(2)}) collective-permute-start(bf16[128,2560]{1,0:T(8,128)(2,1)S(1)} %get-tuple-element.80), channel_id=1, source_target_pairs={{0,96},{1,25},{2,98},{3,27},{4,100},{5,29},{6,102},{7,31},{8,104},... | collective-permute-start | bytes 1966088 | tf_op jit(solution)/shard_map/ppermute | solution.py:65
  41.9 22.8 %collective-permute-start.15 = (bf16[128,5120]{1,0:T(8,128)(2,1)S(1)}, bf16[128,5120]{1,0:T(8,128)(2,1)S(1)}, u32[]{:S(2)}, u32[]{:S(2)}) collective-permute-start(bf16[128,5120]{1,0:T(8,128)(2,1)S(1)} %pad_maximum_fusion.1), channel_id=1, source_target_pairs={{0,96},{1,25},{2,98},{3,27},{4,100},{5,29},{6,102},{7,31},{8,104},... | collective-permute-start | bytes 3932168 | tf_op jit(solution)/shard_map/ppermute | solution.py:65
  43.7 21.0 %collective-permute-start.14 = (bf16[128,5120]{1,0:T(8,128)(2,1)S(1)}, bf16[128,5120]{1,0:T(8,128)(2,1)S(1)}, u32[]{:S(2)}, u32[]{:S(2)}) collective-permute-start(bf16[128,5120]{1,0:T(8,128)(2,1)S(1)} %pad_maximum_fusion), channel_id=1, source_target_pairs={{0,32},{1,9},{2,34},{3,11},{4,36},{5,13},{6,38},{7,15},{8,40},{9,1... | collective-permute-start | bytes 3932168 | tf_op jit(solution)/shard_map/ppermute | solution.py:65
  51.0 34.8 %collective-permute-start.13 = (bf16[128,5120]{1,0:T(8,128)(2,1)S(1)}, bf16[128,5120]{1,0:T(8,128)(2,1)S(1)}, u32[]{:S(2)}, u32[]{:S(2)}) collective-permute-start(bf16[128,5120]{1,0:T(8,128)(2,1)S(1)} %pad_maximum_fusion.3), channel_id=1, source_target_pairs={{0,96},{1,25},{2,98},{3,27},{4,100},{5,29},{6,102},{7,31},{8,104},... | collective-permute-start | bytes 3932168 | tf_op jit(solution)/shard_map/ppermute | solution.py:65
  54.3 31.4 %collective-permute-start.12 = (bf16[128,5120]{1,0:T(8,128)(2,1)S(1)}, bf16[128,5120]{1,0:T(8,128)(2,1)S(1)}, u32[]{:S(2)}, u32[]{:S(2)}) collective-permute-start(bf16[128,5120]{1,0:T(8,128)(2,1)S(1)} %pad_maximum_fusion.2), channel_id=1, source_target_pairs={{0,32},{1,9},{2,34},{3,11},{4,36},{5,13},{6,38},{7,15},{8,40},{9,1... | collective-permute-start | bytes 3932168 | tf_op jit(solution)/shard_map/ppermute | solution.py:65
  65.4 24.3 %collective-permute-start.21 = (bf16[32,5120]{1,0:T(8,128)(2,1)S(1)}, bf16[32,5120]{1,0:T(8,128)(2,1)S(1)}, u32[]{:S(2)}, u32[]{:S(2)}) collective-permute-start(bf16[32,5120]{1,0:T(8,128)(2,1)S(1)} %get-tuple-element.122), channel_id=1, source_target_pairs={{0,24},{1,97},{2,26},{3,99},{4,28},{5,101},{6,30},{7,103},{8,0},{9... | collective-permute-start | bytes 983048 | tf_op jit(solution)/shard_map/ppermute | solution.py:65
  68.5 23.5 %collective-permute-start.20 = (bf16[32,5120]{1,0:T(8,128)(2,1)S(1)}, bf16[32,5120]{1,0:T(8,128)(2,1)S(1)}, u32[]{:S(2)}, u32[]{:S(2)}) collective-permute-start(bf16[32,5120]{1,0:T(8,128)(2,1)S(1)} %get-tuple-element.123), channel_id=1, source_target_pairs={{0,8},{1,33},{2,10},{3,35},{4,12},{5,37},{6,14},{7,39},{8,16},{9,4... | collective-permute-start | bytes 983048 | tf_op jit(solution)/shard_map/ppermute | solution.py:65
  68.5 23.5 %collective-permute-start.19 = (bf16[32,5120]{1,0:T(8,128)(2,1)S(1)}, bf16[32,5120]{1,0:T(8,128)(2,1)S(1)}, u32[]{:S(2)}, u32[]{:S(2)}) collective-permute-start(bf16[32,5120]{1,0:T(8,128)(2,1)S(1)} %get-tuple-element.124), channel_id=1, source_target_pairs={{0,16},{1,65},{2,18},{3,67},{4,20},{5,69},{6,22},{7,71},{8,24},{9,... | collective-permute-start | bytes 983048 | tf_op jit(solution)/shard_map/ppermute | solution.py:65
  89.7 11.8 %collective-permute-start.17 = (bf16[32,5120]{1,0:T(8,128)(2,1)S(1)}, bf16[32,5120]{1,0:T(8,128)(2,1)S(1)}, u32[]{:S(2)}, u32[]{:S(2)}) collective-permute-start(bf16[32,5120]{1,0:T(8,128)(2,1)S(1)} %get-tuple-element.120), channel_id=1, source_target_pairs={{0,8},{1,33},{2,10},{3,35},{4,12},{5,37},{6,14},{7,39},{8,16},{9,4... | collective-permute-start | bytes 983048 | tf_op jit(solution)/shard_map/ppermute | solution.py:65
  89.7 11.8 %collective-permute-start.16 = (bf16[32,5120]{1,0:T(8,128)(2,1)S(1)}, bf16[32,5120]{1,0:T(8,128)(2,1)S(1)}, u32[]{:S(2)}, u32[]{:S(2)}) collective-permute-start(bf16[32,5120]{1,0:T(8,128)(2,1)S(1)} %get-tuple-element.121), channel_id=1, source_target_pairs={{0,16},{1,65},{2,18},{3,67},{4,20},{5,69},{6,22},{7,71},{8,24},{9,... | collective-permute-start | bytes 983048 | tf_op jit(solution)/shard_map/ppermute | solution.py:65
  102.0 11.9 %collective-permute-start.23 = (bf16[32,5120]{1,0:T(8,128)(2,1)S(1)}, bf16[32,5120]{1,0:T(8,128)(2,1)S(1)}, u32[]{:S(2)}, u32[]{:S(2)}) collective-permute-start(bf16[32,5120]{1,0:T(8,128)(2,1)S(1)} %fusion.5), channel_id=1, source_target_pairs={{0,8},{1,33},{2,10},{3,35},{4,12},{5,37},{6,14},{7,39},{8,16},{9,4... | collective-permute-start | bytes 983048 | tf_op jit(solution)/shard_map/ppermute | solution.py:65
  104.0 9.9 %collective-permute-start.22 = (bf16[32,5120]{1,0:T(8,128)(2,1)S(1)}, bf16[32,5120]{1,0:T(8,128)(2,1)S(1)}, u32[]{:S(2)}, u32[]{:S(2)}) collective-permute-start(bf16[32,5120]{1,0:T(8,128)(2,1)S(1)} %fusion.5), channel_id=1, source_target_pairs={{0,16},{1,65},{2,18},{3,67},{4,20},{5,69},{6,22},{7,71},{8,24},{9,... | collective-permute-start | bytes 983048 | tf_op jit(solution)/shard_map/ppermute | solution.py:65
  104.3 15.2 %collective-permute-start.29 = (bf16[32,5120]{1,0:T(8,128)(2,1)S(1)}, bf16[32,5120]{1,0:T(8,128)(2,1)S(1)}, u32[]{:S(2)}, u32[]{:S(2)}) collective-permute-start(bf16[32,5120]{1,0:T(8,128)(2,1)S(1)} %get-tuple-element.117), channel_id=1, source_target_pairs={{0,24},{1,97},{2,26},{3,99},{4,28},{5,101},{6,30},{7,103},{8,0},{9... | collective-permute-start | bytes 983048 | tf_op jit(solution)/shard_map/ppermute | solution.py:65
  106.7 12.8 %collective-permute-start.28 = (bf16[32,5120]{1,0:T(8,128)(2,1)S(1)}, bf16[32,5120]{1,0:T(8,128)(2,1)S(1)}, u32[]{:S(2)}, u32[]{:S(2)}) collective-permute-start(bf16[32,5120]{1,0:T(8,128)(2,1)S(1)} %get-tuple-element.117), channel_id=1, source_target_pairs={{0,8},{1,33},{2,10},{3,35},{4,12},{5,37},{6,14},{7,39},{8,16},{9,4... | collective-permute-start | bytes 983048 | tf_op jit(solution)/shard_map/ppermute | solution.py:65
  109.1 16.1 %collective-permute-start.27 = (bf16[32,5120]{1,0:T(8,128)(2,1)S(1)}, bf16[32,5120]{1,0:T(8,128)(2,1)S(1)}, u32[]{:S(2)}, u32[]{:S(2)}) collective-permute-start(bf16[32,5120]{1,0:T(8,128)(2,1)S(1)} %get-tuple-element.117), channel_id=1, source_target_pairs={{0,16},{1,65},{2,18},{3,67},{4,20},{5,69},{6,22},{7,71},{8,24},{9,... | collective-permute-start | bytes 983048 | tf_op jit(solution)/shard_map/ppermute | solution.py:65
  114.0 18.2 %collective-permute-start.26 = (bf16[128,5120]{1,0:T(8,128)(2,1)S(1)}, bf16[128,5120]{1,0:T(8,128)(2,1)S(1)}, u32[]{:S(2)}, u32[]{:S(2)}) collective-permute-start(bf16[128,5120]{1,0:T(8,128)(2,1)S(1)} %pad_maximum_fusion.4.b0_ref), channel_id=1, source_target_pairs={{0,96},{1,25},{2,98},{3,27},{4,100},{5,29},{6,102},{7,31},{8,104},... | collective-permute-start | bytes 3932168 | tf_op jit(solution)/shard_map/ppermute | solution.py:65
  117.0 18.8 %collective-permute-start.25 = (bf16[128,5120]{1,0:T(8,128)(2,1)S(1)}, bf16[128,5120]{1,0:T(8,128)(2,1)S(1)}, u32[]{:S(2)}, u32[]{:S(2)}) collective-permute-start(bf16[128,5120]{1,0:T(8,128)(2,1)S(1)} %pad_maximum_fusion.4.b0_ref), channel_id=1, source_target_pairs={{0,32},{1,9},{2,34},{3,11},{4,36},{5,13},{6,38},{7,15},{8,40},{9,1... | collective-permute-start | bytes 3932168 | tf_op jit(solution)/shard_map/ppermute | solution.py:65
  125.3 20.9 %collective-permute-start.33 = (bf16[128,5120]{1,0:T(8,128)(2,1)S(1)}, bf16[128,5120]{1,0:T(8,128)(2,1)S(1)}, u32[]{:S(2)}, u32[]{:S(2)}) collective-permute-start(bf16[128,5120]{1,0:T(8,128)(2,1)S(1)} %pad_maximum_fusion.5.b0_ref), channel_id=1, source_target_pairs={{0,96},{1,25},{2,98},{3,27},{4,100},{5,29},{6,102},{7,31},{8,104},... | collective-permute-start | bytes 3932168 | tf_op jit(solution)/shard_map/ppermute | solution.py:65
  130.0 19.8 %collective-permute-start.32 = (bf16[128,5120]{1,0:T(8,128)(2,1)S(1)}, bf16[128,5120]{1,0:T(8,128)(2,1)S(1)}, u32[]{:S(2)}, u32[]{:S(2)}) collective-permute-start(bf16[128,5120]{1,0:T(8,128)(2,1)S(1)} %pad_maximum_fusion.5.b0_ref), channel_id=1, source_target_pairs={{0,32},{1,9},{2,34},{3,11},{4,36},{5,13},{6,38},{7,15},{8,40},{9,1... | collective-permute-start | bytes 3932168 | tf_op jit(solution)/shard_map/ppermute | solution.py:65
  135.9 17.3 %collective-permute-start.31 = (bf16[128,2560]{1,0:T(8,128)(2,1)S(1)}, bf16[128,2560]{1,0:T(8,128)(2,1)S(1)}, u32[]{:S(2)}, u32[]{:S(2)}) collective-permute-start(bf16[128,2560]{1,0:T(8,128)(2,1)S(1)} %slice.97), channel_id=1, source_target_pairs={{0,96},{1,25},{2,98},{3,27},{4,100},{5,29},{6,102},{7,31},{8,104},... | collective-permute-start | bytes 1966088 | tf_op jit(solution)/shard_map/ppermute | solution.py:65
  136.0 20.9 %collective-permute-start.30 = (bf16[128,2560]{1,0:T(8,128)(2,1)S(1)}, bf16[128,2560]{1,0:T(8,128)(2,1)S(1)}, u32[]{:S(2)}, u32[]{:S(2)}) collective-permute-start(bf16[128,2560]{1,0:T(8,128)(2,1)S(1)} %slice.96), channel_id=1, source_target_pairs={{0,32},{1,9},{2,34},{3,11},{4,36},{5,13},{6,38},{7,15},{8,40},{9,1... | collective-permute-start | bytes 1966088 | tf_op jit(solution)/shard_map/ppermute | solution.py:65
  150.0 10.9 %collective-permute-start.36 = (bf16[128,2560]{1,0:T(8,128)(2,1)S(1)}, bf16[128,2560]{1,0:T(8,128)(2,1)S(1)}, u32[]{:S(2)}, u32[]{:S(2)}) collective-permute-start(bf16[128,2560]{1,0:T(8,128)(2,1)S(1)} %slice.99), channel_id=1, source_target_pairs={{0,96},{1,25},{2,98},{3,27},{4,100},{5,29},{6,102},{7,31},{8,104},... | collective-permute-start | bytes 1966088 | tf_op jit(solution)/shard_map/ppermute | solution.py:65
  150.1 13.9 %collective-permute-start.35 = (bf16[128,2560]{1,0:T(8,128)(2,1)S(1)}, bf16[128,2560]{1,0:T(8,128)(2,1)S(1)}, u32[]{:S(2)}, u32[]{:S(2)}) collective-permute-start(bf16[128,2560]{1,0:T(8,128)(2,1)S(1)} %slice.98), channel_id=1, source_target_pairs={{0,32},{1,9},{2,34},{3,11},{4,36},{5,13},{6,38},{7,15},{8,40},{9,1... | collective-permute-start | bytes 1966088 | tf_op jit(solution)/shard_map/ppermute | solution.py:65
  160.8 9.7 %collective-permute-start.34 = (bf16[4,64,640]{2,1,0:T(8,128)(2,1)S(1)}, bf16[4,64,640]{2,1,0:T(8,128)(2,1)S(1)}, u32[]{:S(2)}, u32[]{:S(2)}) collective-permute-start(bf16[4,64,640]{2,1,0:T(8,128)(2,1)S(1)} %bitcast.17), channel_id=1, source_target_pairs={{0,1},{1,0},{2,3},{3,2},{4,5},{5,4},{6,7},{7,6},{8,9},{9,8},{10,11... | collective-permute-start | bytes 983048 | tf_op jit(solution)/shard_map/ppermute | solution.py:73
  170.7 10.3 %collective-permute-start.39 = (bf16[64,640]{1,0:T(8,128)(2,1)S(1)}, bf16[64,640]{1,0:T(8,128)(2,1)S(1)}, u32[]{:S(2)}, u32[]{:S(2)}) collective-permute-start(bf16[64,640]{1,0:T(8,128)(2,1)S(1)} %get-tuple-element.127), channel_id=1, source_target_pairs={{0,6},{1,7},{2,0},{3,1},{4,2},{5,3},{6,4},{7,5},{8,14},{9,15},{10,... | collective-permute-start | bytes 245768 | tf_op jit(solution)/shard_map/ppermute | solution.py:69
  171.1 9.8 %collective-permute-start.38 = (bf16[64,640]{1,0:T(8,128)(2,1)S(1)}, bf16[64,640]{1,0:T(8,128)(2,1)S(1)}, u32[]{:S(2)}, u32[]{:S(2)}) collective-permute-start(bf16[64,640]{1,0:T(8,128)(2,1)S(1)} %get-tuple-element.128), channel_id=1, source_target_pairs={{0,2},{1,3},{2,4},{3,5},{4,6},{5,7},{6,0},{7,1},{8,10},{9,11},{10,... | collective-permute-start | bytes 245768 | tf_op jit(solution)/shard_map/ppermute | solution.py:69
  (12 other events, 144.6 us)

commit v3 on v2

--- a/solution.py
+++ b/solution.py
@@ -24,8 +24,8 @@
     ("g", "gather_core"),
     ("h", "send_far"),
     ("g", "partials"),
+    ("g", "send_far"),
     ("h", "send_near"),
-    ("g", "send_far"),
     ("g", "send_near"),
     ("h", "send_second"),
     ("g", "send_second"),
@@ -141,6 +141,22 @@
     )(order, tokens, weight)
 
 
+def stage_kernel(source_ref, target_ref):
+    target_ref[...] = source_ref[...]
+
+
+def stage(rows):
+    return pl.pallas_call(
+        stage_kernel,
+        out_shape=jax.ShapeDtypeStruct(rows.shape, rows.dtype),
+        compiler_params=pltpu.CompilerParams(vmem_limit_bytes=LIMIT),
+        cost_estimate=pl.CostEstimate(
+            flops=4 * TOK * WID * FFL, bytes_accessed=4 * WID * FFL, transcendentals=0
+        ),
+        name="stage",
+    )(rows)
+
+
 def near_input_grads_kernel(wi_ref, b0_ref, b1_ref, b3_ref, out_ref):
     @pl.when(pl.program_id(0) == 0)
     def _():
@@ -236,9 +252,10 @@
         return ()
 
     def gather_core(self, env):
-        far, left, right = env.after(self.came)
-        self.own = jnp.concatenate([self.own, right, far, left], axis=0)
-        self.came = swap_core(self.own)
+        own, far, left, right = env.after((self.own, *self.came))
+        own = jnp.concatenate([own, right, far, left], axis=0)
+        self.came = swap_core(own)
+        self.own = stage(own) if self.hidden else own
         return (self.own,)
 
     def partials(self, env):
@@ -263,7 +280,7 @@
         q = add(self.p0, from_left, from_right).astype(BF16)
         blocks = [q[32 * i : 32 * (i + 1)] for i in range(4)]
         self.own = blocks[0]
-        self.came = tuple(hop(blocks[i], step, False) for i, step in ((2, 2), (1, 1), (3, -1)))
+        self.came = tuple(hop(blocks[i], step, False) for i, step in ((3, -1), (1, 1), (2, 2)))
         return (q,)
 
     def sum_second(self, env):
@@ -271,10 +288,10 @@
         return (self.own,)
 
     def send_own(self):
-        self.came = tuple(hop(self.own, step, False) for step in (2, 1, -1))
+        self.came = tuple(hop(self.own, step, False) for step in (-1, 1, 2))
 
     def gather_near(self, env):
-        far, left, right = env.after(self.came)
+        right, left, far = env.after(self.came)
         self.quarter = jnp.concatenate([self.own, right, far, left], axis=0)
         self.came = hop(self.quarter, 1, True), hop(self.quarter, -1, True)
         return (self.quarter,)

time: 182 us -> 176 us (0.967); the launches traced: 182 us -> 173 us
  waiting for transfers between devices: 82.9 us -> 69.4 us
  starting transfers between devices: 54.5 us -> 61.5 us
  local copies, waits for them, and re-layouts: 5.64 us -> 2.89 us
    ppermute x28, waiting for transfers between devices: 79.3 us -> 67.8 us  [hop(): return lax.ppermute(value, AXES, neighbours(move))]
    ppermute x28, starting transfers between devices: 39.8 us -> 46.8 us  [hop(): return lax.ppermute(value, AXES, neighbours(move))]
    ppermute x9, waiting for transfers between devices: 3.57 us -> 0.02 us  [hop_z(): lax.ppermute(value, AXES, neighbours(lambda x, y, z, c: (x, y, z + step,...]
    unnamed x16 -> x18, local copies, waits for them, and re-layouts: 4.91 us -> 2.2 us
  transfers between devices with their start and end apart: 40 -> 40, of which waited for: 21 -> 22; matrix products, arithmetic and copies ran while one was open for 3% -> 3% of each run, Pallas kernels for 18% -> 19%
where the time goes in v3:
time: 176 us; the launch traced here: 173 us
  waiting for transfers between devices  69.4 us (39%)
  starting transfers between devices  61.5 us (35%)
  Pallas kernels  33.6 us (19%)
  other arithmetic  4.15 us (2%)
  local copies, waits for them, and re-layouts  2.89 us (2%)
    ppermute x28, waiting for transfers between devices, hop(): return lax.ppermute(value, AXES, neighbours(move))  67.8 us
    ppermute x28, starting transfers between devices, hop(): return lax.ppermute(value, AXES, neighbours(move))  46.8 us
    ppermute x9, starting transfers between devices, hop_z(): lax.ppermute(value, AXES, neighbours(lambda x, y, z, c: (x, y, z + step,...  14.4 us
    pallas_call x2, Pallas kernels, partials(): pl.pallas_call(functools.partial(partial_kernel, hidden), grid=(TILES,),...  12.7 us
    pallas_call x2, Pallas kernels, weight_grads(): pl.pallas_call(w_out_kernel if outer else w_in_kernel, grid=(TILES,), out...  12.4 us
    pallas_call x2, Pallas kernels, input_grads(): pl.pallas_call(far_input_grads_kernel if last else near_input_grads_kerne...  8.45 us
  transfers between devices with their start and end apart: 40, of which 22 were waited for; matrix products, arithmetic and copies ran while one was open for 3% of the time, Pallas kernels for 19%

profile of v3, /device:TPU:0, one launch (start us, length us, event | category | flops | bytes accessed | tf_op | source)
XLA Modules:
  0.0 172.6 jit_solution(398037737492526712)
XLA Ops:
  0.6 4.0 %collective-permute-start.4 = (bf16[64,640]{1,0:T(8,128)(2,1)}, bf16[64,640]{1,0:T(8,128)(2,1)S(1)}, u32[]{:S(2)}, u32[]{:S(2)}) collective-permute-start(bf16[64,640]{1,0:T(8,128)(2,1)} %param.4), channel_id=1, source_target_pairs={{0,4},{1,5},{2,6},{3,7},{4,0},{5,1},{6,2},{7,3},{8,12},{9,13},{10,... | collective-permute-start | bytes 245768 | tf_op jit(solution)/shard_map/ppermute | solution.py:69
  7.7 2.4 %collective-permute-start = (bf16[64,640]{1,0:T(8,128)(2,1)}, bf16[64,640]{1,0:T(8,128)(2,1)S(1)}, u32[]{:S(2)}, u32[]{:S(2)}) collective-permute-start(bf16[64,640]{1,0:T(8,128)(2,1)} %param.5), channel_id=1, source_target_pairs={{0,4},{1,5},{2,6},{3,7},{4,0},{5,1},{6,2},{7,3},{8,12},{9,13},{10,... | collective-permute-start | bytes 245768 | tf_op jit(solution)/shard_map/ppermute | solution.py:69
  15.5 6.4 %hidden_partials.1 = (bf16[512,640]{1,0:T(8,128)(2,1)S(1)}, bf16[128,2560]{1,0:T(8,128)(2,1)S(1)}, bf16[128,2560]{1,0:T(8,128)(2,1)S(1)}, bf16[128,5120]{1,0:T(8...) custom-call(s32[16]{0:T(128)S(1)} %fusion.12.order_ref, ...), custom_call_target="tpu_custom_call" | custom-call | flops 3355443200 | bytes 11796480 | tf_op jit(solution)/shard_map/hidden_partials/pallas_call | solution.py:124
  25.6 6.3 %grad_partials.1 = (bf16[512,640]{1,0:T(8,128)(2,1)S(1)}, bf16[128,2560]{1,0:T(8,128)(2,1)S(1)}, bf16[128,2560]{1,0:T(8,128)(2,1)S(1)}, bf16[128,5120]{1,0:T(8,1...) custom-call(s32[16]{0:T(128)S(1)} %fusion.12.order_ref, ...), custom_call_target="tpu_custom_call" | custom-call | flops 3355443200 | bytes 11796480 | tf_op jit(solution)/shard_map/grad_partials/pallas_call | solution.py:124
  32.3 3.0 %collective-permute-start.9 = (bf16[128,2560]{1,0:T(8,128)(2,1)S(1)}, bf16[128,2560]{1,0:T(8,128)(2,1)S(1)}, u32[]{:S(2)}, u32[]{:S(2)}) collective-permute-start(bf16[128,2560]{1,0:T(8,128)(2,1)S(1)} %get-tuple-element.78), channel_id=1, source_target_pairs={{0,96},{1,25},{2,98},{3,27},{4,100},{5,29},{6,102},{7,31},{8,104},... | collective-permute-start | bytes 1966088 | tf_op jit(solution)/shard_map/ppermute | solution.py:65
  35.7 2.0 %collective-permute-start.15 = (bf16[128,5120]{1,0:T(8,128)(2,1)S(1)}, bf16[128,5120]{1,0:T(8,128)(2,1)S(1)}, u32[]{:S(2)}, u32[]{:S(2)}) collective-permute-start(bf16[128,5120]{1,0:T(8,128)(2,1)S(1)} %pad_maximum_fusion.1), channel_id=1, source_target_pairs={{0,96},{1,25},{2,98},{3,27},{4,100},{5,29},{6,102},{7,31},{8,104},... | collective-permute-start | bytes 3932168 | tf_op jit(solution)/shard_map/ppermute | solution.py:65
  38.0 5.8 %collective-permute-done.8 = bf16[128,2560]{1,0:T(8,128)(2,1)S(1)} collective-permute-done((bf16[128,2560]{1,0:T(8,128)(2,1)S(1)}, bf16[128,2560]{1,0:T(8,128)(2,1)S(1)}, u32[]{:S(2)}, u32[]{:S(2)}) %collective-permute-start.8) | collective-permute-done | bytes 655392 | tf_op jit(solution)/shard_map/ppermute | solution.py:65
  44.1 3.3 %collective-permute-start.13 = (bf16[128,5120]{1,0:T(8,128)(2,1)S(1)}, bf16[128,5120]{1,0:T(8,128)(2,1)S(1)}, u32[]{:S(2)}, u32[]{:S(2)}) collective-permute-start(bf16[128,5120]{1,0:T(8,128)(2,1)S(1)} %pad_maximum_fusion.3), channel_id=1, source_target_pairs={{0,96},{1,25},{2,98},{3,27},{4,100},{5,29},{6,102},{7,31},{8,104},... | collective-permute-start | bytes 3932168 | tf_op jit(solution)/shard_map/ppermute | solution.py:65
  47.8 9.6 %collective-permute-done.15 = bf16[128,5120]{1,0:T(8,128)(2,1)S(1)} collective-permute-done((bf16[128,5120]{1,0:T(8,128)(2,1)S(1)}, bf16[128,5120]{1,0:T(8,128)(2,1)S(1)}, u32[]{:S(2)}, u32[]{:S(2)}) %collective-permute-start.15) | collective-permute-done | bytes 1310752 | tf_op jit(solution)/shard_map/ppermute | solution.py:65
  58.6 3.3 %collective-permute-start.21 = (bf16[32,5120]{1,0:T(8,128)(2,1)S(1)}, bf16[32,5120]{1,0:T(8,128)(2,1)S(1)}, u32[]{:S(2)}, u32[]{:S(2)}) collective-permute-start(bf16[32,5120]{1,0:T(8,128)(2,1)S(1)} %get-tuple-element.124), channel_id=1, source_target_pairs={{0,16},{1,65},{2,18},{3,67},{4,20},{5,69},{6,22},{7,71},{8,24},{9,... | collective-permute-start | bytes 983048 | tf_op jit(solution)/shard_map/ppermute | solution.py:65
  62.5 2.6 %collective-permute-start.19 = (bf16[32,5120]{1,0:T(8,128)(2,1)S(1)}, bf16[32,5120]{1,0:T(8,128)(2,1)S(1)}, u32[]{:S(2)}, u32[]{:S(2)}) collective-permute-start(bf16[32,5120]{1,0:T(8,128)(2,1)S(1)} %get-tuple-element.126), channel_id=1, source_target_pairs={{0,24},{1,97},{2,26},{3,99},{4,28},{5,101},{6,30},{7,103},{8,0},{9... | collective-permute-start | bytes 983048 | tf_op jit(solution)/shard_map/ppermute | solution.py:65
  65.1 13.4 %collective-permute-done.13 = bf16[128,5120]{1,0:T(8,128)(2,1)S(1)} collective-permute-done((bf16[128,5120]{1,0:T(8,128)(2,1)S(1)}, bf16[128,5120]{1,0:T(8,128)(2,1)S(1)}, u32[]{:S(2)}, u32[]{:S(2)}) %collective-permute-start.13) | collective-permute-done | bytes 1310752 | tf_op jit(solution)/shard_map/ppermute | solution.py:65
  79.6 3.3 %collective-permute-start.18 = (bf16[32,5120]{1,0:T(8,128)(2,1)S(1)}, bf16[32,5120]{1,0:T(8,128)(2,1)S(1)}, u32[]{:S(2)}, u32[]{:S(2)}) collective-permute-start(bf16[32,5120]{1,0:T(8,128)(2,1)S(1)} %get-tuple-element.121), channel_id=1, source_target_pairs={{0,16},{1,65},{2,18},{3,67},{4,20},{5,69},{6,22},{7,71},{8,24},{9,... | collective-permute-start | bytes 983048 | tf_op jit(solution)/shard_map/ppermute | solution.py:65
  83.6 2.6 %collective-permute-start.16 = (bf16[32,5120]{1,0:T(8,128)(2,1)S(1)}, bf16[32,5120]{1,0:T(8,128)(2,1)S(1)}, u32[]{:S(2)}, u32[]{:S(2)}) collective-permute-start(bf16[32,5120]{1,0:T(8,128)(2,1)S(1)} %get-tuple-element.123), channel_id=1, source_target_pairs={{0,24},{1,97},{2,26},{3,99},{4,28},{5,101},{6,30},{7,103},{8,0},{9... | collective-permute-start | bytes 983048 | tf_op jit(solution)/shard_map/ppermute | solution.py:65
  88.3 3.4 %collective-permute-done.17 = bf16[32,5120]{1,0:T(8,128)(2,1)S(1)} collective-permute-done((bf16[32,5120]{1,0:T(8,128)(2,1)S(1)}, bf16[32,5120]{1,0:T(8,128)(2,1)S(1)}, u32[]{:S(2)}, u32[]{:S(2)}) %collective-permute-start.17) | collective-permute-done | bytes 327712 | tf_op jit(solution)/shard_map/ppermute | solution.py:65
  92.6 2.2 %collective-permute-start.24 = (bf16[32,5120]{1,0:T(8,128)(2,1)S(1)}, bf16[32,5120]{1,0:T(8,128)(2,1)S(1)}, u32[]{:S(2)}, u32[]{:S(2)}) collective-permute-start(bf16[32,5120]{1,0:T(8,128)(2,1)S(1)} %fusion.5), channel_id=1, source_target_pairs={{0,16},{1,65},{2,18},{3,67},{4,20},{5,69},{6,22},{7,71},{8,24},{9,... | collective-permute-start | bytes 983048 | tf_op jit(solution)/shard_map/ppermute | solution.py:65
  101.3 2.7 %collective-permute-start.27 = (bf16[32,5120]{1,0:T(8,128)(2,1)S(1)}, bf16[32,5120]{1,0:T(8,128)(2,1)S(1)}, u32[]{:S(2)}, u32[]{:S(2)}) collective-permute-start(bf16[32,5120]{1,0:T(8,128)(2,1)S(1)} %get-tuple-element.119), channel_id=1, source_target_pairs={{0,24},{1,97},{2,26},{3,99},{4,28},{5,101},{6,30},{7,103},{8,0},{9... | collective-permute-start | bytes 983048 | tf_op jit(solution)/shard_map/ppermute | solution.py:65
  104.9 3.9 %collective-permute-start.26 = (bf16[128,5120]{1,0:T(8,128)(2,1)S(1)}, bf16[128,5120]{1,0:T(8,128)(2,1)S(1)}, u32[]{:S(2)}, u32[]{:S(2)}) collective-permute-start(bf16[128,5120]{1,0:T(8,128)(2,1)S(1)} %pad_maximum_fusion.4.b0_ref), channel_id=1, source_target_pairs={{0,96},{1,25},{2,98},{3,27},{4,100},{5,29},{6,102},{7,31},{8,104},... | collective-permute-start | bytes 3932168 | tf_op jit(solution)/shard_map/ppermute | solution.py:65
  109.5 5.2 %collective-permute-done.28 = bf16[32,5120]{1,0:T(8,128)(2,1)S(1)} collective-permute-done((bf16[32,5120]{1,0:T(8,128)(2,1)S(1)}, bf16[32,5120]{1,0:T(8,128)(2,1)S(1)}, u32[]{:S(2)}, u32[]{:S(2)}) %collective-permute-start.28) | collective-permute-done | bytes 327712 | tf_op jit(solution)/shard_map/ppermute | solution.py:65
  114.7 4.1 %collective-permute-done.27 = bf16[32,5120]{1,0:T(8,128)(2,1)S(1)} collective-permute-done((bf16[32,5120]{1,0:T(8,128)(2,1)S(1)}, bf16[32,5120]{1,0:T(8,128)(2,1)S(1)}, u32[]{:S(2)}, u32[]{:S(2)}) %collective-permute-start.27) | collective-permute-done | bytes 327712 | tf_op jit(solution)/shard_map/ppermute | solution.py:65
  118.9 3.9 %collective-permute-start.33 = (bf16[128,5120]{1,0:T(8,128)(2,1)S(1)}, bf16[128,5120]{1,0:T(8,128)(2,1)S(1)}, u32[]{:S(2)}, u32[]{:S(2)}) collective-permute-start(bf16[128,5120]{1,0:T(8,128)(2,1)S(1)} %pad_maximum_fusion.5.b0_ref), channel_id=1, source_target_pairs={{0,96},{1,25},{2,98},{3,27},{4,100},{5,29},{6,102},{7,31},{8,104},... | collective-permute-start | bytes 3932168 | tf_op jit(solution)/shard_map/ppermute | solution.py:65
  123.9 3.7 %collective-permute-done.25.b3_ref = bf16[128,5120]{1,0:T(8,128)(2,1)S(1)} collective-permute-done((bf16[128,5120]{1,0:T(8,128)(2,1)S(1)}, bf16[128,5120]{1,0:T(8,128)(2,1)S(1)}, u32[]{:S(2)}, u32[]{:S(2)}) %collective-permute-start.25) | collective-permute-done | bytes 1310752 | tf_op jit(solution)/shard_map/ppermute | solution.py:65
  127.8 2.0 %collective-permute-start.30 = (bf16[128,2560]{1,0:T(8,128)(2,1)S(1)}, bf16[128,2560]{1,0:T(8,128)(2,1)S(1)}, u32[]{:S(2)}, u32[]{:S(2)}) collective-permute-start(bf16[128,2560]{1,0:T(8,128)(2,1)S(1)} %slice.96), channel_id=1, source_target_pairs={{0,32},{1,9},{2,34},{3,11},{4,36},{5,13},{6,38},{7,15},{8,40},{9,1... | collective-permute-start | bytes 1966088 | tf_op jit(solution)/shard_map/ppermute | solution.py:65
  129.8 4.7 %near_input_grads.1.near_ref = f32[384,640]{1,0:T(8,128)S(1)} custom-call(bf16[640,5120]{1,0:T(8,128)(2,1)S(1)} %bitcast.15, bf16[128,5120]{1,0:T(8,128)(2,1)S(1)} %pad_maximum_fusion.4.b0_ref, bf16[128,5120]{1,0:T(8,128)(2,1)S(1)} %collective-permute-done.26.b1_ref, bf16[128,5120]{1,0:T(8,128)(2,1)S(1)} %collective-permute-done.25.b3_ref), custom_call_target="tpu_custom_call" | custom-call | flops 2516582400 | bytes 11796480 | tf_op jit(solution)/shard_map/near_input_grads/pallas_call | solution.py:194
  134.5 3.4 %collective-permute-done.33.b1_ref = bf16[128,5120]{1,0:T(8,128)(2,1)S(1)} collective-permute-done((bf16[128,5120]{1,0:T(8,128)(2,1)S(1)}, bf16[128,5120]{1,0:T(8,128)(2,1)S(1)}, u32[]{:S(2)}, u32[]{:S(2)}) %collective-permute-start.33) | collective-permute-done | bytes 1310752 | tf_op jit(solution)/shard_map/ppermute | solution.py:65
  138.0 3.7 %collective-permute-done.32.b3_ref = bf16[128,5120]{1,0:T(8,128)(2,1)S(1)} collective-permute-done((bf16[128,5120]{1,0:T(8,128)(2,1)S(1)}, bf16[128,5120]{1,0:T(8,128)(2,1)S(1)}, u32[]{:S(2)}, u32[]{:S(2)}) %collective-permute-start.32) | collective-permute-done | bytes 1310752 | tf_op jit(solution)/shard_map/ppermute | solution.py:65
  141.8 2.0 %collective-permute-start.35 = (bf16[128,2560]{1,0:T(8,128)(2,1)S(1)}, bf16[128,2560]{1,0:T(8,128)(2,1)S(1)}, u32[]{:S(2)}, u32[]{:S(2)}) collective-permute-start(bf16[128,2560]{1,0:T(8,128)(2,1)S(1)} %slice.98), channel_id=1, source_target_pairs={{0,32},{1,9},{2,34},{3,11},{4,36},{5,13},{6,38},{7,15},{8,40},{9,1... | collective-permute-start | bytes 1966088 | tf_op jit(solution)/shard_map/ppermute | solution.py:65
  145.0 3.7 %collective-permute-done.30 = bf16[128,2560]{1,0:T(8,128)(2,1)S(1)} collective-permute-done((bf16[128,2560]{1,0:T(8,128)(2,1)S(1)}, bf16[128,2560]{1,0:T(8,128)(2,1)S(1)}, u32[]{:S(2)}, u32[]{:S(2)}) %collective-permute-start.30) | collective-permute-done | bytes 655392 | tf_op jit(solution)/shard_map/ppermute | solution.py:65
  148.8 3.7 %far_input_grads.1 = bf16[512,640]{1,0:T(8,128)(2,1)S(1)} custom-call(s32[16]{0:T(128)S(1)} %fusion.12.order_ref, bf16[640,5120]{1,0:T(8,128)(2,1)S(1)} %bitcast.15, bf16[128,5120]{1,0:T(8,128)(2,1)S(1)} %constant_dynamic-update-slice_fusion.13.b2_ref, f32[384,640]{1,0:T(8,128)S(1)} %near_input_grads.1.near_ref), custom_call_target="tpu_custom_call" | custom-call | flops 838860800 | bytes 11796480 | tf_op jit(solution)/shard_map/far_input_grads/pallas_call | solution.py:194
  152.7 3.0 %collective-permute-done.35 = bf16[128,2560]{1,0:T(8,128)(2,1)S(1)} collective-permute-done((bf16[128,2560]{1,0:T(8,128)(2,1)S(1)}, bf16[128,2560]{1,0:T(8,128)(2,1)S(1)}, u32[]{:S(2)}, u32[]{:S(2)}) %collective-permute-start.35) | collective-permute-done | bytes 655392 | tf_op jit(solution)/shard_map/ppermute | solution.py:65
  155.8 6.5 %grad_w_out.1 = bf16[5120,640]{1,0:T(8,128)(2,1)} custom-call(bf16[512,640]{1,0:T(8,128)(2,1)S(1)} %get-tuple-element.110.c_ref, bf16[128,5120]{1,0:T(8,128)(2,1)S(1)} %pad_maximum_fusion.5.b0_ref, bf16[128,5120]{1,0:T(8,128)(2,1)S(1)} %collective-permute-done.33.b1_ref, bf16[128,5120]{1,0:T(8,128)(2,1)S(1)} %pad_maximum_fusion.6.b2_ref, ...), custom_call_target="tpu_custom_call" | custom-call | flops 655360 | bytes 2304 | tf_op jit(solution)/shard_map/grad_w_out/pallas_call | solution.py:227
  166.0 5.9 %grad_w_in.1 = bf16[640,5120]{1,0:T(8,128)(2,1)} custom-call(bf16[512,640]{1,0:T(8,128)(2,1)S(1)} %get-tuple-element.115.x_ref, bf16[128,5120]{1,0:T(8,128)(2,1)S(1)} %pad_maximum_fusion.4.b0_ref, bf16[128,5120]{1,0:T(8,128)(2,1)S(1)} %collective-permute-done.26.b1_ref, bf16[128,5120]{1,0:T(8,128)(2,1)S(1)} %constant_dynamic-update-slice_fusion.13.b2_ref, ...), custom_call_target="tpu_custom_call" | custom-call | flops 655360 | bytes 2304 | tf_op jit(solution)/shard_map/grad_w_in/pallas_call | solution.py:227
  (109 shorter events, 35.8 us)
Async XLA Ops:
  0.6 11.9 %collective-permute-start.4 = (bf16[64,640]{1,0:T(8,128)(2,1)}, bf16[64,640]{1,0:T(8,128)(2,1)S(1)}, u32[]{:S(2)}, u32[]{:S(2)}) collective-permute-start(bf16[64,640]{1,0:T(8,128)(2,1)} %param.4), channel_id=1, source_target_pairs={{0,4},{1,5},{2,6},{3,7},{4,0},{5,1},{6,2},{7,3},{8,12},{9,13},{10,... | collective-permute-start | bytes 245768 | tf_op jit(solution)/shard_map/ppermute | solution.py:69
  6.7 15.2 %collective-permute-start.1 = (bf16[64,640]{1,0:T(8,128)(2,1)}, bf16[64,640]{1,0:T(8,128)(2,1)S(1)}, u32[]{:S(2)}, u32[]{:S(2)}) collective-permute-start(bf16[64,640]{1,0:T(8,128)(2,1)} %param.5), channel_id=1, source_target_pairs={{0,2},{1,3},{2,4},{3,5},{4,6},{5,7},{6,0},{7,1},{8,10},{9,11},{10,... | collective-permute-start | bytes 245768 | tf_op jit(solution)/shard_map/ppermute | solution.py:69
  7.7 14.2 %collective-permute-start = (bf16[64,640]{1,0:T(8,128)(2,1)}, bf16[64,640]{1,0:T(8,128)(2,1)S(1)}, u32[]{:S(2)}, u32[]{:S(2)}) collective-permute-start(bf16[64,640]{1,0:T(8,128)(2,1)} %param.5), channel_id=1, source_target_pairs={{0,4},{1,5},{2,6},{3,7},{4,0},{5,1},{6,2},{7,3},{8,12},{9,13},{10,... | collective-permute-start | bytes 245768 | tf_op jit(solution)/shard_map/ppermute | solution.py:69
  11.0 10.9 %collective-permute-start.2 = (bf16[64,640]{1,0:T(8,128)(2,1)}, bf16[64,640]{1,0:T(8,128)(2,1)S(1)}, u32[]{:S(2)}, u32[]{:S(2)}) collective-permute-start(bf16[64,640]{1,0:T(8,128)(2,1)} %param.5), channel_id=1, source_target_pairs={{0,6},{1,7},{2,0},{3,1},{4,2},{5,3},{6,4},{7,5},{8,14},{9,15},{10,... | collective-permute-start | bytes 245768 | tf_op jit(solution)/shard_map/ppermute | solution.py:69
  22.1 13.2 %collective-permute-start.10 = (bf16[128,2560]{1,0:T(8,128)(2,1)S(1)}, bf16[128,2560]{1,0:T(8,128)(2,1)S(1)}, u32[]{:S(2)}, u32[]{:S(2)}) collective-permute-start(bf16[128,2560]{1,0:T(8,128)(2,1)S(1)} %get-tuple-element.79), channel_id=1, source_target_pairs={{0,32},{1,9},{2,34},{3,11},{4,36},{5,13},{6,38},{7,15},{8,40},{9,1... | collective-permute-start | bytes 1966088 | tf_op jit(solution)/shard_map/ppermute | solution.py:65
  23.7 11.6 %collective-permute-start.11 = (bf16[128,2560]{1,0:T(8,128)(2,1)S(1)}, bf16[128,2560]{1,0:T(8,128)(2,1)S(1)}, u32[]{:S(2)}, u32[]{:S(2)}) collective-permute-start(bf16[128,2560]{1,0:T(8,128)(2,1)S(1)} %get-tuple-element.80), channel_id=1, source_target_pairs={{0,96},{1,25},{2,98},{3,27},{4,100},{5,29},{6,102},{7,31},{8,104},... | collective-permute-start | bytes 1966088 | tf_op jit(solution)/shard_map/ppermute | solution.py:65
  32.0 11.9 %collective-permute-start.8 = (bf16[128,2560]{1,0:T(8,128)(2,1)S(1)}, bf16[128,2560]{1,0:T(8,128)(2,1)S(1)}, u32[]{:S(2)}, u32[]{:S(2)}) collective-permute-start(bf16[128,2560]{1,0:T(8,128)(2,1)S(1)} %get-tuple-element.77), channel_id=1, source_target_pairs={{0,32},{1,9},{2,34},{3,11},{4,36},{5,13},{6,38},{7,15},{8,40},{9,1... | collective-permute-start | bytes 1966088 | tf_op jit(solution)/shard_map/ppermute | solution.py:65
  32.3 11.5 %collective-permute-start.9 = (bf16[128,2560]{1,0:T(8,128)(2,1)S(1)}, bf16[128,2560]{1,0:T(8,128)(2,1)S(1)}, u32[]{:S(2)}, u32[]{:S(2)}) collective-permute-start(bf16[128,2560]{1,0:T(8,128)(2,1)S(1)} %get-tuple-element.78), channel_id=1, source_target_pairs={{0,96},{1,25},{2,98},{3,27},{4,100},{5,29},{6,102},{7,31},{8,104},... | collective-permute-start | bytes 1966088 | tf_op jit(solution)/shard_map/ppermute | solution.py:65
  35.7 21.7 %collective-permute-start.15 = (bf16[128,5120]{1,0:T(8,128)(2,1)S(1)}, bf16[128,5120]{1,0:T(8,128)(2,1)S(1)}, u32[]{:S(2)}, u32[]{:S(2)}) collective-permute-start(bf16[128,5120]{1,0:T(8,128)(2,1)S(1)} %pad_maximum_fusion.1), channel_id=1, source_target_pairs={{0,96},{1,25},{2,98},{3,27},{4,100},{5,29},{6,102},{7,31},{8,104},... | collective-permute-start | bytes 3932168 | tf_op jit(solution)/shard_map/ppermute | solution.py:65
  37.9 20.0 %collective-permute-start.14 = (bf16[128,5120]{1,0:T(8,128)(2,1)S(1)}, bf16[128,5120]{1,0:T(8,128)(2,1)S(1)}, u32[]{:S(2)}, u32[]{:S(2)}) collective-permute-start(bf16[128,5120]{1,0:T(8,128)(2,1)S(1)} %pad_maximum_fusion), channel_id=1, source_target_pairs={{0,32},{1,9},{2,34},{3,11},{4,36},{5,13},{6,38},{7,15},{8,40},{9,1... | collective-permute-start | bytes 3932168 | tf_op jit(solution)/shard_map/ppermute | solution.py:65
  44.1 34.4 %collective-permute-start.13 = (bf16[128,5120]{1,0:T(8,128)(2,1)S(1)}, bf16[128,5120]{1,0:T(8,128)(2,1)S(1)}, u32[]{:S(2)}, u32[]{:S(2)}) collective-permute-start(bf16[128,5120]{1,0:T(8,128)(2,1)S(1)} %pad_maximum_fusion.3), channel_id=1, source_target_pairs={{0,96},{1,25},{2,98},{3,27},{4,100},{5,29},{6,102},{7,31},{8,104},... | collective-permute-start | bytes 3932168 | tf_op jit(solution)/shard_map/ppermute | solution.py:65
  47.7 31.2 %collective-permute-start.12 = (bf16[128,5120]{1,0:T(8,128)(2,1)S(1)}, bf16[128,5120]{1,0:T(8,128)(2,1)S(1)}, u32[]{:S(2)}, u32[]{:S(2)}) collective-permute-start(bf16[128,5120]{1,0:T(8,128)(2,1)S(1)} %pad_maximum_fusion.2), channel_id=1, source_target_pairs={{0,32},{1,9},{2,34},{3,11},{4,36},{5,13},{6,38},{7,15},{8,40},{9,1... | collective-permute-start | bytes 3932168 | tf_op jit(solution)/shard_map/ppermute | solution.py:65
  58.6 25.0 %collective-permute-start.21 = (bf16[32,5120]{1,0:T(8,128)(2,1)S(1)}, bf16[32,5120]{1,0:T(8,128)(2,1)S(1)}, u32[]{:S(2)}, u32[]{:S(2)}) collective-permute-start(bf16[32,5120]{1,0:T(8,128)(2,1)S(1)} %get-tuple-element.124), channel_id=1, source_target_pairs={{0,16},{1,65},{2,18},{3,67},{4,20},{5,69},{6,22},{7,71},{8,24},{9,... | collective-permute-start | bytes 983048 | tf_op jit(solution)/shard_map/ppermute | solution.py:65
  61.8 24.3 %collective-permute-start.20 = (bf16[32,5120]{1,0:T(8,128)(2,1)S(1)}, bf16[32,5120]{1,0:T(8,128)(2,1)S(1)}, u32[]{:S(2)}, u32[]{:S(2)}) collective-permute-start(bf16[32,5120]{1,0:T(8,128)(2,1)S(1)} %get-tuple-element.125), channel_id=1, source_target_pairs={{0,8},{1,33},{2,10},{3,35},{4,12},{5,37},{6,14},{7,39},{8,16},{9,4... | collective-permute-start | bytes 983048 | tf_op jit(solution)/shard_map/ppermute | solution.py:65
  62.5 23.6 %collective-permute-start.19 = (bf16[32,5120]{1,0:T(8,128)(2,1)S(1)}, bf16[32,5120]{1,0:T(8,128)(2,1)S(1)}, u32[]{:S(2)}, u32[]{:S(2)}) collective-permute-start(bf16[32,5120]{1,0:T(8,128)(2,1)S(1)} %get-tuple-element.126), channel_id=1, source_target_pairs={{0,24},{1,97},{2,26},{3,99},{4,28},{5,101},{6,30},{7,103},{8,0},{9... | collective-permute-start | bytes 983048 | tf_op jit(solution)/shard_map/ppermute | solution.py:65
  82.9 8.9 %collective-permute-start.17 = (bf16[32,5120]{1,0:T(8,128)(2,1)S(1)}, bf16[32,5120]{1,0:T(8,128)(2,1)S(1)}, u32[]{:S(2)}, u32[]{:S(2)}) collective-permute-start(bf16[32,5120]{1,0:T(8,128)(2,1)S(1)} %get-tuple-element.122), channel_id=1, source_target_pairs={{0,8},{1,33},{2,10},{3,35},{4,12},{5,37},{6,14},{7,39},{8,16},{9,4... | collective-permute-start | bytes 983048 | tf_op jit(solution)/shard_map/ppermute | solution.py:65
  92.6 8.8 %collective-permute-start.24 = (bf16[32,5120]{1,0:T(8,128)(2,1)S(1)}, bf16[32,5120]{1,0:T(8,128)(2,1)S(1)}, u32[]{:S(2)}, u32[]{:S(2)}) collective-permute-start(bf16[32,5120]{1,0:T(8,128)(2,1)S(1)} %fusion.5), channel_id=1, source_target_pairs={{0,16},{1,65},{2,18},{3,67},{4,20},{5,69},{6,22},{7,71},{8,24},{9,... | collective-permute-start | bytes 983048 | tf_op jit(solution)/shard_map/ppermute | solution.py:65
  94.7 10.0 %collective-permute-start.23 = (bf16[32,5120]{1,0:T(8,128)(2,1)S(1)}, bf16[32,5120]{1,0:T(8,128)(2,1)S(1)}, u32[]{:S(2)}, u32[]{:S(2)}) collective-permute-start(bf16[32,5120]{1,0:T(8,128)(2,1)S(1)} %fusion.5), channel_id=1, source_target_pairs={{0,8},{1,33},{2,10},{3,35},{4,12},{5,37},{6,14},{7,39},{8,16},{9,4... | collective-permute-start | bytes 983048 | tf_op jit(solution)/shard_map/ppermute | solution.py:65
  97.9 11.5 %collective-permute-start.29 = (bf16[32,5120]{1,0:T(8,128)(2,1)S(1)}, bf16[32,5120]{1,0:T(8,128)(2,1)S(1)}, u32[]{:S(2)}, u32[]{:S(2)}) collective-permute-start(bf16[32,5120]{1,0:T(8,128)(2,1)S(1)} %get-tuple-element.119), channel_id=1, source_target_pairs={{0,16},{1,65},{2,18},{3,67},{4,20},{5,69},{6,22},{7,71},{8,24},{9,... | collective-permute-start | bytes 983048 | tf_op jit(solution)/shard_map/ppermute | solution.py:65
  98.2 16.5 %collective-permute-start.28 = (bf16[32,5120]{1,0:T(8,128)(2,1)S(1)}, bf16[32,5120]{1,0:T(8,128)(2,1)S(1)}, u32[]{:S(2)}, u32[]{:S(2)}) collective-permute-start(bf16[32,5120]{1,0:T(8,128)(2,1)S(1)} %get-tuple-element.119), channel_id=1, source_target_pairs={{0,8},{1,33},{2,10},{3,35},{4,12},{5,37},{6,14},{7,39},{8,16},{9,4... | collective-permute-start | bytes 983048 | tf_op jit(solution)/shard_map/ppermute | solution.py:65
  101.3 17.5 %collective-permute-start.27 = (bf16[32,5120]{1,0:T(8,128)(2,1)S(1)}, bf16[32,5120]{1,0:T(8,128)(2,1)S(1)}, u32[]{:S(2)}, u32[]{:S(2)}) collective-permute-start(bf16[32,5120]{1,0:T(8,128)(2,1)S(1)} %get-tuple-element.119), channel_id=1, source_target_pairs={{0,24},{1,97},{2,26},{3,99},{4,28},{5,101},{6,30},{7,103},{8,0},{9... | collective-permute-start | bytes 983048 | tf_op jit(solution)/shard_map/ppermute | solution.py:65
  104.9 19.0 %collective-permute-start.26 = (bf16[128,5120]{1,0:T(8,128)(2,1)S(1)}, bf16[128,5120]{1,0:T(8,128)(2,1)S(1)}, u32[]{:S(2)}, u32[]{:S(2)}) collective-permute-start(bf16[128,5120]{1,0:T(8,128)(2,1)S(1)} %pad_maximum_fusion.4.b0_ref), channel_id=1, source_target_pairs={{0,96},{1,25},{2,98},{3,27},{4,100},{5,29},{6,102},{7,31},{8,104},... | collective-permute-start | bytes 3932168 | tf_op jit(solution)/shard_map/ppermute | solution.py:65
  108.8 18.8 %collective-permute-start.25 = (bf16[128,5120]{1,0:T(8,128)(2,1)S(1)}, bf16[128,5120]{1,0:T(8,128)(2,1)S(1)}, u32[]{:S(2)}, u32[]{:S(2)}) collective-permute-start(bf16[128,5120]{1,0:T(8,128)(2,1)S(1)} %pad_maximum_fusion.4.b0_ref), channel_id=1, source_target_pairs={{0,32},{1,9},{2,34},{3,11},{4,36},{5,13},{6,38},{7,15},{8,40},{9,1... | collective-permute-start | bytes 3932168 | tf_op jit(solution)/shard_map/ppermute | solution.py:65
  118.9 19.0 %collective-permute-start.33 = (bf16[128,5120]{1,0:T(8,128)(2,1)S(1)}, bf16[128,5120]{1,0:T(8,128)(2,1)S(1)}, u32[]{:S(2)}, u32[]{:S(2)}) collective-permute-start(bf16[128,5120]{1,0:T(8,128)(2,1)S(1)} %pad_maximum_fusion.5.b0_ref), channel_id=1, source_target_pairs={{0,96},{1,25},{2,98},{3,27},{4,100},{5,29},{6,102},{7,31},{8,104},... | collective-permute-start | bytes 3932168 | tf_op jit(solution)/shard_map/ppermute | solution.py:65
  122.8 18.8 %collective-permute-start.32 = (bf16[128,5120]{1,0:T(8,128)(2,1)S(1)}, bf16[128,5120]{1,0:T(8,128)(2,1)S(1)}, u32[]{:S(2)}, u32[]{:S(2)}) collective-permute-start(bf16[128,5120]{1,0:T(8,128)(2,1)S(1)} %pad_maximum_fusion.5.b0_ref), channel_id=1, source_target_pairs={{0,32},{1,9},{2,34},{3,11},{4,36},{5,13},{6,38},{7,15},{8,40},{9,1... | collective-permute-start | bytes 3932168 | tf_op jit(solution)/shard_map/ppermute | solution.py:65
  127.7 17.3 %collective-permute-start.31 = (bf16[128,2560]{1,0:T(8,128)(2,1)S(1)}, bf16[128,2560]{1,0:T(8,128)(2,1)S(1)}, u32[]{:S(2)}, u32[]{:S(2)}) collective-permute-start(bf16[128,2560]{1,0:T(8,128)(2,1)S(1)} %slice.97), channel_id=1, source_target_pairs={{0,96},{1,25},{2,98},{3,27},{4,100},{5,29},{6,102},{7,31},{8,104},... | collective-permute-start | bytes 1966088 | tf_op jit(solution)/shard_map/ppermute | solution.py:65
  127.8 20.9 %collective-permute-start.30 = (bf16[128,2560]{1,0:T(8,128)(2,1)S(1)}, bf16[128,2560]{1,0:T(8,128)(2,1)S(1)}, u32[]{:S(2)}, u32[]{:S(2)}) collective-permute-start(bf16[128,2560]{1,0:T(8,128)(2,1)S(1)} %slice.96), channel_id=1, source_target_pairs={{0,32},{1,9},{2,34},{3,11},{4,36},{5,13},{6,38},{7,15},{8,40},{9,1... | collective-permute-start | bytes 1966088 | tf_op jit(solution)/shard_map/ppermute | solution.py:65
  141.7 10.9 %collective-permute-start.36 = (bf16[128,2560]{1,0:T(8,128)(2,1)S(1)}, bf16[128,2560]{1,0:T(8,128)(2,1)S(1)}, u32[]{:S(2)}, u32[]{:S(2)}) collective-permute-start(bf16[128,2560]{1,0:T(8,128)(2,1)S(1)} %slice.99), channel_id=1, source_target_pairs={{0,96},{1,25},{2,98},{3,27},{4,100},{5,29},{6,102},{7,31},{8,104},... | collective-permute-start | bytes 1966088 | tf_op jit(solution)/shard_map/ppermute | solution.py:65
  141.8 13.9 %collective-permute-start.35 = (bf16[128,2560]{1,0:T(8,128)(2,1)S(1)}, bf16[128,2560]{1,0:T(8,128)(2,1)S(1)}, u32[]{:S(2)}, u32[]{:S(2)}) collective-permute-start(bf16[128,2560]{1,0:T(8,128)(2,1)S(1)} %slice.98), channel_id=1, source_target_pairs={{0,32},{1,9},{2,34},{3,11},{4,36},{5,13},{6,38},{7,15},{8,40},{9,1... | collective-permute-start | bytes 1966088 | tf_op jit(solution)/shard_map/ppermute | solution.py:65
  152.6 9.8 %collective-permute-start.34 = (bf16[4,64,640]{2,1,0:T(8,128)(2,1)S(1)}, bf16[4,64,640]{2,1,0:T(8,128)(2,1)S(1)}, u32[]{:S(2)}, u32[]{:S(2)}) collective-permute-start(bf16[4,64,640]{2,1,0:T(8,128)(2,1)S(1)} %bitcast.19), channel_id=1, source_target_pairs={{0,1},{1,0},{2,3},{3,2},{4,5},{5,4},{6,7},{7,6},{8,9},{9,8},{10,11... | collective-permute-start | bytes 983048 | tf_op jit(solution)/shard_map/ppermute | solution.py:73
  162.5 9.4 %collective-permute-start.39 = (bf16[64,640]{1,0:T(8,128)(2,1)S(1)}, bf16[64,640]{1,0:T(8,128)(2,1)S(1)}, u32[]{:S(2)}, u32[]{:S(2)}) collective-permute-start(bf16[64,640]{1,0:T(8,128)(2,1)S(1)} %get-tuple-element.129), channel_id=1, source_target_pairs={{0,6},{1,7},{2,0},{3,1},{4,2},{5,3},{6,4},{7,5},{8,14},{9,15},{10,... | collective-permute-start | bytes 245768 | tf_op jit(solution)/shard_map/ppermute | solution.py:69
  162.9 9.0 %collective-permute-start.38 = (bf16[64,640]{1,0:T(8,128)(2,1)S(1)}, bf16[64,640]{1,0:T(8,128)(2,1)S(1)}, u32[]{:S(2)}, u32[]{:S(2)}) collective-permute-start(bf16[64,640]{1,0:T(8,128)(2,1)S(1)} %get-tuple-element.130), channel_id=1, source_target_pairs={{0,2},{1,3},{2,4},{3,5},{4,6},{5,7},{6,0},{7,1},{8,10},{9,11},{10,... | collective-permute-start | bytes 245768 | tf_op jit(solution)/shard_map/ppermute | solution.py:69
  (13 other events, 84.9 us)

commit v4 on v3

--- a/solution.py
+++ b/solution.py
@@ -11,15 +11,16 @@
 N_X, N_Y, N_Z, N_C = 4, 4, 4, 2
 TOK, WID, FFL = 512, 640, 5120
 HALF = FFL // 2
-TILE = 1280
+TILE = 2560
 TILES = FFL // TILE
 AXES = ("row", "col")
 F32, BF16 = jnp.float32, jnp.bfloat16
-LIMIT = 24 * 2**20
+LIMIT = 32 * 2**20
 STEPS = (
     ("h", "gather_z"),
     ("g", "gather_z"),
     ("h", "gather_core"),
+    ("g", "gather_z_far"),
     ("h", "partials"),
     ("g", "gather_core"),
     ("h", "send_far"),
@@ -36,7 +37,9 @@
     ("h", "gather_near"),
     ("g", "gather_far"),
     ("", "near_input_grads"),
+    ("", "near_grad_w_in"),
     ("h", "gather_far"),
+    ("", "near_grad_w_out"),
     ("", "far_input_grads"),
     ("", "grad_w_out"),
     ("", "sum_cores"),
@@ -166,13 +169,17 @@
     out_ref[...] += lax.dot_general(grad, wi_ref[...], (((1,), (1,)), ((), ())), preferred_element_type=F32)
 
 
-def far_input_grads_kernel(order_ref, wi_ref, b2_ref, near_ref, out_ref, total):
+def chosen(left_ref, right_ref):
+    return jnp.where(pl.program_id(0) < TILES // 2, left_ref[...], right_ref[...])
+
+
+def far_input_grads_kernel(order_ref, wi_ref, left_ref, right_ref, near_ref, out_ref, total):
     @pl.when(pl.program_id(0) == 0)
     def _():
         total[...] = jnp.zeros_like(total)
 
     total[...] += lax.dot_general(
-        b2_ref[...], wi_ref[...], (((1,), (1,)), ((), ())), preferred_element_type=F32
+        chosen(left_ref, right_ref), wi_ref[...], (((1,), (1,)), ((), ())), preferred_element_type=F32
     )
 
     @pl.when(pl.program_id(0) == pl.num_programs(0) - 1)
@@ -188,6 +195,15 @@
             out_ref[rows, :] = term.astype(BF16)
 
 
+def block_specs(last, blocks):
+    if not last:
+        return [pl.BlockSpec((128, TILE), lambda i: (0, i)) for _ in blocks]
+    return [
+        pl.BlockSpec((128, TILE), lambda i: (0, jnp.minimum(i, TILES // 2 - 1))),
+        pl.BlockSpec((128, TILE), lambda i: (0, jnp.maximum(i - TILES // 2, 0))),
+    ]
+
+
 def input_grads(w_in, blocks, near=None, order=None):
     last = near is not None
     whole = lambda rows: pl.BlockSpec((rows, WID), lambda i: (0, 0))
@@ -197,7 +213,7 @@
         out_shape=jax.ShapeDtypeStruct((TOK, WID), BF16) if last else jax.ShapeDtypeStruct((384, WID), F32),
         in_specs=([pl.BlockSpec(memory_space=pltpu.SMEM)] if last else [])
         + [pl.BlockSpec((WID, TILE), lambda i: (0, i))]
-        + [pl.BlockSpec((128, TILE), lambda i: (0, i)) for _ in blocks]
+        + block_specs(last, blocks)
         + ([whole(384)] if last else []),
         out_specs=whole(TOK if last else 384),
         scratch_shapes=[pltpu.VMEM((128, WID), F32)] if last else [],
@@ -209,38 +225,37 @@
     )(*((order,) if last else ()), w_in, *blocks, *((near,) if last else ()))
 
 
-def w_out_kernel(c_ref, b0_ref, b1_ref, b2_ref, b3_ref, out_ref):
-    act = jnp.concatenate([b0_ref[...], b1_ref[...], b2_ref[...], b3_ref[...]], axis=0)
-    out_ref[...] = lax.dot_general(
-        act, c_ref[...], (((0,), (0,)), ((), ())), preferred_element_type=F32
-    ).astype(BF16)
-
-
-def w_in_kernel(x_ref, b0_ref, b1_ref, b2_ref, b3_ref, out_ref):
-    grad = jnp.concatenate([b0_ref[...], b1_ref[...], b2_ref[...], b3_ref[...]], axis=0)
-    out_ref[...] = lax.dot_general(
-        x_ref[...], grad, (((0,), (0,)), ((), ())), preferred_element_type=F32
-    ).astype(BF16)
-
-
-def weight_grads(outer, rows, blocks):
+def near_weight_kernel(outer, rows_ref, b0_ref, b1_ref, b3_ref, out_ref):
+    rows = jnp.concatenate([rows_ref[:256], rows_ref[384:]], axis=0)
+    block = jnp.concatenate([b0_ref[...], b1_ref[...], b3_ref[...]], axis=0)
+    pair = (block, rows) if outer else (rows, block)
+    out_ref[...] = lax.dot_general(*pair, (((0,), (0,)), ((), ())), preferred_element_type=F32).astype(BF16)
+
+
+def far_weight_kernel(outer, rows_ref, left_ref, right_ref, near_ref, out_ref):
+    rows, block = rows_ref[256:384], chosen(left_ref, right_ref)
+    pair = (block, rows) if outer else (rows, block)
+    term = lax.dot_general(*pair, (((0,), (0,)), ((), ())), preferred_element_type=F32)
+    out_ref[...] = (near_ref[...].astype(F32) + term).astype(BF16)
+
+
+def weight_grads(outer, rows, blocks, near=None):
+    last = near is not None
+    spec = (
+        pl.BlockSpec((TILE, WID), lambda i: (i, 0)) if outer else pl.BlockSpec((WID, TILE), lambda i: (0, i))
+    )
     return pl.pallas_call(
-        w_out_kernel if outer else w_in_kernel,
+        functools.partial(far_weight_kernel if last else near_weight_kernel, outer),
         grid=(TILES,),
         out_shape=jax.ShapeDtypeStruct((FFL, WID) if outer else (WID, FFL), BF16),
         in_specs=[pl.BlockSpec((TOK, WID), lambda i: (0, 0))]
-        + [pl.BlockSpec((128, TILE), lambda i: (0, i))] * 4,
-        out_specs=(
-            pl.BlockSpec((TILE, WID), lambda i: (i, 0))
-            if outer
-            else pl.BlockSpec((WID, TILE), lambda i: (0, i))
-        ),
+        + block_specs(last, blocks)
+        + [spec] * last,
+        out_specs=spec,
         compiler_params=pltpu.CompilerParams(vmem_limit_bytes=LIMIT),
-        cost_estimate=pl.CostEstimate(
-            flops=2 * TOK * WID, bytes_accessed=2 * (TOK + WID), transcendentals=0
-        ),
-        name="grad_w_out" if outer else "grad_w_in",
-    )(rows, *blocks)
+        cost_estimate=pl.CostEstimate(flops=TOK * WID, bytes_accessed=TOK * WID, transcendentals=0),
+        name=("far_" if last else "near_") + ("grad_w_out" if outer else "grad_w_in"),
+    )(rows, *blocks, *((near,) if last else ()))
 
 
 class Stream:
@@ -248,8 +263,11 @@
         self.hidden, self.own, self.weight = hidden, tokens, weight
 
     def gather_z(self, env):
-        self.came = tuple(hop_z(self.own, step) for step in (2, 1, -1))
-        return ()
+        steps = (2, 1, -1) if self.hidden else (1, -1)
+        self.came = tuple(hop_z(self.own, step) for step in steps)
+
+    def gather_z_far(self, env):
+        self.came = hop_z(env.after(self.own), 2), *self.came
 
     def gather_core(self, env):
         own, far, left, right = env.after((self.own, *self.came))
@@ -302,9 +320,11 @@
         self.came = hop(halves[0], 1, True), hop(halves[1], -1, True)
         return halves
 
-    def blocks(self, env):
-        far = jnp.concatenate(env.after(self.came), axis=1)
-        return self.quarter, self.right, far, self.left
+    def near(self):
+        return self.quarter, self.right, self.left
+
+    def far(self, env):
+        return env.after(self.came)
 
 
 class Env:
@@ -323,30 +343,37 @@
         return self.g.own, self.h.own
 
     def near_input_grads(self, env):
-        g = self.g
-        self.near = input_grads(self.w_in, env.after((g.quarter, g.right, g.left)))
+        self.near = input_grads(self.w_in, env.after(self.g.near()))
         return (self.near,)
 
+    def near_grad_w_in(self, env):
+        self.near_w_in = weight_grads(False, env.after(self.h.rows), self.g.near())
+        return (self.near_w_in,)
+
+    def near_grad_w_out(self, env):
+        self.near_w_out = weight_grads(True, env.after(self.g.rows), self.h.near())
+        return (self.near_w_out,)
+
     def far_input_grads(self, env):
-        self.grad_blocks = self.g.blocks(env)
-        sums = input_grads(self.w_in, self.grad_blocks[2:3], self.near, self.order)
+        self.g_far = self.g.far(env)
+        sums = input_grads(self.w_in, self.g_far, self.near, self.order)
         self.sums = sums.reshape(2, N_Z, 64, WID)
         self.swapped = swap_core(self.sums[1])
         return (self.sums,)
 
     def grad_w_in(self, env):
-        self.w_in_result = weight_grads(False, env.after(self.h.rows), self.grad_blocks)
+        self.w_in_result = weight_grads(False, env.after(self.h.rows), self.g_far, self.near_w_in)
         return (self.w_in_result,)
+
+    def grad_w_out(self, env):
+        self.w_out_result = weight_grads(True, self.g.rows, self.h.far(env), self.near_w_out)
+        return (self.w_out_result,)
 
     def sum_cores(self, env):
         total = add(self.sums[0], env.after(self.swapped)).astype(BF16)
         self.kept = total[0]
         self.crossed = tuple(hop_z(total[step % N_Z], step) for step in (2, 1, -1))
         return (total,)
-
-    def grad_w_out(self, env):
-        self.w_out_result = weight_grads(True, self.g.rows, self.h.blocks(env))
-        return (self.w_out_result,)
 
     def sum_z(self, env):
         self.inputs_result = add(self.kept, *env.after(self.crossed)).astype(BF16)

time: 176 us -> 170 us (0.966)
  waiting for transfers between devices: 69.4 us -> 60.3 us
  Pallas kernels: 33.6 us -> 35.9 us
    ppermute x28, waiting for transfers between devices: 67.8 us -> 59.8 us  [hop(): return lax.ppermute(value, AXES, neighbours(move))]
    pallas_call x2 -> x4, Pallas kernels: 12.4 us -> 17.2 us  [weight_grads(): pl.pallas_call(functools.partial(far_weight_kernel if last else near_weig...]
  transfers between devices with their start and end apart: 40 -> 40, of which waited for: 22 -> 20; matrix products, arithmetic and copies ran while one was open for 3% -> 3% of each run, Pallas kernels for 19% -> 22%
where the time goes in v4:
time: 170 us; the launch traced here: 167 us
  starting transfers between devices  62 us (36%)
  waiting for transfers between devices  60.3 us (35%)
  Pallas kernels  35.9 us (21%)
  other arithmetic  4.01 us (2%)
  local copies, waits for them, and re-layouts  3.41 us (2%)
    ppermute x28, waiting for transfers between devices, hop(): return lax.ppermute(value, AXES, neighbours(move))  59.8 us
    ppermute x28, starting transfers between devices, hop(): return lax.ppermute(value, AXES, neighbours(move))  46.8 us
    pallas_call x4, Pallas kernels, weight_grads(): pl.pallas_call(functools.partial(far_weight_kernel if last else near_weig...  17.2 us
    ppermute x9, starting transfers between devices, hop_z(): lax.ppermute(value, AXES, neighbours(lambda x, y, z, c: (x, y, z + step,...  14.9 us
    pallas_call x2, Pallas kernels, partials(): pl.pallas_call(functools.partial(partial_kernel, hidden), grid=(TILES,),...  11.3 us
    pallas_call x2, Pallas kernels, input_grads(): pl.pallas_call(far_input_grads_kernel if last else near_input_grads_kerne...  7.45 us
  transfers between devices with their start and end apart: 40, of which 20 were waited for; matrix products, arithmetic and copies ran while one was open for 3% of the time, Pallas kernels for 22%

profile of v4, /device:TPU:0, one launch (start us, length us, event | category | flops | bytes accessed | tf_op | source)
XLA Modules:
  0.0 166.8 jit_solution(12578618573957112361)
XLA Ops:
  0.6 4.0 %collective-permute-start.1 = (bf16[64,640]{1,0:T(8,128)(2,1)}, bf16[64,640]{1,0:T(8,128)(2,1)S(1)}, u32[]{:S(2)}, u32[]{:S(2)}) collective-permute-start(bf16[64,640]{1,0:T(8,128)(2,1)} %param.4), channel_id=1, source_target_pairs={{0,4},{1,5},{2,6},{3,7},{4,0},{5,1},{6,2},{7,3},{8,12},{9,13},{10,... | collective-permute-start | bytes 245768 | tf_op jit(solution)/shard_map/ppermute | solution.py:72
  7.7 2.2 %collective-permute-start.5 = (bf16[64,640]{1,0:T(8,128)(2,1)}, bf16[64,640]{1,0:T(8,128)(2,1)S(1)}, u32[]{:S(2)}, u32[]{:S(2)}) collective-permute-start(bf16[64,640]{1,0:T(8,128)(2,1)} %param.5), channel_id=1, source_target_pairs={{0,6},{1,7},{2,0},{3,1},{4,2},{5,3},{6,4},{7,5},{8,14},{9,15},{10,... | collective-permute-start | bytes 245768 | tf_op jit(solution)/shard_map/ppermute | solution.py:72
  14.4 5.8 %hidden_partials.1 = (bf16[512,640]{1,0:T(8,128)(2,1)S(1)}, bf16[128,2560]{1,0:T(8,128)(2,1)S(1)}, bf16[128,2560]{1,0:T(8,128)(2,1)S(1)}, bf16[128,5120]{1,0:T(8...) custom-call(s32[16]{0:T(128)S(1)} %fusion.12.order_ref, ...), custom_call_target="tpu_custom_call" | custom-call | flops 3355443200 | bytes 11796480 | tf_op jit(solution)/shard_map/hidden_partials/pallas_call | solution.py:127
  23.8 5.5 %grad_partials.1 = (bf16[512,640]{1,0:T(8,128)(2,1)S(1)}, bf16[128,2560]{1,0:T(8,128)(2,1)S(1)}, bf16[128,2560]{1,0:T(8,128)(2,1)S(1)}, bf16[128,5120]{1,0:T(8,1...) custom-call(s32[16]{0:T(128)S(1)} %fusion.12.order_ref, ...), custom_call_target="tpu_custom_call" | custom-call | flops 3355443200 | bytes 11796480 | tf_op jit(solution)/shard_map/grad_partials/pallas_call | solution.py:127
  30.5 3.0 %collective-permute-start.9 = (bf16[128,2560]{1,0:T(8,128)(2,1)S(1)}, bf16[128,2560]{1,0:T(8,128)(2,1)S(1)}, u32[]{:S(2)}, u32[]{:S(2)}) collective-permute-start(bf16[128,2560]{1,0:T(8,128)(2,1)S(1)} %get-tuple-element.82), channel_id=1, source_target_pairs={{0,96},{1,25},{2,98},{3,27},{4,100},{5,29},{6,102},{7,31},{8,104},... | collective-permute-start | bytes 1966088 | tf_op jit(solution)/shard_map/ppermute | solution.py:68
  33.9 2.0 %collective-permute-start.15 = (bf16[128,5120]{1,0:T(8,128)(2,1)S(1)}, bf16[128,5120]{1,0:T(8,128)(2,1)S(1)}, u32[]{:S(2)}, u32[]{:S(2)}) collective-permute-start(bf16[128,5120]{1,0:T(8,128)(2,1)S(1)} %pad_maximum_fusion.1), channel_id=1, source_target_pairs={{0,96},{1,25},{2,98},{3,27},{4,100},{5,29},{6,102},{7,31},{8,104},... | collective-permute-start | bytes 3932168 | tf_op jit(solution)/shard_map/ppermute | solution.py:68
  36.2 5.8 %collective-permute-done.8 = bf16[128,2560]{1,0:T(8,128)(2,1)S(1)} collective-permute-done((bf16[128,2560]{1,0:T(8,128)(2,1)S(1)}, bf16[128,2560]{1,0:T(8,128)(2,1)S(1)}, u32[]{:S(2)}, u32[]{:S(2)}) %collective-permute-start.8) | collective-permute-done | bytes 655392 | tf_op jit(solution)/shard_map/ppermute | solution.py:68
  42.3 3.3 %collective-permute-start.13 = (bf16[128,5120]{1,0:T(8,128)(2,1)S(1)}, bf16[128,5120]{1,0:T(8,128)(2,1)S(1)}, u32[]{:S(2)}, u32[]{:S(2)}) collective-permute-start(bf16[128,5120]{1,0:T(8,128)(2,1)S(1)} %pad_maximum_fusion.3), channel_id=1, source_target_pairs={{0,96},{1,25},{2,98},{3,27},{4,100},{5,29},{6,102},{7,31},{8,104},... | collective-permute-start | bytes 3932168 | tf_op jit(solution)/shard_map/ppermute | solution.py:68
  46.0 9.6 %collective-permute-done.15 = bf16[128,5120]{1,0:T(8,128)(2,1)S(1)} collective-permute-done((bf16[128,5120]{1,0:T(8,128)(2,1)S(1)}, bf16[128,5120]{1,0:T(8,128)(2,1)S(1)}, u32[]{:S(2)}, u32[]{:S(2)}) %collective-permute-start.15) | collective-permute-done | bytes 1310752 | tf_op jit(solution)/shard_map/ppermute | solution.py:68
  56.8 3.3 %collective-permute-start.21 = (bf16[32,5120]{1,0:T(8,128)(2,1)S(1)}, bf16[32,5120]{1,0:T(8,128)(2,1)S(1)}, u32[]{:S(2)}, u32[]{:S(2)}) collective-permute-start(bf16[32,5120]{1,0:T(8,128)(2,1)S(1)} %get-tuple-element.130), channel_id=1, source_target_pairs={{0,16},{1,65},{2,18},{3,67},{4,20},{5,69},{6,22},{7,71},{8,24},{9,... | collective-permute-start | bytes 983048 | tf_op jit(solution)/shard_map/ppermute | solution.py:68
  60.7 2.6 %collective-permute-start.19 = (bf16[32,5120]{1,0:T(8,128)(2,1)S(1)}, bf16[32,5120]{1,0:T(8,128)(2,1)S(1)}, u32[]{:S(2)}, u32[]{:S(2)}) collective-permute-start(bf16[32,5120]{1,0:T(8,128)(2,1)S(1)} %get-tuple-element.132), channel_id=1, source_target_pairs={{0,24},{1,97},{2,26},{3,99},{4,28},{5,101},{6,30},{7,103},{8,0},{9... | collective-permute-start | bytes 983048 | tf_op jit(solution)/shard_map/ppermute | solution.py:68
  63.3 13.4 %collective-permute-done.13 = bf16[128,5120]{1,0:T(8,128)(2,1)S(1)} collective-permute-done((bf16[128,5120]{1,0:T(8,128)(2,1)S(1)}, bf16[128,5120]{1,0:T(8,128)(2,1)S(1)}, u32[]{:S(2)}, u32[]{:S(2)}) %collective-permute-start.13) | collective-permute-done | bytes 1310752 | tf_op jit(solution)/shard_map/ppermute | solution.py:68
  77.8 3.3 %collective-permute-start.18 = (bf16[32,5120]{1,0:T(8,128)(2,1)S(1)}, bf16[32,5120]{1,0:T(8,128)(2,1)S(1)}, u32[]{:S(2)}, u32[]{:S(2)}) collective-permute-start(bf16[32,5120]{1,0:T(8,128)(2,1)S(1)} %get-tuple-element.127), channel_id=1, source_target_pairs={{0,16},{1,65},{2,18},{3,67},{4,20},{5,69},{6,22},{7,71},{8,24},{9,... | collective-permute-start | bytes 983048 | tf_op jit(solution)/shard_map/ppermute | solution.py:68
  81.8 2.6 %collective-permute-start.16 = (bf16[32,5120]{1,0:T(8,128)(2,1)S(1)}, bf16[32,5120]{1,0:T(8,128)(2,1)S(1)}, u32[]{:S(2)}, u32[]{:S(2)}) collective-permute-start(bf16[32,5120]{1,0:T(8,128)(2,1)S(1)} %get-tuple-element.129), channel_id=1, source_target_pairs={{0,24},{1,97},{2,26},{3,99},{4,28},{5,101},{6,30},{7,103},{8,0},{9... | collective-permute-start | bytes 983048 | tf_op jit(solution)/shard_map/ppermute | solution.py:68
  86.6 3.4 %collective-permute-done.17 = bf16[32,5120]{1,0:T(8,128)(2,1)S(1)} collective-permute-done((bf16[32,5120]{1,0:T(8,128)(2,1)S(1)}, bf16[32,5120]{1,0:T(8,128)(2,1)S(1)}, u32[]{:S(2)}, u32[]{:S(2)}) %collective-permute-start.17) | collective-permute-done | bytes 327712 | tf_op jit(solution)/shard_map/ppermute | solution.py:68
  90.8 2.2 %collective-permute-start.24 = (bf16[32,5120]{1,0:T(8,128)(2,1)S(1)}, bf16[32,5120]{1,0:T(8,128)(2,1)S(1)}, u32[]{:S(2)}, u32[]{:S(2)}) collective-permute-start(bf16[32,5120]{1,0:T(8,128)(2,1)S(1)} %fusion.5), channel_id=1, source_target_pairs={{0,16},{1,65},{2,18},{3,67},{4,20},{5,69},{6,22},{7,71},{8,24},{9,... | collective-permute-start | bytes 983048 | tf_op jit(solution)/shard_map/ppermute | solution.py:68
  99.5 2.7 %collective-permute-start.27 = (bf16[32,5120]{1,0:T(8,128)(2,1)S(1)}, bf16[32,5120]{1,0:T(8,128)(2,1)S(1)}, u32[]{:S(2)}, u32[]{:S(2)}) collective-permute-start(bf16[32,5120]{1,0:T(8,128)(2,1)S(1)} %get-tuple-element.125), channel_id=1, source_target_pairs={{0,24},{1,97},{2,26},{3,99},{4,28},{5,101},{6,30},{7,103},{8,0},{9... | collective-permute-start | bytes 983048 | tf_op jit(solution)/shard_map/ppermute | solution.py:68
  103.1 3.9 %collective-permute-start.26 = (bf16[128,5120]{1,0:T(8,128)(2,1)S(1)}, bf16[128,5120]{1,0:T(8,128)(2,1)S(1)}, u32[]{:S(2)}, u32[]{:S(2)}) collective-permute-start(bf16[128,5120]{1,0:T(8,128)(2,1)S(1)} %pad_maximum_fusion.4.b0_ref), channel_id=1, source_target_pairs={{0,96},{1,25},{2,98},{3,27},{4,100},{5,29},{6,102},{7,31},{8,104},... | collective-permute-start | bytes 3932168 | tf_op jit(solution)/shard_map/ppermute | solution.py:68
  107.6 5.2 %collective-permute-done.28 = bf16[32,5120]{1,0:T(8,128)(2,1)S(1)} collective-permute-done((bf16[32,5120]{1,0:T(8,128)(2,1)S(1)}, bf16[32,5120]{1,0:T(8,128)(2,1)S(1)}, u32[]{:S(2)}, u32[]{:S(2)}) %collective-permute-start.28) | collective-permute-done | bytes 327712 | tf_op jit(solution)/shard_map/ppermute | solution.py:68
  112.9 4.1 %collective-permute-done.27 = bf16[32,5120]{1,0:T(8,128)(2,1)S(1)} collective-permute-done((bf16[32,5120]{1,0:T(8,128)(2,1)S(1)}, bf16[32,5120]{1,0:T(8,128)(2,1)S(1)}, u32[]{:S(2)}, u32[]{:S(2)}) %collective-permute-start.27) | collective-permute-done | bytes 327712 | tf_op jit(solution)/shard_map/ppermute | solution.py:68
  117.1 3.9 %collective-permute-start.33 = (bf16[128,5120]{1,0:T(8,128)(2,1)S(1)}, bf16[128,5120]{1,0:T(8,128)(2,1)S(1)}, u32[]{:S(2)}, u32[]{:S(2)}) collective-permute-start(bf16[128,5120]{1,0:T(8,128)(2,1)S(1)} %pad_maximum_fusion.5.b0_ref), channel_id=1, source_target_pairs={{0,96},{1,25},{2,98},{3,27},{4,100},{5,29},{6,102},{7,31},{8,104},... | collective-permute-start | bytes 3932168 | tf_op jit(solution)/shard_map/ppermute | solution.py:68
  122.1 3.7 %collective-permute-done.25.b3_ref = bf16[128,5120]{1,0:T(8,128)(2,1)S(1)} collective-permute-done((bf16[128,5120]{1,0:T(8,128)(2,1)S(1)}, bf16[128,5120]{1,0:T(8,128)(2,1)S(1)}, u32[]{:S(2)}, u32[]{:S(2)}) %collective-permute-start.25) | collective-permute-done | bytes 1310752 | tf_op jit(solution)/shard_map/ppermute | solution.py:68
  126.0 2.0 %collective-permute-start.30 = (bf16[128,2560]{1,0:T(8,128)(2,1)S(1)}, bf16[128,2560]{1,0:T(8,128)(2,1)S(1)}, u32[]{:S(2)}, u32[]{:S(2)}) collective-permute-start(bf16[128,2560]{1,0:T(8,128)(2,1)S(1)} %slice.96), channel_id=1, source_target_pairs={{0,32},{1,9},{2,34},{3,11},{4,36},{5,13},{6,38},{7,15},{8,40},{9,1... | collective-permute-start | bytes 1966088 | tf_op jit(solution)/shard_map/ppermute | solution.py:68
  128.0 4.2 %near_input_grads.1.near_ref = f32[384,640]{1,0:T(8,128)S(1)} custom-call(bf16[640,5120]{1,0:T(8,128)(2,1)S(1)} %bitcast.15, bf16[128,5120]{1,0:T(8,128)(2,1)S(1)} %pad_maximum_fusion.4.b0_ref, bf16[128,5120]{1,0:T(8,128)(2,1)S(1)} %collective-permute-done.26.b1_ref, bf16[128,5120]{1,0:T(8,128)(2,1)S(1)} %collective-permute-done.25.b3_ref), custom_call_target="tpu_custom_call" | custom-call | flops 2516582400 | bytes 11796480 | tf_op jit(solution)/shard_map/near_input_grads/pallas_call | solution.py:210
  132.2 4.5 %near_grad_w_in.1.near_ref = bf16[640,5120]{1,0:T(8,128)(2,1)S(1)} custom-call(bf16[512,640]{1,0:T(8,128)(2,1)S(1)} %get-tuple-element.121.rows_ref, bf16[128,5120]{1,0:T(8,128)(2,1)S(1)} %pad_maximum_fusion.4.b0_ref, bf16[128,5120]{1,0:T(8,128)(2,1)S(1)} %collective-permute-done.26.b1_ref, bf16[128,5120]{1,0:T(8,128)(2,1)S(1)} %collective-permute-done.25.b3_ref), custom_call_target="tpu_custom_call" | custom-call | flops 327680 | bytes 327680 | tf_op jit(solution)/shard_map/near_grad_w_in/pallas_call | solution.py:247
  136.8 3.0 %collective-permute-done.32.b3_ref = bf16[128,5120]{1,0:T(8,128)(2,1)S(1)} collective-permute-done((bf16[128,5120]{1,0:T(8,128)(2,1)S(1)}, bf16[128,5120]{1,0:T(8,128)(2,1)S(1)}, u32[]{:S(2)}, u32[]{:S(2)}) %collective-permute-start.32) | collective-permute-done | bytes 1310752 | tf_op jit(solution)/shard_map/ppermute | solution.py:68
  140.0 2.0 %collective-permute-start.35 = (bf16[128,2560]{1,0:T(8,128)(2,1)S(1)}, bf16[128,2560]{1,0:T(8,128)(2,1)S(1)}, u32[]{:S(2)}, u32[]{:S(2)}) collective-permute-start(bf16[128,2560]{1,0:T(8,128)(2,1)S(1)} %slice.98), channel_id=1, source_target_pairs={{0,32},{1,9},{2,34},{3,11},{4,36},{5,13},{6,38},{7,15},{8,40},{9,1... | collective-permute-start | bytes 1966088 | tf_op jit(solution)/shard_map/ppermute | solution.py:68
  142.0 4.5 %near_grad_w_out.1.near_ref = bf16[5120,640]{1,0:T(8,128)(2,1)S(1)} custom-call(bf16[512,640]{1,0:T(8,128)(2,1)S(1)} %copy-done.1, bf16[128,5120]{1,0:T(8,128)(2,1)S(1)} %pad_maximum_fusion.5.b0_ref, bf16[128,5120]{1,0:T(8,128)(2,1)S(1)} %collective-permute-done.33.b1_ref, bf16[128,5120]{1,0:T(8,128)(2,1)S(1)} %collective-permute-done.32.b3_ref), custom_call_target="tpu_custom_call" | custom-call | flops 327680 | bytes 327680 | tf_op jit(solution)/shard_map/near_grad_w_out/pallas_call | solution.py:247
  146.8 3.2 %far_input_grads.1 = bf16[512,640]{1,0:T(8,128)(2,1)S(1)} custom-call(s32[16]{0:T(128)S(1)} %fusion.12.order_ref, bf16[640,5120]{1,0:T(8,128)(2,1)S(1)} %bitcast.15, bf16[128,2560]{1,0:T(8,128)(2,1)S(1)} %collective-permute-done.30.left_ref, bf16[128,2560]{1,0:T(8,128)(2,1)S(1)} %collective-permute-done.31.right_ref, f32[384,640]{1,0:T(8,128)S(1)} %near_input_grads.1.near_ref), custom_call_target="tpu_custom_call" | custom-call | flops 1677721600 | bytes 11796480 | tf_op jit(solution)/shard_map/far_input_grads/pallas_call | solution.py:210
  150.6 3.3 %collective-permute-done.35.left_ref = bf16[128,2560]{1,0:T(8,128)(2,1)S(1)} collective-permute-done((bf16[128,2560]{1,0:T(8,128)(2,1)S(1)}, bf16[128,2560]{1,0:T(8,128)(2,1)S(1)}, u32[]{:S(2)}, u32[]{:S(2)}) %collective-permute-start.35) | collective-permute-done | bytes 655392 | tf_op jit(solution)/shard_map/ppermute | solution.py:68
  153.9 3.9 %far_grad_w_out.1 = bf16[5120,640]{1,0:T(8,128)(2,1)} custom-call(bf16[512,640]{1,0:T(8,128)(2,1)S(1)} %copy-done.1, bf16[128,2560]{1,0:T(8,128)(2,1)S(1)} %collective-permute-done.35.left_ref, bf16[128,2560]{1,0:T(8,128)(2,1)S(1)} %collective-permute-done.36.right_ref, bf16[5120,640]{1,0:T(8,128)(2,1)S(1)} %near_grad_w_out.1.near_ref), custom_call_target="tpu_custom_call" | custom-call | flops 327680 | bytes 327680 | tf_op jit(solution)/shard_map/far_grad_w_out/pallas_call | solution.py:247
  161.9 4.3 %far_grad_w_in.1 = bf16[640,5120]{1,0:T(8,128)(2,1)} custom-call(bf16[512,640]{1,0:T(8,128)(2,1)S(1)} %get-tuple-element.121.rows_ref, bf16[128,2560]{1,0:T(8,128)(2,1)S(1)} %collective-permute-done.30.left_ref, bf16[128,2560]{1,0:T(8,128)(2,1)S(1)} %collective-permute-done.31.right_ref, bf16[640,5120]{1,0:T(8,128)(2,1)S(1)} %near_grad_w_in.1.near_ref), custom_call_target="tpu_custom_call" | custom-call | flops 327680 | bytes 327680 | tf_op jit(solution)/shard_map/far_grad_w_in/pallas_call | solution.py:247
  (112 shorter events, 35.2 us)
Async XLA Ops:
  0.6 10.3 %collective-permute-start.1 = (bf16[64,640]{1,0:T(8,128)(2,1)}, bf16[64,640]{1,0:T(8,128)(2,1)S(1)}, u32[]{:S(2)}, u32[]{:S(2)}) collective-permute-start(bf16[64,640]{1,0:T(8,128)(2,1)} %param.4), channel_id=1, source_target_pairs={{0,4},{1,5},{2,6},{3,7},{4,0},{5,1},{6,2},{7,3},{8,12},{9,13},{10,... | collective-permute-start | bytes 245768 | tf_op jit(solution)/shard_map/ppermute | solution.py:72
  6.7 13.4 %collective-permute-start.4 = (bf16[64,640]{1,0:T(8,128)(2,1)}, bf16[64,640]{1,0:T(8,128)(2,1)S(1)}, u32[]{:S(2)}, u32[]{:S(2)}) collective-permute-start(bf16[64,640]{1,0:T(8,128)(2,1)} %param.5), channel_id=1, source_target_pairs={{0,2},{1,3},{2,4},{3,5},{4,6},{5,7},{6,0},{7,1},{8,10},{9,11},{10,... | collective-permute-start | bytes 245768 | tf_op jit(solution)/shard_map/ppermute | solution.py:72
  7.7 12.4 %collective-permute-start.5 = (bf16[64,640]{1,0:T(8,128)(2,1)}, bf16[64,640]{1,0:T(8,128)(2,1)S(1)}, u32[]{:S(2)}, u32[]{:S(2)}) collective-permute-start(bf16[64,640]{1,0:T(8,128)(2,1)} %param.5), channel_id=1, source_target_pairs={{0,6},{1,7},{2,0},{3,1},{4,2},{5,3},{6,4},{7,5},{8,14},{9,15},{10,... | collective-permute-start | bytes 245768 | tf_op jit(solution)/shard_map/ppermute | solution.py:72
  20.4 13.1 %collective-permute-start.10 = (bf16[128,2560]{1,0:T(8,128)(2,1)S(1)}, bf16[128,2560]{1,0:T(8,128)(2,1)S(1)}, u32[]{:S(2)}, u32[]{:S(2)}) collective-permute-start(bf16[128,2560]{1,0:T(8,128)(2,1)S(1)} %get-tuple-element.83), channel_id=1, source_target_pairs={{0,32},{1,9},{2,34},{3,11},{4,36},{5,13},{6,38},{7,15},{8,40},{9,1... | collective-permute-start | bytes 1966088 | tf_op jit(solution)/shard_map/ppermute | solution.py:68
  21.9 11.6 %collective-permute-start.11 = (bf16[128,2560]{1,0:T(8,128)(2,1)S(1)}, bf16[128,2560]{1,0:T(8,128)(2,1)S(1)}, u32[]{:S(2)}, u32[]{:S(2)}) collective-permute-start(bf16[128,2560]{1,0:T(8,128)(2,1)S(1)} %get-tuple-element.84), channel_id=1, source_target_pairs={{0,96},{1,25},{2,98},{3,27},{4,100},{5,29},{6,102},{7,31},{8,104},... | collective-permute-start | bytes 1966088 | tf_op jit(solution)/shard_map/ppermute | solution.py:68
  30.2 11.8 %collective-permute-start.8 = (bf16[128,2560]{1,0:T(8,128)(2,1)S(1)}, bf16[128,2560]{1,0:T(8,128)(2,1)S(1)}, u32[]{:S(2)}, u32[]{:S(2)}) collective-permute-start(bf16[128,2560]{1,0:T(8,128)(2,1)S(1)} %get-tuple-element.81), channel_id=1, source_target_pairs={{0,32},{1,9},{2,34},{3,11},{4,36},{5,13},{6,38},{7,15},{8,40},{9,1... | collective-permute-start | bytes 1966088 | tf_op jit(solution)/shard_map/ppermute | solution.py:68
  30.5 11.5 %collective-permute-start.9 = (bf16[128,2560]{1,0:T(8,128)(2,1)S(1)}, bf16[128,2560]{1,0:T(8,128)(2,1)S(1)}, u32[]{:S(2)}, u32[]{:S(2)}) collective-permute-start(bf16[128,2560]{1,0:T(8,128)(2,1)S(1)} %get-tuple-element.82), channel_id=1, source_target_pairs={{0,96},{1,25},{2,98},{3,27},{4,100},{5,29},{6,102},{7,31},{8,104},... | collective-permute-start | bytes 1966088 | tf_op jit(solution)/shard_map/ppermute | solution.py:68
  33.9 21.7 %collective-permute-start.15 = (bf16[128,5120]{1,0:T(8,128)(2,1)S(1)}, bf16[128,5120]{1,0:T(8,128)(2,1)S(1)}, u32[]{:S(2)}, u32[]{:S(2)}) collective-permute-start(bf16[128,5120]{1,0:T(8,128)(2,1)S(1)} %pad_maximum_fusion.1), channel_id=1, source_target_pairs={{0,96},{1,25},{2,98},{3,27},{4,100},{5,29},{6,102},{7,31},{8,104},... | collective-permute-start | bytes 3932168 | tf_op jit(solution)/shard_map/ppermute | solution.py:68
  36.1 20.0 %collective-permute-start.14 = (bf16[128,5120]{1,0:T(8,128)(2,1)S(1)}, bf16[128,5120]{1,0:T(8,128)(2,1)S(1)}, u32[]{:S(2)}, u32[]{:S(2)}) collective-permute-start(bf16[128,5120]{1,0:T(8,128)(2,1)S(1)} %pad_maximum_fusion), channel_id=1, source_target_pairs={{0,32},{1,9},{2,34},{3,11},{4,36},{5,13},{6,38},{7,15},{8,40},{9,1... | collective-permute-start | bytes 3932168 | tf_op jit(solution)/shard_map/ppermute | solution.py:68
  42.3 34.4 %collective-permute-start.13 = (bf16[128,5120]{1,0:T(8,128)(2,1)S(1)}, bf16[128,5120]{1,0:T(8,128)(2,1)S(1)}, u32[]{:S(2)}, u32[]{:S(2)}) collective-permute-start(bf16[128,5120]{1,0:T(8,128)(2,1)S(1)} %pad_maximum_fusion.3), channel_id=1, source_target_pairs={{0,96},{1,25},{2,98},{3,27},{4,100},{5,29},{6,102},{7,31},{8,104},... | collective-permute-start | bytes 3932168 | tf_op jit(solution)/shard_map/ppermute | solution.py:68
  45.9 31.2 %collective-permute-start.12 = (bf16[128,5120]{1,0:T(8,128)(2,1)S(1)}, bf16[128,5120]{1,0:T(8,128)(2,1)S(1)}, u32[]{:S(2)}, u32[]{:S(2)}) collective-permute-start(bf16[128,5120]{1,0:T(8,128)(2,1)S(1)} %pad_maximum_fusion.2), channel_id=1, source_target_pairs={{0,32},{1,9},{2,34},{3,11},{4,36},{5,13},{6,38},{7,15},{8,40},{9,1... | collective-permute-start | bytes 3932168 | tf_op jit(solution)/shard_map/ppermute | solution.py:68
  56.8 25.0 %collective-permute-start.21 = (bf16[32,5120]{1,0:T(8,128)(2,1)S(1)}, bf16[32,5120]{1,0:T(8,128)(2,1)S(1)}, u32[]{:S(2)}, u32[]{:S(2)}) collective-permute-start(bf16[32,5120]{1,0:T(8,128)(2,1)S(1)} %get-tuple-element.130), channel_id=1, source_target_pairs={{0,16},{1,65},{2,18},{3,67},{4,20},{5,69},{6,22},{7,71},{8,24},{9,... | collective-permute-start | bytes 983048 | tf_op jit(solution)/shard_map/ppermute | solution.py:68
  60.0 24.3 %collective-permute-start.20 = (bf16[32,5120]{1,0:T(8,128)(2,1)S(1)}, bf16[32,5120]{1,0:T(8,128)(2,1)S(1)}, u32[]{:S(2)}, u32[]{:S(2)}) collective-permute-start(bf16[32,5120]{1,0:T(8,128)(2,1)S(1)} %get-tuple-element.131), channel_id=1, source_target_pairs={{0,8},{1,33},{2,10},{3,35},{4,12},{5,37},{6,14},{7,39},{8,16},{9,4... | collective-permute-start | bytes 983048 | tf_op jit(solution)/shard_map/ppermute | solution.py:68
  60.7 23.6 %collective-permute-start.19 = (bf16[32,5120]{1,0:T(8,128)(2,1)S(1)}, bf16[32,5120]{1,0:T(8,128)(2,1)S(1)}, u32[]{:S(2)}, u32[]{:S(2)}) collective-permute-start(bf16[32,5120]{1,0:T(8,128)(2,1)S(1)} %get-tuple-element.132), channel_id=1, source_target_pairs={{0,24},{1,97},{2,26},{3,99},{4,28},{5,101},{6,30},{7,103},{8,0},{9... | collective-permute-start | bytes 983048 | tf_op jit(solution)/shard_map/ppermute | solution.py:68
  77.8 8.7 %collective-permute-start.18 = (bf16[32,5120]{1,0:T(8,128)(2,1)S(1)}, bf16[32,5120]{1,0:T(8,128)(2,1)S(1)}, u32[]{:S(2)}, u32[]{:S(2)}) collective-permute-start(bf16[32,5120]{1,0:T(8,128)(2,1)S(1)} %get-tuple-element.127), channel_id=1, source_target_pairs={{0,16},{1,65},{2,18},{3,67},{4,20},{5,69},{6,22},{7,71},{8,24},{9,... | collective-permute-start | bytes 983048 | tf_op jit(solution)/shard_map/ppermute | solution.py:68
  81.1 8.9 %collective-permute-start.17 = (bf16[32,5120]{1,0:T(8,128)(2,1)S(1)}, bf16[32,5120]{1,0:T(8,128)(2,1)S(1)}, u32[]{:S(2)}, u32[]{:S(2)}) collective-permute-start(bf16[32,5120]{1,0:T(8,128)(2,1)S(1)} %get-tuple-element.128), channel_id=1, source_target_pairs={{0,8},{1,33},{2,10},{3,35},{4,12},{5,37},{6,14},{7,39},{8,16},{9,4... | collective-permute-start | bytes 983048 | tf_op jit(solution)/shard_map/ppermute | solution.py:68
  81.8 8.6 %collective-permute-start.16 = (bf16[32,5120]{1,0:T(8,128)(2,1)S(1)}, bf16[32,5120]{1,0:T(8,128)(2,1)S(1)}, u32[]{:S(2)}, u32[]{:S(2)}) collective-permute-start(bf16[32,5120]{1,0:T(8,128)(2,1)S(1)} %get-tuple-element.129), channel_id=1, source_target_pairs={{0,24},{1,97},{2,26},{3,99},{4,28},{5,101},{6,30},{7,103},{8,0},{9... | collective-permute-start | bytes 983048 | tf_op jit(solution)/shard_map/ppermute | solution.py:68
  90.8 8.8 %collective-permute-start.24 = (bf16[32,5120]{1,0:T(8,128)(2,1)S(1)}, bf16[32,5120]{1,0:T(8,128)(2,1)S(1)}, u32[]{:S(2)}, u32[]{:S(2)}) collective-permute-start(bf16[32,5120]{1,0:T(8,128)(2,1)S(1)} %fusion.5), channel_id=1, source_target_pairs={{0,16},{1,65},{2,18},{3,67},{4,20},{5,69},{6,22},{7,71},{8,24},{9,... | collective-permute-start | bytes 983048 | tf_op jit(solution)/shard_map/ppermute | solution.py:68
  92.9 10.0 %collective-permute-start.23 = (bf16[32,5120]{1,0:T(8,128)(2,1)S(1)}, bf16[32,5120]{1,0:T(8,128)(2,1)S(1)}, u32[]{:S(2)}, u32[]{:S(2)}) collective-permute-start(bf16[32,5120]{1,0:T(8,128)(2,1)S(1)} %fusion.5), channel_id=1, source_target_pairs={{0,8},{1,33},{2,10},{3,35},{4,12},{5,37},{6,14},{7,39},{8,16},{9,4... | collective-permute-start | bytes 983048 | tf_op jit(solution)/shard_map/ppermute | solution.py:68
  94.4 8.6 %collective-permute-start.22 = (bf16[32,5120]{1,0:T(8,128)(2,1)S(1)}, bf16[32,5120]{1,0:T(8,128)(2,1)S(1)}, u32[]{:S(2)}, u32[]{:S(2)}) collective-permute-start(bf16[32,5120]{1,0:T(8,128)(2,1)S(1)} %fusion.5), channel_id=1, source_target_pairs={{0,24},{1,97},{2,26},{3,99},{4,28},{5,101},{6,30},{7,103},{8,0},{9... | collective-permute-start | bytes 983048 | tf_op jit(solution)/shard_map/ppermute | solution.py:68
  96.2 11.5 %collective-permute-start.29 = (bf16[32,5120]{1,0:T(8,128)(2,1)S(1)}, bf16[32,5120]{1,0:T(8,128)(2,1)S(1)}, u32[]{:S(2)}, u32[]{:S(2)}) collective-permute-start(bf16[32,5120]{1,0:T(8,128)(2,1)S(1)} %get-tuple-element.125), channel_id=1, source_target_pairs={{0,16},{1,65},{2,18},{3,67},{4,20},{5,69},{6,22},{7,71},{8,24},{9,... | collective-permute-start | bytes 983048 | tf_op jit(solution)/shard_map/ppermute | solution.py:68
  96.4 16.4 %collective-permute-start.28 = (bf16[32,5120]{1,0:T(8,128)(2,1)S(1)}, bf16[32,5120]{1,0:T(8,128)(2,1)S(1)}, u32[]{:S(2)}, u32[]{:S(2)}) collective-permute-start(bf16[32,5120]{1,0:T(8,128)(2,1)S(1)} %get-tuple-element.125), channel_id=1, source_target_pairs={{0,8},{1,33},{2,10},{3,35},{4,12},{5,37},{6,14},{7,39},{8,16},{9,4... | collective-permute-start | bytes 983048 | tf_op jit(solution)/shard_map/ppermute | solution.py:68
  99.5 17.5 %collective-permute-start.27 = (bf16[32,5120]{1,0:T(8,128)(2,1)S(1)}, bf16[32,5120]{1,0:T(8,128)(2,1)S(1)}, u32[]{:S(2)}, u32[]{:S(2)}) collective-permute-start(bf16[32,5120]{1,0:T(8,128)(2,1)S(1)} %get-tuple-element.125), channel_id=1, source_target_pairs={{0,24},{1,97},{2,26},{3,99},{4,28},{5,101},{6,30},{7,103},{8,0},{9... | collective-permute-start | bytes 983048 | tf_op jit(solution)/shard_map/ppermute | solution.py:68
  103.1 19.0 %collective-permute-start.26 = (bf16[128,5120]{1,0:T(8,128)(2,1)S(1)}, bf16[128,5120]{1,0:T(8,128)(2,1)S(1)}, u32[]{:S(2)}, u32[]{:S(2)}) collective-permute-start(bf16[128,5120]{1,0:T(8,128)(2,1)S(1)} %pad_maximum_fusion.4.b0_ref), channel_id=1, source_target_pairs={{0,96},{1,25},{2,98},{3,27},{4,100},{5,29},{6,102},{7,31},{8,104},... | collective-permute-start | bytes 3932168 | tf_op jit(solution)/shard_map/ppermute | solution.py:68
  107.0 18.8 %collective-permute-start.25 = (bf16[128,5120]{1,0:T(8,128)(2,1)S(1)}, bf16[128,5120]{1,0:T(8,128)(2,1)S(1)}, u32[]{:S(2)}, u32[]{:S(2)}) collective-permute-start(bf16[128,5120]{1,0:T(8,128)(2,1)S(1)} %pad_maximum_fusion.4.b0_ref), channel_id=1, source_target_pairs={{0,32},{1,9},{2,34},{3,11},{4,36},{5,13},{6,38},{7,15},{8,40},{9,1... | collective-permute-start | bytes 3932168 | tf_op jit(solution)/shard_map/ppermute | solution.py:68
  117.1 19.7 %collective-permute-start.33 = (bf16[128,5120]{1,0:T(8,128)(2,1)S(1)}, bf16[128,5120]{1,0:T(8,128)(2,1)S(1)}, u32[]{:S(2)}, u32[]{:S(2)}) collective-permute-start(bf16[128,5120]{1,0:T(8,128)(2,1)S(1)} %pad_maximum_fusion.5.b0_ref), channel_id=1, source_target_pairs={{0,96},{1,25},{2,98},{3,27},{4,100},{5,29},{6,102},{7,31},{8,104},... | collective-permute-start | bytes 3932168 | tf_op jit(solution)/shard_map/ppermute | solution.py:68
  121.0 18.8 %collective-permute-start.32 = (bf16[128,5120]{1,0:T(8,128)(2,1)S(1)}, bf16[128,5120]{1,0:T(8,128)(2,1)S(1)}, u32[]{:S(2)}, u32[]{:S(2)}) collective-permute-start(bf16[128,5120]{1,0:T(8,128)(2,1)S(1)} %pad_maximum_fusion.5.b0_ref), channel_id=1, source_target_pairs={{0,32},{1,9},{2,34},{3,11},{4,36},{5,13},{6,38},{7,15},{8,40},{9,1... | collective-permute-start | bytes 3932168 | tf_op jit(solution)/shard_map/ppermute | solution.py:68
  125.9 20.6 %collective-permute-start.31 = (bf16[128,2560]{1,0:T(8,128)(2,1)S(1)}, bf16[128,2560]{1,0:T(8,128)(2,1)S(1)}, u32[]{:S(2)}, u32[]{:S(2)}) collective-permute-start(bf16[128,2560]{1,0:T(8,128)(2,1)S(1)} %slice.97), channel_id=1, source_target_pairs={{0,96},{1,25},{2,98},{3,27},{4,100},{5,29},{6,102},{7,31},{8,104},... | collective-permute-start | bytes 1966088 | tf_op jit(solution)/shard_map/ppermute | solution.py:68
  126.0 20.9 %collective-permute-start.30 = (bf16[128,2560]{1,0:T(8,128)(2,1)S(1)}, bf16[128,2560]{1,0:T(8,128)(2,1)S(1)}, u32[]{:S(2)}, u32[]{:S(2)}) collective-permute-start(bf16[128,2560]{1,0:T(8,128)(2,1)S(1)} %slice.96), channel_id=1, source_target_pairs={{0,32},{1,9},{2,34},{3,11},{4,36},{5,13},{6,38},{7,15},{8,40},{9,1... | collective-permute-start | bytes 1966088 | tf_op jit(solution)/shard_map/ppermute | solution.py:68
  139.9 10.7 %collective-permute-start.36 = (bf16[128,2560]{1,0:T(8,128)(2,1)S(1)}, bf16[128,2560]{1,0:T(8,128)(2,1)S(1)}, u32[]{:S(2)}, u32[]{:S(2)}) collective-permute-start(bf16[128,2560]{1,0:T(8,128)(2,1)S(1)} %slice.99), channel_id=1, source_target_pairs={{0,96},{1,25},{2,98},{3,27},{4,100},{5,29},{6,102},{7,31},{8,104},... | collective-permute-start | bytes 1966088 | tf_op jit(solution)/shard_map/ppermute | solution.py:68
  140.0 13.9 %collective-permute-start.35 = (bf16[128,2560]{1,0:T(8,128)(2,1)S(1)}, bf16[128,2560]{1,0:T(8,128)(2,1)S(1)}, u32[]{:S(2)}, u32[]{:S(2)}) collective-permute-start(bf16[128,2560]{1,0:T(8,128)(2,1)S(1)} %slice.98), channel_id=1, source_target_pairs={{0,32},{1,9},{2,34},{3,11},{4,36},{5,13},{6,38},{7,15},{8,40},{9,1... | collective-permute-start | bytes 1966088 | tf_op jit(solution)/shard_map/ppermute | solution.py:68
  157.8 8.3 %collective-permute-start.39 = (bf16[64,640]{1,0:T(8,128)(2,1)S(1)}, bf16[64,640]{1,0:T(8,128)(2,1)S(1)}, u32[]{:S(2)}, u32[]{:S(2)}) collective-permute-start(bf16[64,640]{1,0:T(8,128)(2,1)S(1)} %get-tuple-element.135), channel_id=1, source_target_pairs={{0,6},{1,7},{2,0},{3,1},{4,2},{5,3},{6,4},{7,5},{8,14},{9,15},{10,... | collective-permute-start | bytes 245768 | tf_op jit(solution)/shard_map/ppermute | solution.py:72
  (15 other events, 79.1 us)

commit v5 on v4

--- a/solution.py
+++ b/solution.py
@@ -15,7 +15,7 @@
 TILES = FFL // TILE
 AXES = ("row", "col")
 F32, BF16 = jnp.float32, jnp.bfloat16
-LIMIT = 32 * 2**20
+LIMIT = 24 * 2**20
 STEPS = (
     ("h", "gather_z"),
     ("g", "gather_z"),
@@ -41,9 +41,11 @@
     ("h", "gather_far"),
     ("", "near_grad_w_out"),
     ("", "far_input_grads"),
+    ("", "grad_w_in_left"),
+    ("", "take_far"),
+    ("", "sum_cores"),
     ("", "grad_w_out"),
-    ("", "sum_cores"),
-    ("", "grad_w_in"),
+    ("", "grad_w_in_right"),
     ("", "sum_z"),
 )
 
@@ -258,6 +260,33 @@
     )(rows, *blocks, *((near,) if last else ()))
 
 
+def far_half_kernel(rows_ref, b2_ref, near_ref, *rest):
+    term = lax.dot_general(
+        rows_ref[256:384], b2_ref[...], (((0,), (0,)), ((), ())), preferred_element_type=F32
+    )
+    rest[-1][...] = (near_ref[...].astype(F32) + term).astype(BF16)
+
+
+def far_grad_w_in(rows, half, near, base, before=()):
+    spec = pl.BlockSpec((WID, TILE), lambda i: (0, base + i))
+    return pl.pallas_call(
+        far_half_kernel,
+        grid=(TILES // 2,),
+        out_shape=jax.ShapeDtypeStruct((WID, FFL), BF16),
+        in_specs=[
+            pl.BlockSpec((TOK, WID), lambda i: (0, 0)),
+            pl.BlockSpec((128, TILE), lambda i: (0, i)),
+            spec,
+        ]
+        + [pl.BlockSpec(memory_space=pl.ANY)] * len(before),
+        out_specs=spec,
+        input_output_aliases={3: 0} if before else {},
+        compiler_params=pltpu.CompilerParams(vmem_limit_bytes=LIMIT),
+        cost_estimate=pl.CostEstimate(flops=TOK * WID, bytes_accessed=TOK * WID, transcendentals=0),
+        name="far_grad_w_in",
+    )(rows, half, near, *before)
+
+
 class Stream:
     def __init__(self, hidden, tokens, weight):
         self.hidden, self.own, self.weight = hidden, tokens, weight
@@ -361,12 +390,22 @@
         self.swapped = swap_core(self.sums[1])
         return (self.sums,)
 
-    def grad_w_in(self, env):
-        self.w_in_result = weight_grads(False, env.after(self.h.rows), self.g_far, self.near_w_in)
+    def grad_w_in_left(self, env):
+        rows = env.after(self.h.rows)
+        self.w_in_left = far_grad_w_in(rows, self.g_far[0], self.near_w_in, 0)
+        return (self.w_in_left,)
+
+    def grad_w_in_right(self, env):
+        rows = env.after(self.h.rows)
+        self.w_in_result = far_grad_w_in(rows, self.g_far[1], self.near_w_in, TILES // 2, (self.w_in_left,))
         return (self.w_in_result,)
 
+    def take_far(self, env):
+        self.h_far = self.h.far(env)
+        return self.h_far
+
     def grad_w_out(self, env):
-        self.w_out_result = weight_grads(True, self.g.rows, self.h.far(env), self.near_w_out)
+        self.w_out_result = weight_grads(True, env.after(self.g.rows), self.h_far, self.near_w_out)
         return (self.w_out_result,)
 
     def sum_cores(self, env):

time: 170 us -> 168 us (0.988)
  waiting for transfers between devices: 60.3 us -> 57 us
    pallas_call x0 -> x2, Pallas kernels: none -> 5.49 us  [far_grad_w_in(): pl.pallas_call(far_half_kernel, grid=(TILES // 2,), out_shape=jax.ShapeDt...]
    pallas_call x4 -> x3, Pallas kernels: 17.2 us -> 12.9 us  [weight_grads(): pl.pallas_call(functools.partial(far_weight_kernel if last else near_weig...]
    ppermute x28, waiting for transfers between devices: 59.8 us -> 56.4 us  [hop(): return lax.ppermute(value, AXES, neighbours(move))]
  transfers between devices with their start and end apart: 40 -> 40, of which waited for: 20 -> 19; matrix products, arithmetic and copies ran while one was open for 3% -> 3% of each run, Pallas kernels for 22% -> 23%
where the time goes in v5:
time: 168 us; the launch traced here: 165 us
  starting transfers between devices  62.6 us (37%)
  waiting for transfers between devices  57 us (34%)
  Pallas kernels  37.1 us (22%)
  other arithmetic  4.02 us (2%)
  local copies, waits for them, and re-layouts  2.69 us (2%)
    ppermute x28, waiting for transfers between devices, hop(): return lax.ppermute(value, AXES, neighbours(move))  56.4 us
    ppermute x28, starting transfers between devices, hop(): return lax.ppermute(value, AXES, neighbours(move))  47.5 us
    ppermute x9, starting transfers between devices, hop_z(): lax.ppermute(value, AXES, neighbours(lambda x, y, z, c: (x, y, z + step,...  14.9 us
    pallas_call x3, Pallas kernels, weight_grads(): pl.pallas_call(functools.partial(far_weight_kernel if last else near_weig...  12.9 us
    pallas_call x2, Pallas kernels, partials(): pl.pallas_call(functools.partial(partial_kernel, hidden), grid=(TILES,),...  11.3 us
    pallas_call x2, Pallas kernels, input_grads(): pl.pallas_call(far_input_grads_kernel if last else near_input_grads_kerne...  7.49 us
    pallas_call x2, Pallas kernels, far_grad_w_in(): pl.pallas_call(far_half_kernel, grid=(TILES // 2,), out_shape=jax.ShapeDt...  5.49 us
  transfers between devices with their start and end apart: 40, of which 19 were waited for; matrix products, arithmetic and copies ran while one was open for 3% of the time, Pallas kernels for 23%

profile of v5, /device:TPU:0, one launch (start us, length us, event | category | flops | bytes accessed | tf_op | source)
XLA Modules:
  0.0 164.6 jit_solution(15052628467641438156)
XLA Ops:
  0.6 4.0 %collective-permute-start.1 = (bf16[64,640]{1,0:T(8,128)(2,1)}, bf16[64,640]{1,0:T(8,128)(2,1)S(1)}, u32[]{:S(2)}, u32[]{:S(2)}) collective-permute-start(bf16[64,640]{1,0:T(8,128)(2,1)} %param.4), channel_id=1, source_target_pairs={{0,4},{1,5},{2,6},{3,7},{4,0},{5,1},{6,2},{7,3},{8,12},{9,13},{10,... | collective-permute-start | bytes 245768 | tf_op jit(solution)/shard_map/ppermute | solution.py:74
  7.7 2.2 %collective-permute-start.5 = (bf16[64,640]{1,0:T(8,128)(2,1)}, bf16[64,640]{1,0:T(8,128)(2,1)S(1)}, u32[]{:S(2)}, u32[]{:S(2)}) collective-permute-start(bf16[64,640]{1,0:T(8,128)(2,1)} %param.5), channel_id=1, source_target_pairs={{0,6},{1,7},{2,0},{3,1},{4,2},{5,3},{6,4},{7,5},{8,14},{9,15},{10,... | collective-permute-start | bytes 245768 | tf_op jit(solution)/shard_map/ppermute | solution.py:74
  14.4 5.7 %hidden_partials.1 = (bf16[512,640]{1,0:T(8,128)(2,1)S(1)}, bf16[128,2560]{1,0:T(8,128)(2,1)S(1)}, bf16[128,2560]{1,0:T(8,128)(2,1)S(1)}, bf16[128,5120]{1,0:T(8...) custom-call(s32[16]{0:T(128)S(1)} %fusion.12.order_ref, ...), custom_call_target="tpu_custom_call" | custom-call | flops 3355443200 | bytes 11796480 | tf_op jit(solution)/shard_map/hidden_partials/pallas_call | solution.py:129
  23.8 5.5 %grad_partials.1 = (bf16[512,640]{1,0:T(8,128)(2,1)S(1)}, bf16[128,2560]{1,0:T(8,128)(2,1)S(1)}, bf16[128,2560]{1,0:T(8,128)(2,1)S(1)}, bf16[128,5120]{1,0:T(8,1...) custom-call(s32[16]{0:T(128)S(1)} %fusion.12.order_ref, ...), custom_call_target="tpu_custom_call" | custom-call | flops 3355443200 | bytes 11796480 | tf_op jit(solution)/shard_map/grad_partials/pallas_call | solution.py:129
  29.8 3.0 %collective-permute-start.9 = (bf16[128,2560]{1,0:T(8,128)(2,1)S(1)}, bf16[128,2560]{1,0:T(8,128)(2,1)S(1)}, u32[]{:S(2)}, u32[]{:S(2)}) collective-permute-start(bf16[128,2560]{1,0:T(8,128)(2,1)S(1)} %get-tuple-element.83), channel_id=1, source_target_pairs={{0,96},{1,25},{2,98},{3,27},{4,100},{5,29},{6,102},{7,31},{8,104},... | collective-permute-start | bytes 1966088 | tf_op jit(solution)/shard_map/ppermute | solution.py:70
  33.2 2.7 %collective-permute-start.15 = (bf16[128,5120]{1,0:T(8,128)(2,1)S(1)}, bf16[128,5120]{1,0:T(8,128)(2,1)S(1)}, u32[]{:S(2)}, u32[]{:S(2)}) collective-permute-start(bf16[128,5120]{1,0:T(8,128)(2,1)S(1)} %pad_maximum_fusion.1), channel_id=1, source_target_pairs={{0,96},{1,25},{2,98},{3,27},{4,100},{5,29},{6,102},{7,31},{8,104},... | collective-permute-start | bytes 3932168 | tf_op jit(solution)/shard_map/ppermute | solution.py:70
  36.1 5.2 %collective-permute-done.8 = bf16[128,2560]{1,0:T(8,128)(2,1)S(1)} collective-permute-done((bf16[128,2560]{1,0:T(8,128)(2,1)S(1)}, bf16[128,2560]{1,0:T(8,128)(2,1)S(1)}, u32[]{:S(2)}, u32[]{:S(2)}) %collective-permute-start.8) | collective-permute-done | bytes 655392 | tf_op jit(solution)/shard_map/ppermute | solution.py:70
  41.6 3.3 %collective-permute-start.13 = (bf16[128,5120]{1,0:T(8,128)(2,1)S(1)}, bf16[128,5120]{1,0:T(8,128)(2,1)S(1)}, u32[]{:S(2)}, u32[]{:S(2)}) collective-permute-start(bf16[128,5120]{1,0:T(8,128)(2,1)S(1)} %pad_maximum_fusion.3), channel_id=1, source_target_pairs={{0,96},{1,25},{2,98},{3,27},{4,100},{5,29},{6,102},{7,31},{8,104},... | collective-permute-start | bytes 3932168 | tf_op jit(solution)/shard_map/ppermute | solution.py:70
  45.3 9.6 %collective-permute-done.15 = bf16[128,5120]{1,0:T(8,128)(2,1)S(1)} collective-permute-done((bf16[128,5120]{1,0:T(8,128)(2,1)S(1)}, bf16[128,5120]{1,0:T(8,128)(2,1)S(1)}, u32[]{:S(2)}, u32[]{:S(2)}) %collective-permute-start.15) | collective-permute-done | bytes 1310752 | tf_op jit(solution)/shard_map/ppermute | solution.py:70
  56.1 3.3 %collective-permute-start.21 = (bf16[32,5120]{1,0:T(8,128)(2,1)S(1)}, bf16[32,5120]{1,0:T(8,128)(2,1)S(1)}, u32[]{:S(2)}, u32[]{:S(2)}) collective-permute-start(bf16[32,5120]{1,0:T(8,128)(2,1)S(1)} %get-tuple-element.132), channel_id=1, source_target_pairs={{0,16},{1,65},{2,18},{3,67},{4,20},{5,69},{6,22},{7,71},{8,24},{9,... | collective-permute-start | bytes 983048 | tf_op jit(solution)/shard_map/ppermute | solution.py:70
  60.0 2.6 %collective-permute-start.19 = (bf16[32,5120]{1,0:T(8,128)(2,1)S(1)}, bf16[32,5120]{1,0:T(8,128)(2,1)S(1)}, u32[]{:S(2)}, u32[]{:S(2)}) collective-permute-start(bf16[32,5120]{1,0:T(8,128)(2,1)S(1)} %get-tuple-element.134), channel_id=1, source_target_pairs={{0,24},{1,97},{2,26},{3,99},{4,28},{5,101},{6,30},{7,103},{8,0},{9... | collective-permute-start | bytes 983048 | tf_op jit(solution)/shard_map/ppermute | solution.py:70
  62.6 13.4 %collective-permute-done.13 = bf16[128,5120]{1,0:T(8,128)(2,1)S(1)} collective-permute-done((bf16[128,5120]{1,0:T(8,128)(2,1)S(1)}, bf16[128,5120]{1,0:T(8,128)(2,1)S(1)}, u32[]{:S(2)}, u32[]{:S(2)}) %collective-permute-start.13) | collective-permute-done | bytes 1310752 | tf_op jit(solution)/shard_map/ppermute | solution.py:70
  77.1 3.3 %collective-permute-start.18 = (bf16[32,5120]{1,0:T(8,128)(2,1)S(1)}, bf16[32,5120]{1,0:T(8,128)(2,1)S(1)}, u32[]{:S(2)}, u32[]{:S(2)}) collective-permute-start(bf16[32,5120]{1,0:T(8,128)(2,1)S(1)} %get-tuple-element.129), channel_id=1, source_target_pairs={{0,16},{1,65},{2,18},{3,67},{4,20},{5,69},{6,22},{7,71},{8,24},{9,... | collective-permute-start | bytes 983048 | tf_op jit(solution)/shard_map/ppermute | solution.py:70
  81.1 2.6 %collective-permute-start.16 = (bf16[32,5120]{1,0:T(8,128)(2,1)S(1)}, bf16[32,5120]{1,0:T(8,128)(2,1)S(1)}, u32[]{:S(2)}, u32[]{:S(2)}) collective-permute-start(bf16[32,5120]{1,0:T(8,128)(2,1)S(1)} %get-tuple-element.131), channel_id=1, source_target_pairs={{0,24},{1,97},{2,26},{3,99},{4,28},{5,101},{6,30},{7,103},{8,0},{9... | collective-permute-start | bytes 983048 | tf_op jit(solution)/shard_map/ppermute | solution.py:70
  85.8 3.4 %collective-permute-done.17 = bf16[32,5120]{1,0:T(8,128)(2,1)S(1)} collective-permute-done((bf16[32,5120]{1,0:T(8,128)(2,1)S(1)}, bf16[32,5120]{1,0:T(8,128)(2,1)S(1)}, u32[]{:S(2)}, u32[]{:S(2)}) %collective-permute-start.17) | collective-permute-done | bytes 327712 | tf_op jit(solution)/shard_map/ppermute | solution.py:70
  90.1 2.2 %collective-permute-start.24 = (bf16[32,5120]{1,0:T(8,128)(2,1)S(1)}, bf16[32,5120]{1,0:T(8,128)(2,1)S(1)}, u32[]{:S(2)}, u32[]{:S(2)}) collective-permute-start(bf16[32,5120]{1,0:T(8,128)(2,1)S(1)} %fusion.5), channel_id=1, source_target_pairs={{0,16},{1,65},{2,18},{3,67},{4,20},{5,69},{6,22},{7,71},{8,24},{9,... | collective-permute-start | bytes 983048 | tf_op jit(solution)/shard_map/ppermute | solution.py:70
  98.8 2.7 %collective-permute-start.27 = (bf16[32,5120]{1,0:T(8,128)(2,1)S(1)}, bf16[32,5120]{1,0:T(8,128)(2,1)S(1)}, u32[]{:S(2)}, u32[]{:S(2)}) collective-permute-start(bf16[32,5120]{1,0:T(8,128)(2,1)S(1)} %get-tuple-element.127), channel_id=1, source_target_pairs={{0,24},{1,97},{2,26},{3,99},{4,28},{5,101},{6,30},{7,103},{8,0},{9... | collective-permute-start | bytes 983048 | tf_op jit(solution)/shard_map/ppermute | solution.py:70
  102.4 3.9 %collective-permute-start.26 = (bf16[128,5120]{1,0:T(8,128)(2,1)S(1)}, bf16[128,5120]{1,0:T(8,128)(2,1)S(1)}, u32[]{:S(2)}, u32[]{:S(2)}) collective-permute-start(bf16[128,5120]{1,0:T(8,128)(2,1)S(1)} %pad_maximum_fusion.4.b0_ref), channel_id=1, source_target_pairs={{0,96},{1,25},{2,98},{3,27},{4,100},{5,29},{6,102},{7,31},{8,104},... | collective-permute-start | bytes 3932168 | tf_op jit(solution)/shard_map/ppermute | solution.py:70
  106.9 5.2 %collective-permute-done.28 = bf16[32,5120]{1,0:T(8,128)(2,1)S(1)} collective-permute-done((bf16[32,5120]{1,0:T(8,128)(2,1)S(1)}, bf16[32,5120]{1,0:T(8,128)(2,1)S(1)}, u32[]{:S(2)}, u32[]{:S(2)}) %collective-permute-start.28) | collective-permute-done | bytes 327712 | tf_op jit(solution)/shard_map/ppermute | solution.py:70
  112.2 4.1 %collective-permute-done.27 = bf16[32,5120]{1,0:T(8,128)(2,1)S(1)} collective-permute-done((bf16[32,5120]{1,0:T(8,128)(2,1)S(1)}, bf16[32,5120]{1,0:T(8,128)(2,1)S(1)}, u32[]{:S(2)}, u32[]{:S(2)}) %collective-permute-start.27) | collective-permute-done | bytes 327712 | tf_op jit(solution)/shard_map/ppermute | solution.py:70
  116.4 3.9 %collective-permute-start.33 = (bf16[128,5120]{1,0:T(8,128)(2,1)S(1)}, bf16[128,5120]{1,0:T(8,128)(2,1)S(1)}, u32[]{:S(2)}, u32[]{:S(2)}) collective-permute-start(bf16[128,5120]{1,0:T(8,128)(2,1)S(1)} %pad_maximum_fusion.5.b0_ref), channel_id=1, source_target_pairs={{0,96},{1,25},{2,98},{3,27},{4,100},{5,29},{6,102},{7,31},{8,104},... | collective-permute-start | bytes 3932168 | tf_op jit(solution)/shard_map/ppermute | solution.py:70
  121.4 3.7 %collective-permute-done.25.b3_ref = bf16[128,5120]{1,0:T(8,128)(2,1)S(1)} collective-permute-done((bf16[128,5120]{1,0:T(8,128)(2,1)S(1)}, bf16[128,5120]{1,0:T(8,128)(2,1)S(1)}, u32[]{:S(2)}, u32[]{:S(2)}) %collective-permute-start.25) | collective-permute-done | bytes 1310752 | tf_op jit(solution)/shard_map/ppermute | solution.py:70
  125.3 2.0 %collective-permute-start.30 = (bf16[128,2560]{1,0:T(8,128)(2,1)S(1)}, bf16[128,2560]{1,0:T(8,128)(2,1)S(1)}, u32[]{:S(2)}, u32[]{:S(2)}) collective-permute-start(bf16[128,2560]{1,0:T(8,128)(2,1)S(1)} %slice.96), channel_id=1, source_target_pairs={{0,32},{1,9},{2,34},{3,11},{4,36},{5,13},{6,38},{7,15},{8,40},{9,1... | collective-permute-start | bytes 1966088 | tf_op jit(solution)/shard_map/ppermute | solution.py:70
  127.3 4.3 %near_input_grads.1.near_ref = f32[384,640]{1,0:T(8,128)S(1)} custom-call(bf16[640,5120]{1,0:T(8,128)(2,1)S(1)} %bitcast.15, bf16[128,5120]{1,0:T(8,128)(2,1)S(1)} %pad_maximum_fusion.4.b0_ref, bf16[128,5120]{1,0:T(8,128)(2,1)S(1)} %collective-permute-done.26.b1_ref, bf16[128,5120]{1,0:T(8,128)(2,1)S(1)} %collective-permute-done.25.b3_ref), custom_call_target="tpu_custom_call" | custom-call | flops 2516582400 | bytes 11796480 | tf_op jit(solution)/shard_map/near_input_grads/pallas_call | solution.py:212
  131.6 4.5 %near_grad_w_in.1.near_ref = bf16[640,5120]{1,0:T(8,128)(2,1)S(1)} custom-call(bf16[512,640]{1,0:T(8,128)(2,1)S(1)} %get-tuple-element.123.rows_ref, bf16[128,5120]{1,0:T(8,128)(2,1)S(1)} %pad_maximum_fusion.4.b0_ref, bf16[128,5120]{1,0:T(8,128)(2,1)S(1)} %collective-permute-done.26.b1_ref, bf16[128,5120]{1,0:T(8,128)(2,1)S(1)} %collective-permute-done.25.b3_ref), custom_call_target="tpu_custom_call" | custom-call | flops 327680 | bytes 327680 | tf_op jit(solution)/shard_map/near_grad_w_in/pallas_call | solution.py:249
  136.1 3.0 %collective-permute-done.32.b3_ref = bf16[128,5120]{1,0:T(8,128)(2,1)S(1)} collective-permute-done((bf16[128,5120]{1,0:T(8,128)(2,1)S(1)}, bf16[128,5120]{1,0:T(8,128)(2,1)S(1)}, u32[]{:S(2)}, u32[]{:S(2)}) %collective-permute-start.32) | collective-permute-done | bytes 1310752 | tf_op jit(solution)/shard_map/ppermute | solution.py:70
  139.3 2.0 %collective-permute-start.35 = (bf16[128,2560]{1,0:T(8,128)(2,1)S(1)}, bf16[128,2560]{1,0:T(8,128)(2,1)S(1)}, u32[]{:S(2)}, u32[]{:S(2)}) collective-permute-start(bf16[128,2560]{1,0:T(8,128)(2,1)S(1)} %slice.98), channel_id=1, source_target_pairs={{0,32},{1,9},{2,34},{3,11},{4,36},{5,13},{6,38},{7,15},{8,40},{9,1... | collective-permute-start | bytes 1966088 | tf_op jit(solution)/shard_map/ppermute | solution.py:70
  141.3 4.5 %near_grad_w_out.1.near_ref = bf16[5120,640]{1,0:T(8,128)(2,1)S(1)} custom-call(bf16[512,640]{1,0:T(8,128)(2,1)S(1)} %get-tuple-element.122.rows_ref, bf16[128,5120]{1,0:T(8,128)(2,1)S(1)} %pad_maximum_fusion.5.b0_ref, bf16[128,5120]{1,0:T(8,128)(2,1)S(1)} %collective-permute-done.33.b1_ref, bf16[128,5120]{1,0:T(8,128)(2,1)S(1)} %collective-permute-done.32.b3_ref), custom_call_target="tpu_custom_call" | custom-call | flops 327680 | bytes 327680 | tf_op jit(solution)/shard_map/near_grad_w_out/pallas_call | solution.py:249
  146.2 3.2 %far_input_grads.1 = bf16[512,640]{1,0:T(8,128)(2,1)S(1)} custom-call(s32[16]{0:T(128)S(1)} %fusion.12.order_ref, bf16[640,5120]{1,0:T(8,128)(2,1)S(1)} %bitcast.15, bf16[128,2560]{1,0:T(8,128)(2,1)S(1)} %collective-permute-done.30.left_ref.b2_ref, bf16[128,2560]{1,0:T(8,128)(2,1)S(1)} %collective-permute-done.31.right_ref.b2_ref, ...), custom_call_target="tpu_custom_call" | custom-call | flops 1677721600 | bytes 11796480 | tf_op jit(solution)/shard_map/far_input_grads/pallas_call | solution.py:212
  149.5 2.7 %far_grad_w_in.2.rest_0_ = bf16[640,5120]{1,0:T(8,128)(2,1)} custom-call(bf16[512,640]{1,0:T(8,128)(2,1)S(1)} %get-tuple-element.123.rows_ref, bf16[128,2560]{1,0:T(8,128)(2,1)S(1)} %collective-permute-done.30.left_ref.b2_ref, bf16[640,5120]{1,0:T(8,128)(2,1)S(1)} %near_grad_w_in.1.near_ref), custom_call_target="tpu_custom_call" | custom-call | flops 327680 | bytes 327680 | tf_op jit(solution)/shard_map/far_grad_w_in/pallas_call | solution.py:272
  157.3 3.8 %far_grad_w_out.1 = bf16[5120,640]{1,0:T(8,128)(2,1)} custom-call(bf16[512,640]{1,0:T(8,128)(2,1)S(1)} %get-tuple-element.122.rows_ref, bf16[128,2560]{1,0:T(8,128)(2,1)S(1)} %collective-permute-done.35.left_ref, bf16[128,2560]{1,0:T(8,128)(2,1)S(1)} %collective-permute-done.36.right_ref, bf16[5120,640]{1,0:T(8,128)(2,1)S(1)} %near_grad_w_out.1.near_ref), custom_call_target="tpu_custom_call" | custom-call | flops 327680 | bytes 327680 | tf_op jit(solution)/shard_map/far_grad_w_out/pallas_call | solution.py:249
  161.2 2.7 %far_grad_w_in.3 = bf16[640,5120]{1,0:T(8,128)(2,1)} custom-call(bf16[512,640]{1,0:T(8,128)(2,1)S(1)} %get-tuple-element.123.rows_ref, bf16[128,2560]{1,0:T(8,128)(2,1)S(1)} %collective-permute-done.31.right_ref.b2_ref, bf16[640,5120]{1,0:T(8,128)(2,1)S(1)} %near_grad_w_in.1.near_ref, ...), custom_call_target="tpu_custom_call", output_to_operand_aliasing={{}: (3, {})} | custom-call | flops 327680 | bytes 327680 | tf_op jit(solution)/shard_map/far_grad_w_in/pallas_call | solution.py:272
  (109 shorter events, 35.1 us)
Async XLA Ops:
  0.6 10.3 %collective-permute-start.1 = (bf16[64,640]{1,0:T(8,128)(2,1)}, bf16[64,640]{1,0:T(8,128)(2,1)S(1)}, u32[]{:S(2)}, u32[]{:S(2)}) collective-permute-start(bf16[64,640]{1,0:T(8,128)(2,1)} %param.4), channel_id=1, source_target_pairs={{0,4},{1,5},{2,6},{3,7},{4,0},{5,1},{6,2},{7,3},{8,12},{9,13},{10,... | collective-permute-start | bytes 245768 | tf_op jit(solution)/shard_map/ppermute | solution.py:74
  6.7 13.4 %collective-permute-start.4 = (bf16[64,640]{1,0:T(8,128)(2,1)}, bf16[64,640]{1,0:T(8,128)(2,1)S(1)}, u32[]{:S(2)}, u32[]{:S(2)}) collective-permute-start(bf16[64,640]{1,0:T(8,128)(2,1)} %param.5), channel_id=1, source_target_pairs={{0,2},{1,3},{2,4},{3,5},{4,6},{5,7},{6,0},{7,1},{8,10},{9,11},{10,... | collective-permute-start | bytes 245768 | tf_op jit(solution)/shard_map/ppermute | solution.py:74
  7.7 12.4 %collective-permute-start.5 = (bf16[64,640]{1,0:T(8,128)(2,1)}, bf16[64,640]{1,0:T(8,128)(2,1)S(1)}, u32[]{:S(2)}, u32[]{:S(2)}) collective-permute-start(bf16[64,640]{1,0:T(8,128)(2,1)} %param.5), channel_id=1, source_target_pairs={{0,6},{1,7},{2,0},{3,1},{4,2},{5,3},{6,4},{7,5},{8,14},{9,15},{10,... | collective-permute-start | bytes 245768 | tf_op jit(solution)/shard_map/ppermute | solution.py:74
  20.3 12.5 %collective-permute-start.10 = (bf16[128,2560]{1,0:T(8,128)(2,1)S(1)}, bf16[128,2560]{1,0:T(8,128)(2,1)S(1)}, u32[]{:S(2)}, u32[]{:S(2)}) collective-permute-start(bf16[128,2560]{1,0:T(8,128)(2,1)S(1)} %get-tuple-element.84), channel_id=1, source_target_pairs={{0,32},{1,9},{2,34},{3,11},{4,36},{5,13},{6,38},{7,15},{8,40},{9,1... | collective-permute-start | bytes 1966088 | tf_op jit(solution)/shard_map/ppermute | solution.py:70
  21.9 10.9 %collective-permute-start.11 = (bf16[128,2560]{1,0:T(8,128)(2,1)S(1)}, bf16[128,2560]{1,0:T(8,128)(2,1)S(1)}, u32[]{:S(2)}, u32[]{:S(2)}) collective-permute-start(bf16[128,2560]{1,0:T(8,128)(2,1)S(1)} %get-tuple-element.85), channel_id=1, source_target_pairs={{0,96},{1,25},{2,98},{3,27},{4,100},{5,29},{6,102},{7,31},{8,104},... | collective-permute-start | bytes 1966088 | tf_op jit(solution)/shard_map/ppermute | solution.py:70
  29.5 11.9 %collective-permute-start.8 = (bf16[128,2560]{1,0:T(8,128)(2,1)S(1)}, bf16[128,2560]{1,0:T(8,128)(2,1)S(1)}, u32[]{:S(2)}, u32[]{:S(2)}) collective-permute-start(bf16[128,2560]{1,0:T(8,128)(2,1)S(1)} %get-tuple-element.82), channel_id=1, source_target_pairs={{0,32},{1,9},{2,34},{3,11},{4,36},{5,13},{6,38},{7,15},{8,40},{9,1... | collective-permute-start | bytes 1966088 | tf_op jit(solution)/shard_map/ppermute | solution.py:70
  29.8 11.5 %collective-permute-start.9 = (bf16[128,2560]{1,0:T(8,128)(2,1)S(1)}, bf16[128,2560]{1,0:T(8,128)(2,1)S(1)}, u32[]{:S(2)}, u32[]{:S(2)}) collective-permute-start(bf16[128,2560]{1,0:T(8,128)(2,1)S(1)} %get-tuple-element.83), channel_id=1, source_target_pairs={{0,96},{1,25},{2,98},{3,27},{4,100},{5,29},{6,102},{7,31},{8,104},... | collective-permute-start | bytes 1966088 | tf_op jit(solution)/shard_map/ppermute | solution.py:70
  33.2 21.7 %collective-permute-start.15 = (bf16[128,5120]{1,0:T(8,128)(2,1)S(1)}, bf16[128,5120]{1,0:T(8,128)(2,1)S(1)}, u32[]{:S(2)}, u32[]{:S(2)}) collective-permute-start(bf16[128,5120]{1,0:T(8,128)(2,1)S(1)} %pad_maximum_fusion.1), channel_id=1, source_target_pairs={{0,96},{1,25},{2,98},{3,27},{4,100},{5,29},{6,102},{7,31},{8,104},... | collective-permute-start | bytes 3932168 | tf_op jit(solution)/shard_map/ppermute | solution.py:70
  36.1 19.3 %collective-permute-start.14 = (bf16[128,5120]{1,0:T(8,128)(2,1)S(1)}, bf16[128,5120]{1,0:T(8,128)(2,1)S(1)}, u32[]{:S(2)}, u32[]{:S(2)}) collective-permute-start(bf16[128,5120]{1,0:T(8,128)(2,1)S(1)} %pad_maximum_fusion), channel_id=1, source_target_pairs={{0,32},{1,9},{2,34},{3,11},{4,36},{5,13},{6,38},{7,15},{8,40},{9,1... | collective-permute-start | bytes 3932168 | tf_op jit(solution)/shard_map/ppermute | solution.py:70
  41.6 34.4 %collective-permute-start.13 = (bf16[128,5120]{1,0:T(8,128)(2,1)S(1)}, bf16[128,5120]{1,0:T(8,128)(2,1)S(1)}, u32[]{:S(2)}, u32[]{:S(2)}) collective-permute-start(bf16[128,5120]{1,0:T(8,128)(2,1)S(1)} %pad_maximum_fusion.3), channel_id=1, source_target_pairs={{0,96},{1,25},{2,98},{3,27},{4,100},{5,29},{6,102},{7,31},{8,104},... | collective-permute-start | bytes 3932168 | tf_op jit(solution)/shard_map/ppermute | solution.py:70
  45.2 31.2 %collective-permute-start.12 = (bf16[128,5120]{1,0:T(8,128)(2,1)S(1)}, bf16[128,5120]{1,0:T(8,128)(2,1)S(1)}, u32[]{:S(2)}, u32[]{:S(2)}) collective-permute-start(bf16[128,5120]{1,0:T(8,128)(2,1)S(1)} %pad_maximum_fusion.2), channel_id=1, source_target_pairs={{0,32},{1,9},{2,34},{3,11},{4,36},{5,13},{6,38},{7,15},{8,40},{9,1... | collective-permute-start | bytes 3932168 | tf_op jit(solution)/shard_map/ppermute | solution.py:70
  56.1 25.0 %collective-permute-start.21 = (bf16[32,5120]{1,0:T(8,128)(2,1)S(1)}, bf16[32,5120]{1,0:T(8,128)(2,1)S(1)}, u32[]{:S(2)}, u32[]{:S(2)}) collective-permute-start(bf16[32,5120]{1,0:T(8,128)(2,1)S(1)} %get-tuple-element.132), channel_id=1, source_target_pairs={{0,16},{1,65},{2,18},{3,67},{4,20},{5,69},{6,22},{7,71},{8,24},{9,... | collective-permute-start | bytes 983048 | tf_op jit(solution)/shard_map/ppermute | solution.py:70
  59.3 24.3 %collective-permute-start.20 = (bf16[32,5120]{1,0:T(8,128)(2,1)S(1)}, bf16[32,5120]{1,0:T(8,128)(2,1)S(1)}, u32[]{:S(2)}, u32[]{:S(2)}) collective-permute-start(bf16[32,5120]{1,0:T(8,128)(2,1)S(1)} %get-tuple-element.133), channel_id=1, source_target_pairs={{0,8},{1,33},{2,10},{3,35},{4,12},{5,37},{6,14},{7,39},{8,16},{9,4... | collective-permute-start | bytes 983048 | tf_op jit(solution)/shard_map/ppermute | solution.py:70
  60.0 23.6 %collective-permute-start.19 = (bf16[32,5120]{1,0:T(8,128)(2,1)S(1)}, bf16[32,5120]{1,0:T(8,128)(2,1)S(1)}, u32[]{:S(2)}, u32[]{:S(2)}) collective-permute-start(bf16[32,5120]{1,0:T(8,128)(2,1)S(1)} %get-tuple-element.134), channel_id=1, source_target_pairs={{0,24},{1,97},{2,26},{3,99},{4,28},{5,101},{6,30},{7,103},{8,0},{9... | collective-permute-start | bytes 983048 | tf_op jit(solution)/shard_map/ppermute | solution.py:70
  77.1 8.7 %collective-permute-start.18 = (bf16[32,5120]{1,0:T(8,128)(2,1)S(1)}, bf16[32,5120]{1,0:T(8,128)(2,1)S(1)}, u32[]{:S(2)}, u32[]{:S(2)}) collective-permute-start(bf16[32,5120]{1,0:T(8,128)(2,1)S(1)} %get-tuple-element.129), channel_id=1, source_target_pairs={{0,16},{1,65},{2,18},{3,67},{4,20},{5,69},{6,22},{7,71},{8,24},{9,... | collective-permute-start | bytes 983048 | tf_op jit(solution)/shard_map/ppermute | solution.py:70
  80.4 8.9 %collective-permute-start.17 = (bf16[32,5120]{1,0:T(8,128)(2,1)S(1)}, bf16[32,5120]{1,0:T(8,128)(2,1)S(1)}, u32[]{:S(2)}, u32[]{:S(2)}) collective-permute-start(bf16[32,5120]{1,0:T(8,128)(2,1)S(1)} %get-tuple-element.130), channel_id=1, source_target_pairs={{0,8},{1,33},{2,10},{3,35},{4,12},{5,37},{6,14},{7,39},{8,16},{9,4... | collective-permute-start | bytes 983048 | tf_op jit(solution)/shard_map/ppermute | solution.py:70
  90.1 8.8 %collective-permute-start.24 = (bf16[32,5120]{1,0:T(8,128)(2,1)S(1)}, bf16[32,5120]{1,0:T(8,128)(2,1)S(1)}, u32[]{:S(2)}, u32[]{:S(2)}) collective-permute-start(bf16[32,5120]{1,0:T(8,128)(2,1)S(1)} %fusion.5), channel_id=1, source_target_pairs={{0,16},{1,65},{2,18},{3,67},{4,20},{5,69},{6,22},{7,71},{8,24},{9,... | collective-permute-start | bytes 983048 | tf_op jit(solution)/shard_map/ppermute | solution.py:70
  92.2 10.0 %collective-permute-start.23 = (bf16[32,5120]{1,0:T(8,128)(2,1)S(1)}, bf16[32,5120]{1,0:T(8,128)(2,1)S(1)}, u32[]{:S(2)}, u32[]{:S(2)}) collective-permute-start(bf16[32,5120]{1,0:T(8,128)(2,1)S(1)} %fusion.5), channel_id=1, source_target_pairs={{0,8},{1,33},{2,10},{3,35},{4,12},{5,37},{6,14},{7,39},{8,16},{9,4... | collective-permute-start | bytes 983048 | tf_op jit(solution)/shard_map/ppermute | solution.py:70
  93.7 8.6 %collective-permute-start.22 = (bf16[32,5120]{1,0:T(8,128)(2,1)S(1)}, bf16[32,5120]{1,0:T(8,128)(2,1)S(1)}, u32[]{:S(2)}, u32[]{:S(2)}) collective-permute-start(bf16[32,5120]{1,0:T(8,128)(2,1)S(1)} %fusion.5), channel_id=1, source_target_pairs={{0,24},{1,97},{2,26},{3,99},{4,28},{5,101},{6,30},{7,103},{8,0},{9... | collective-permute-start | bytes 983048 | tf_op jit(solution)/shard_map/ppermute | solution.py:70
  95.4 11.5 %collective-permute-start.29 = (bf16[32,5120]{1,0:T(8,128)(2,1)S(1)}, bf16[32,5120]{1,0:T(8,128)(2,1)S(1)}, u32[]{:S(2)}, u32[]{:S(2)}) collective-permute-start(bf16[32,5120]{1,0:T(8,128)(2,1)S(1)} %get-tuple-element.127), channel_id=1, source_target_pairs={{0,16},{1,65},{2,18},{3,67},{4,20},{5,69},{6,22},{7,71},{8,24},{9,... | collective-permute-start | bytes 983048 | tf_op jit(solution)/shard_map/ppermute | solution.py:70
  95.7 16.4 %collective-permute-start.28 = (bf16[32,5120]{1,0:T(8,128)(2,1)S(1)}, bf16[32,5120]{1,0:T(8,128)(2,1)S(1)}, u32[]{:S(2)}, u32[]{:S(2)}) collective-permute-start(bf16[32,5120]{1,0:T(8,128)(2,1)S(1)} %get-tuple-element.127), channel_id=1, source_target_pairs={{0,8},{1,33},{2,10},{3,35},{4,12},{5,37},{6,14},{7,39},{8,16},{9,4... | collective-permute-start | bytes 983048 | tf_op jit(solution)/shard_map/ppermute | solution.py:70
  98.8 17.5 %collective-permute-start.27 = (bf16[32,5120]{1,0:T(8,128)(2,1)S(1)}, bf16[32,5120]{1,0:T(8,128)(2,1)S(1)}, u32[]{:S(2)}, u32[]{:S(2)}) collective-permute-start(bf16[32,5120]{1,0:T(8,128)(2,1)S(1)} %get-tuple-element.127), channel_id=1, source_target_pairs={{0,24},{1,97},{2,26},{3,99},{4,28},{5,101},{6,30},{7,103},{8,0},{9... | collective-permute-start | bytes 983048 | tf_op jit(solution)/shard_map/ppermute | solution.py:70
  102.4 19.0 %collective-permute-start.26 = (bf16[128,5120]{1,0:T(8,128)(2,1)S(1)}, bf16[128,5120]{1,0:T(8,128)(2,1)S(1)}, u32[]{:S(2)}, u32[]{:S(2)}) collective-permute-start(bf16[128,5120]{1,0:T(8,128)(2,1)S(1)} %pad_maximum_fusion.4.b0_ref), channel_id=1, source_target_pairs={{0,96},{1,25},{2,98},{3,27},{4,100},{5,29},{6,102},{7,31},{8,104},... | collective-permute-start | bytes 3932168 | tf_op jit(solution)/shard_map/ppermute | solution.py:70
  106.3 18.8 %collective-permute-start.25 = (bf16[128,5120]{1,0:T(8,128)(2,1)S(1)}, bf16[128,5120]{1,0:T(8,128)(2,1)S(1)}, u32[]{:S(2)}, u32[]{:S(2)}) collective-permute-start(bf16[128,5120]{1,0:T(8,128)(2,1)S(1)} %pad_maximum_fusion.4.b0_ref), channel_id=1, source_target_pairs={{0,32},{1,9},{2,34},{3,11},{4,36},{5,13},{6,38},{7,15},{8,40},{9,1... | collective-permute-start | bytes 3932168 | tf_op jit(solution)/shard_map/ppermute | solution.py:70
  116.4 19.7 %collective-permute-start.33 = (bf16[128,5120]{1,0:T(8,128)(2,1)S(1)}, bf16[128,5120]{1,0:T(8,128)(2,1)S(1)}, u32[]{:S(2)}, u32[]{:S(2)}) collective-permute-start(bf16[128,5120]{1,0:T(8,128)(2,1)S(1)} %pad_maximum_fusion.5.b0_ref), channel_id=1, source_target_pairs={{0,96},{1,25},{2,98},{3,27},{4,100},{5,29},{6,102},{7,31},{8,104},... | collective-permute-start | bytes 3932168 | tf_op jit(solution)/shard_map/ppermute | solution.py:70
  120.3 18.8 %collective-permute-start.32 = (bf16[128,5120]{1,0:T(8,128)(2,1)S(1)}, bf16[128,5120]{1,0:T(8,128)(2,1)S(1)}, u32[]{:S(2)}, u32[]{:S(2)}) collective-permute-start(bf16[128,5120]{1,0:T(8,128)(2,1)S(1)} %pad_maximum_fusion.5.b0_ref), channel_id=1, source_target_pairs={{0,32},{1,9},{2,34},{3,11},{4,36},{5,13},{6,38},{7,15},{8,40},{9,1... | collective-permute-start | bytes 3932168 | tf_op jit(solution)/shard_map/ppermute | solution.py:70
  125.2 20.6 %collective-permute-start.31 = (bf16[128,2560]{1,0:T(8,128)(2,1)S(1)}, bf16[128,2560]{1,0:T(8,128)(2,1)S(1)}, u32[]{:S(2)}, u32[]{:S(2)}) collective-permute-start(bf16[128,2560]{1,0:T(8,128)(2,1)S(1)} %slice.97), channel_id=1, source_target_pairs={{0,96},{1,25},{2,98},{3,27},{4,100},{5,29},{6,102},{7,31},{8,104},... | collective-permute-start | bytes 1966088 | tf_op jit(solution)/shard_map/ppermute | solution.py:70
  125.3 20.9 %collective-permute-start.30 = (bf16[128,2560]{1,0:T(8,128)(2,1)S(1)}, bf16[128,2560]{1,0:T(8,128)(2,1)S(1)}, u32[]{:S(2)}, u32[]{:S(2)}) collective-permute-start(bf16[128,2560]{1,0:T(8,128)(2,1)S(1)} %slice.96), channel_id=1, source_target_pairs={{0,32},{1,9},{2,34},{3,11},{4,36},{5,13},{6,38},{7,15},{8,40},{9,1... | collective-permute-start | bytes 1966088 | tf_op jit(solution)/shard_map/ppermute | solution.py:70
  139.2 13.0 %collective-permute-start.36 = (bf16[128,2560]{1,0:T(8,128)(2,1)S(1)}, bf16[128,2560]{1,0:T(8,128)(2,1)S(1)}, u32[]{:S(2)}, u32[]{:S(2)}) collective-permute-start(bf16[128,2560]{1,0:T(8,128)(2,1)S(1)} %slice.99), channel_id=1, source_target_pairs={{0,96},{1,25},{2,98},{3,27},{4,100},{5,29},{6,102},{7,31},{8,104},... | collective-permute-start | bytes 1966088 | tf_op jit(solution)/shard_map/ppermute | solution.py:70
  139.3 13.9 %collective-permute-start.35 = (bf16[128,2560]{1,0:T(8,128)(2,1)S(1)}, bf16[128,2560]{1,0:T(8,128)(2,1)S(1)}, u32[]{:S(2)}, u32[]{:S(2)}) collective-permute-start(bf16[128,2560]{1,0:T(8,128)(2,1)S(1)} %slice.98), channel_id=1, source_target_pairs={{0,32},{1,9},{2,34},{3,11},{4,36},{5,13},{6,38},{7,15},{8,40},{9,1... | collective-permute-start | bytes 1966088 | tf_op jit(solution)/shard_map/ppermute | solution.py:70
  153.3 10.6 %collective-permute-start.39 = (bf16[64,640]{1,0:T(8,128)(2,1)S(1)}, bf16[64,640]{1,0:T(8,128)(2,1)S(1)}, u32[]{:S(2)}, u32[]{:S(2)}) collective-permute-start(bf16[64,640]{1,0:T(8,128)(2,1)S(1)} %get-tuple-element.137), channel_id=1, source_target_pairs={{0,6},{1,7},{2,0},{3,1},{4,2},{5,3},{6,4},{7,5},{8,14},{9,15},{10,... | collective-permute-start | bytes 245768 | tf_op jit(solution)/shard_map/ppermute | solution.py:74
  154.9 9.0 %collective-permute-start.38 = (bf16[64,640]{1,0:T(8,128)(2,1)S(1)}, bf16[64,640]{1,0:T(8,128)(2,1)S(1)}, u32[]{:S(2)}, u32[]{:S(2)}) collective-permute-start(bf16[64,640]{1,0:T(8,128)(2,1)S(1)} %get-tuple-element.138), channel_id=1, source_target_pairs={{0,2},{1,3},{2,4},{3,5},{4,6},{5,7},{6,0},{7,1},{8,10},{9,11},{10,... | collective-permute-start | bytes 245768 | tf_op jit(solution)/shard_map/ppermute | solution.py:74
  (13 other events, 73.2 us)

commit v6 on v5

--- a/solution.py
+++ b/solution.py
@@ -44,8 +44,7 @@
     ("", "grad_w_in_left"),
     ("", "take_far"),
     ("", "sum_cores"),
-    ("", "grad_w_out"),
-    ("", "grad_w_in_right"),
+    ("", "last_grads"),
     ("", "sum_z"),
 )
 
@@ -287,6 +286,46 @@
     )(rows, half, near, *before)
 
 
+STEP = 1280
+
+
+def last_grads_kernel(c_ref, left_ref, right_ref, near_out_ref, x_ref, half_ref, near_in_ref, _, out_ref, in_ref):
+    side = jnp.where(pl.program_id(0) < HALF // STEP, left_ref[...], right_ref[...])
+    for rows, block, near_ref, target_ref in (
+        (side, c_ref[256:384], near_out_ref, out_ref),
+        (x_ref[256:384], half_ref[...], near_in_ref, in_ref),
+    ):
+        term = lax.dot_general(rows, block, (((0,), (0,)), ((), ())), preferred_element_type=F32)
+        target_ref[...] = (near_ref[...].astype(F32) + term).astype(BF16)
+
+
+def last_grads(c_all, far, near_out, x_all, half, near_in, before):
+    steps, cut = FFL // STEP, HALF // STEP
+    whole = pl.BlockSpec((TOK, WID), lambda i: (0, 0))
+    out_spec = pl.BlockSpec((STEP, WID), lambda i: (i, 0))
+    in_spec = pl.BlockSpec((WID, STEP // 2), lambda i: (0, steps + i))
+    return pl.pallas_call(
+        last_grads_kernel,
+        grid=(steps,),
+        out_shape=(jax.ShapeDtypeStruct((FFL, WID), BF16), jax.ShapeDtypeStruct((WID, FFL), BF16)),
+        in_specs=[
+            whole,
+            pl.BlockSpec((128, STEP), lambda i: (0, jnp.minimum(i, cut - 1))),
+            pl.BlockSpec((128, STEP), lambda i: (0, jnp.maximum(i - cut, 0))),
+            out_spec,
+            whole,
+            pl.BlockSpec((128, STEP // 2), lambda i: (0, i)),
+            in_spec,
+            pl.BlockSpec(memory_space=pl.ANY),
+        ],
+        out_specs=(out_spec, in_spec),
+        input_output_aliases={7: 1},
+        compiler_params=pltpu.CompilerParams(vmem_limit_bytes=LIMIT),
+        cost_estimate=pl.CostEstimate(flops=TOK * WID, bytes_accessed=TOK * WID, transcendentals=0),
+        name="last_grads",
+    )(c_all, *far, near_out, x_all, half, near_in, before)
+
+
 class Stream:
     def __init__(self, hidden, tokens, weight):
         self.hidden, self.own, self.weight = hidden, tokens, weight
@@ -395,18 +434,21 @@
         self.w_in_left = far_grad_w_in(rows, self.g_far[0], self.near_w_in, 0)
         return (self.w_in_left,)
 
-    def grad_w_in_right(self, env):
-        rows = env.after(self.h.rows)
-        self.w_in_result = far_grad_w_in(rows, self.g_far[1], self.near_w_in, TILES // 2, (self.w_in_left,))
-        return (self.w_in_result,)
-
     def take_far(self, env):
         self.h_far = self.h.far(env)
         return self.h_far
 
-    def grad_w_out(self, env):
-        self.w_out_result = weight_grads(True, env.after(self.g.rows), self.h_far, self.near_w_out)
-        return (self.w_out_result,)
+    def last_grads(self, env):
+        self.w_out_result, self.w_in_result = last_grads(
+            env.after(self.g.rows),
+            self.h_far,
+            self.near_w_out,
+            self.h.rows,
+            self.g_far[1],
+            self.near_w_in,
+            self.w_in_left,
+        )
+        return self.w_out_result, self.w_in_result
 
     def sum_cores(self, env):
         total = add(self.sums[0], env.after(self.swapped)).astype(BF16)

time: 168 us -> 167 us (level)
    pallas_call x0 -> x1, Pallas kernels: none -> 5.44 us  [last_grads(): pl.pallas_call(last_grads_kernel, grid=(steps,), out_shape=(jax.ShapeDtyp...]
    pallas_call x3 -> x2, Pallas kernels: 12.9 us -> 9.04 us  [weight_grads(): pl.pallas_call(functools.partial(far_weight_kernel if last else near_weig...]
    pallas_call x2 -> x1, Pallas kernels: 5.49 us -> 2.75 us  [far_grad_w_in(): pl.pallas_call(far_half_kernel, grid=(TILES // 2,), out_shape=jax.ShapeDt...]
  transfers between devices with their start and end apart: 40 -> 40, of which waited for: 19 -> 19; matrix products, arithmetic and copies ran while one was open for 3% -> 3% of each run, Pallas kernels for 23% -> 22%
where the time goes in v6:
time: 167 us; the launch traced here: 163 us
  starting transfers between devices  62.6 us (37%)
  waiting for transfers between devices  56.9 us (34%)
  Pallas kernels  36 us (22%)
  other arithmetic  4.08 us (2%)
  local copies, waits for them, and re-layouts  2.68 us (2%)
    ppermute x28, waiting for transfers between devices, hop(): return lax.ppermute(value, AXES, neighbours(move))  56.4 us
    ppermute x28, starting transfers between devices, hop(): return lax.ppermute(value, AXES, neighbours(move))  47.5 us
    ppermute x9, starting transfers between devices, hop_z(): lax.ppermute(value, AXES, neighbours(lambda x, y, z, c: (x, y, z + step,...  14.9 us
    pallas_call x2, Pallas kernels, partials(): pl.pallas_call(functools.partial(partial_kernel, hidden), grid=(TILES,),...  11.3 us
    pallas_call x2, Pallas kernels, weight_grads(): pl.pallas_call(functools.partial(far_weight_kernel if last else near_weig...  9.04 us
    pallas_call x2, Pallas kernels, input_grads(): pl.pallas_call(far_input_grads_kernel if last else near_input_grads_kerne...  7.46 us
    pallas_call x1, Pallas kernels, last_grads(): pl.pallas_call(last_grads_kernel, grid=(steps,), out_shape=(jax.ShapeDtyp...  5.44 us
  transfers between devices with their start and end apart: 40, of which 19 were waited for; matrix products, arithmetic and copies ran while one was open for 3% of the time, Pallas kernels for 22%

profile of v6, /device:TPU:0, one launch (start us, length us, event | category | flops | bytes accessed | tf_op | source)
XLA Modules:
  0.0 163.5 jit_solution(16558832715144652666)
XLA Ops:
  0.6 4.0 %collective-permute-start.1 = (bf16[64,640]{1,0:T(8,128)(2,1)}, bf16[64,640]{1,0:T(8,128)(2,1)S(1)}, u32[]{:S(2)}, u32[]{:S(2)}) collective-permute-start(bf16[64,640]{1,0:T(8,128)(2,1)} %param.4), channel_id=1, source_target_pairs={{0,4},{1,5},{2,6},{3,7},{4,0},{5,1},{6,2},{7,3},{8,12},{9,13},{10,... | collective-permute-start | bytes 245768 | tf_op jit(solution)/shard_map/ppermute | solution.py:73
  7.7 2.2 %collective-permute-start.5 = (bf16[64,640]{1,0:T(8,128)(2,1)}, bf16[64,640]{1,0:T(8,128)(2,1)S(1)}, u32[]{:S(2)}, u32[]{:S(2)}) collective-permute-start(bf16[64,640]{1,0:T(8,128)(2,1)} %param.5), channel_id=1, source_target_pairs={{0,6},{1,7},{2,0},{3,1},{4,2},{5,3},{6,4},{7,5},{8,14},{9,15},{10,... | collective-permute-start | bytes 245768 | tf_op jit(solution)/shard_map/ppermute | solution.py:73
  14.4 5.7 %hidden_partials.1 = (bf16[512,640]{1,0:T(8,128)(2,1)S(1)}, bf16[128,2560]{1,0:T(8,128)(2,1)S(1)}, bf16[128,2560]{1,0:T(8,128)(2,1)S(1)}, bf16[128,5120]{1,0:T(8...) custom-call(s32[16]{0:T(128)S(1)} %fusion.12.order_ref, ...), custom_call_target="tpu_custom_call" | custom-call | flops 3355443200 | bytes 11796480 | tf_op jit(solution)/shard_map/hidden_partials/pallas_call | solution.py:128
  23.8 5.6 %grad_partials.1 = (bf16[512,640]{1,0:T(8,128)(2,1)S(1)}, bf16[128,2560]{1,0:T(8,128)(2,1)S(1)}, bf16[128,2560]{1,0:T(8,128)(2,1)S(1)}, bf16[128,5120]{1,0:T(8,1...) custom-call(s32[16]{0:T(128)S(1)} %fusion.12.order_ref, ...), custom_call_target="tpu_custom_call" | custom-call | flops 3355443200 | bytes 11796480 | tf_op jit(solution)/shard_map/grad_partials/pallas_call | solution.py:128
  29.9 3.0 %collective-permute-start.9 = (bf16[128,2560]{1,0:T(8,128)(2,1)S(1)}, bf16[128,2560]{1,0:T(8,128)(2,1)S(1)}, u32[]{:S(2)}, u32[]{:S(2)}) collective-permute-start(bf16[128,2560]{1,0:T(8,128)(2,1)S(1)} %get-tuple-element.84), channel_id=1, source_target_pairs={{0,96},{1,25},{2,98},{3,27},{4,100},{5,29},{6,102},{7,31},{8,104},... | collective-permute-start | bytes 1966088 | tf_op jit(solution)/shard_map/ppermute | solution.py:69
  33.3 2.7 %collective-permute-start.15 = (bf16[128,5120]{1,0:T(8,128)(2,1)S(1)}, bf16[128,5120]{1,0:T(8,128)(2,1)S(1)}, u32[]{:S(2)}, u32[]{:S(2)}) collective-permute-start(bf16[128,5120]{1,0:T(8,128)(2,1)S(1)} %pad_maximum_fusion.1), channel_id=1, source_target_pairs={{0,96},{1,25},{2,98},{3,27},{4,100},{5,29},{6,102},{7,31},{8,104},... | collective-permute-start | bytes 3932168 | tf_op jit(solution)/shard_map/ppermute | solution.py:69
  36.2 5.2 %collective-permute-done.8 = bf16[128,2560]{1,0:T(8,128)(2,1)S(1)} collective-permute-done((bf16[128,2560]{1,0:T(8,128)(2,1)S(1)}, bf16[128,2560]{1,0:T(8,128)(2,1)S(1)}, u32[]{:S(2)}, u32[]{:S(2)}) %collective-permute-start.8) | collective-permute-done | bytes 655392 | tf_op jit(solution)/shard_map/ppermute | solution.py:69
  41.7 3.3 %collective-permute-start.13 = (bf16[128,5120]{1,0:T(8,128)(2,1)S(1)}, bf16[128,5120]{1,0:T(8,128)(2,1)S(1)}, u32[]{:S(2)}, u32[]{:S(2)}) collective-permute-start(bf16[128,5120]{1,0:T(8,128)(2,1)S(1)} %pad_maximum_fusion.3), channel_id=1, source_target_pairs={{0,96},{1,25},{2,98},{3,27},{4,100},{5,29},{6,102},{7,31},{8,104},... | collective-permute-start | bytes 3932168 | tf_op jit(solution)/shard_map/ppermute | solution.py:69
  45.4 9.6 %collective-permute-done.15 = bf16[128,5120]{1,0:T(8,128)(2,1)S(1)} collective-permute-done((bf16[128,5120]{1,0:T(8,128)(2,1)S(1)}, bf16[128,5120]{1,0:T(8,128)(2,1)S(1)}, u32[]{:S(2)}, u32[]{:S(2)}) %collective-permute-start.15) | collective-permute-done | bytes 1310752 | tf_op jit(solution)/shard_map/ppermute | solution.py:69
  56.1 3.3 %collective-permute-start.21 = (bf16[32,5120]{1,0:T(8,128)(2,1)S(1)}, bf16[32,5120]{1,0:T(8,128)(2,1)S(1)}, u32[]{:S(2)}, u32[]{:S(2)}) collective-permute-start(bf16[32,5120]{1,0:T(8,128)(2,1)S(1)} %get-tuple-element.134), channel_id=1, source_target_pairs={{0,16},{1,65},{2,18},{3,67},{4,20},{5,69},{6,22},{7,71},{8,24},{9,... | collective-permute-start | bytes 983048 | tf_op jit(solution)/shard_map/ppermute | solution.py:69
  60.0 2.6 %collective-permute-start.19 = (bf16[32,5120]{1,0:T(8,128)(2,1)S(1)}, bf16[32,5120]{1,0:T(8,128)(2,1)S(1)}, u32[]{:S(2)}, u32[]{:S(2)}) collective-permute-start(bf16[32,5120]{1,0:T(8,128)(2,1)S(1)} %get-tuple-element.136), channel_id=1, source_target_pairs={{0,24},{1,97},{2,26},{3,99},{4,28},{5,101},{6,30},{7,103},{8,0},{9... | collective-permute-start | bytes 983048 | tf_op jit(solution)/shard_map/ppermute | solution.py:69
  62.6 13.4 %collective-permute-done.13 = bf16[128,5120]{1,0:T(8,128)(2,1)S(1)} collective-permute-done((bf16[128,5120]{1,0:T(8,128)(2,1)S(1)}, bf16[128,5120]{1,0:T(8,128)(2,1)S(1)}, u32[]{:S(2)}, u32[]{:S(2)}) %collective-permute-start.13) | collective-permute-done | bytes 1310752 | tf_op jit(solution)/shard_map/ppermute | solution.py:69
  77.2 3.3 %collective-permute-start.18 = (bf16[32,5120]{1,0:T(8,128)(2,1)S(1)}, bf16[32,5120]{1,0:T(8,128)(2,1)S(1)}, u32[]{:S(2)}, u32[]{:S(2)}) collective-permute-start(bf16[32,5120]{1,0:T(8,128)(2,1)S(1)} %get-tuple-element.131), channel_id=1, source_target_pairs={{0,16},{1,65},{2,18},{3,67},{4,20},{5,69},{6,22},{7,71},{8,24},{9,... | collective-permute-start | bytes 983048 | tf_op jit(solution)/shard_map/ppermute | solution.py:69
  81.1 2.6 %collective-permute-start.16 = (bf16[32,5120]{1,0:T(8,128)(2,1)S(1)}, bf16[32,5120]{1,0:T(8,128)(2,1)S(1)}, u32[]{:S(2)}, u32[]{:S(2)}) collective-permute-start(bf16[32,5120]{1,0:T(8,128)(2,1)S(1)} %get-tuple-element.133), channel_id=1, source_target_pairs={{0,24},{1,97},{2,26},{3,99},{4,28},{5,101},{6,30},{7,103},{8,0},{9... | collective-permute-start | bytes 983048 | tf_op jit(solution)/shard_map/ppermute | solution.py:69
  84.0 1.9 %collective-permute-done.18 = bf16[32,5120]{1,0:T(8,128)(2,1)S(1)} collective-permute-done((bf16[32,5120]{1,0:T(8,128)(2,1)S(1)}, bf16[32,5120]{1,0:T(8,128)(2,1)S(1)}, u32[]{:S(2)}, u32[]{:S(2)}) %collective-permute-start.18) | collective-permute-done | bytes 327712 | tf_op jit(solution)/shard_map/ppermute | solution.py:69
  85.9 3.4 %collective-permute-done.17 = bf16[32,5120]{1,0:T(8,128)(2,1)S(1)} collective-permute-done((bf16[32,5120]{1,0:T(8,128)(2,1)S(1)}, bf16[32,5120]{1,0:T(8,128)(2,1)S(1)}, u32[]{:S(2)}, u32[]{:S(2)}) %collective-permute-start.17) | collective-permute-done | bytes 327712 | tf_op jit(solution)/shard_map/ppermute | solution.py:69
  90.1 2.2 %collective-permute-start.24 = (bf16[32,5120]{1,0:T(8,128)(2,1)S(1)}, bf16[32,5120]{1,0:T(8,128)(2,1)S(1)}, u32[]{:S(2)}, u32[]{:S(2)}) collective-permute-start(bf16[32,5120]{1,0:T(8,128)(2,1)S(1)} %fusion.5), channel_id=1, source_target_pairs={{0,16},{1,65},{2,18},{3,67},{4,20},{5,69},{6,22},{7,71},{8,24},{9,... | collective-permute-start | bytes 983048 | tf_op jit(solution)/shard_map/ppermute | solution.py:69
  98.9 2.7 %collective-permute-start.27 = (bf16[32,5120]{1,0:T(8,128)(2,1)S(1)}, bf16[32,5120]{1,0:T(8,128)(2,1)S(1)}, u32[]{:S(2)}, u32[]{:S(2)}) collective-permute-start(bf16[32,5120]{1,0:T(8,128)(2,1)S(1)} %get-tuple-element.129), channel_id=1, source_target_pairs={{0,24},{1,97},{2,26},{3,99},{4,28},{5,101},{6,30},{7,103},{8,0},{9... | collective-permute-start | bytes 983048 | tf_op jit(solution)/shard_map/ppermute | solution.py:69
  102.4 3.9 %collective-permute-start.26 = (bf16[128,5120]{1,0:T(8,128)(2,1)S(1)}, bf16[128,5120]{1,0:T(8,128)(2,1)S(1)}, u32[]{:S(2)}, u32[]{:S(2)}) collective-permute-start(bf16[128,5120]{1,0:T(8,128)(2,1)S(1)} %pad_maximum_fusion.4.b0_ref), channel_id=1, source_target_pairs={{0,96},{1,25},{2,98},{3,27},{4,100},{5,29},{6,102},{7,31},{8,104},... | collective-permute-start | bytes 3932168 | tf_op jit(solution)/shard_map/ppermute | solution.py:69
  107.0 5.2 %collective-permute-done.28 = bf16[32,5120]{1,0:T(8,128)(2,1)S(1)} collective-permute-done((bf16[32,5120]{1,0:T(8,128)(2,1)S(1)}, bf16[32,5120]{1,0:T(8,128)(2,1)S(1)}, u32[]{:S(2)}, u32[]{:S(2)}) %collective-permute-start.28) | collective-permute-done | bytes 327712 | tf_op jit(solution)/shard_map/ppermute | solution.py:69
  112.2 4.1 %collective-permute-done.27 = bf16[32,5120]{1,0:T(8,128)(2,1)S(1)} collective-permute-done((bf16[32,5120]{1,0:T(8,128)(2,1)S(1)}, bf16[32,5120]{1,0:T(8,128)(2,1)S(1)}, u32[]{:S(2)}, u32[]{:S(2)}) %collective-permute-start.27) | collective-permute-done | bytes 327712 | tf_op jit(solution)/shard_map/ppermute | solution.py:69
  116.4 3.9 %collective-permute-start.33 = (bf16[128,5120]{1,0:T(8,128)(2,1)S(1)}, bf16[128,5120]{1,0:T(8,128)(2,1)S(1)}, u32[]{:S(2)}, u32[]{:S(2)}) collective-permute-start(bf16[128,5120]{1,0:T(8,128)(2,1)S(1)} %pad_maximum_fusion.5.b0_ref), channel_id=1, source_target_pairs={{0,96},{1,25},{2,98},{3,27},{4,100},{5,29},{6,102},{7,31},{8,104},... | collective-permute-start | bytes 3932168 | tf_op jit(solution)/shard_map/ppermute | solution.py:69
  121.4 3.7 %collective-permute-done.25.b3_ref = bf16[128,5120]{1,0:T(8,128)(2,1)S(1)} collective-permute-done((bf16[128,5120]{1,0:T(8,128)(2,1)S(1)}, bf16[128,5120]{1,0:T(8,128)(2,1)S(1)}, u32[]{:S(2)}, u32[]{:S(2)}) %collective-permute-start.25) | collective-permute-done | bytes 1310752 | tf_op jit(solution)/shard_map/ppermute | solution.py:69
  125.3 2.0 %collective-permute-start.30 = (bf16[128,2560]{1,0:T(8,128)(2,1)S(1)}, bf16[128,2560]{1,0:T(8,128)(2,1)S(1)}, u32[]{:S(2)}, u32[]{:S(2)}) collective-permute-start(bf16[128,2560]{1,0:T(8,128)(2,1)S(1)} %slice.96), channel_id=1, source_target_pairs={{0,32},{1,9},{2,34},{3,11},{4,36},{5,13},{6,38},{7,15},{8,40},{9,1... | collective-permute-start | bytes 1966088 | tf_op jit(solution)/shard_map/ppermute | solution.py:69
  127.3 4.2 %near_input_grads.1.near_ref = f32[384,640]{1,0:T(8,128)S(1)} custom-call(bf16[640,5120]{1,0:T(8,128)(2,1)S(1)} %bitcast.15, bf16[128,5120]{1,0:T(8,128)(2,1)S(1)} %pad_maximum_fusion.4.b0_ref, bf16[128,5120]{1,0:T(8,128)(2,1)S(1)} %collective-permute-done.26.b1_ref, bf16[128,5120]{1,0:T(8,128)(2,1)S(1)} %collective-permute-done.25.b3_ref), custom_call_target="tpu_custom_call" | custom-call | flops 2516582400 | bytes 11796480 | tf_op jit(solution)/shard_map/near_input_grads/pallas_call | solution.py:211
  131.6 4.5 %near_grad_w_in.1.near_ref.near_in_ref = bf16[640,5120]{1,0:T(8,128)(2,1)S(1)} custom-call(bf16[512,640]{1,0:T(8,128)(2,1)S(1)} %get-tuple-element.114.rows_ref.x_ref, bf16[128,5120]{1,0:T(8,128)(2,1)S(1)} %pad_maximum_fusion.4.b0_ref, bf16[128,5120]{1,0:T(8,128)(2,1)S(1)} %collective-permute-done.26.b1_ref, bf16[128,5120]{1,0:T(8,128)(2,1)S(1)} %collective-permute-done.25.b3_ref), custom_call_target="tpu_custom_call" | custom-call | flops 327680 | bytes 327680 | tf_op jit(solution)/shard_map/near_grad_w_in/pallas_call | solution.py:248
  136.1 3.0 %collective-permute-done.32.b3_ref = bf16[128,5120]{1,0:T(8,128)(2,1)S(1)} collective-permute-done((bf16[128,5120]{1,0:T(8,128)(2,1)S(1)}, bf16[128,5120]{1,0:T(8,128)(2,1)S(1)}, u32[]{:S(2)}, u32[]{:S(2)}) %collective-permute-start.32) | collective-permute-done | bytes 1310752 | tf_op jit(solution)/shard_map/ppermute | solution.py:69
  139.4 2.0 %collective-permute-start.35 = (bf16[128,2560]{1,0:T(8,128)(2,1)S(1)}, bf16[128,2560]{1,0:T(8,128)(2,1)S(1)}, u32[]{:S(2)}, u32[]{:S(2)}) collective-permute-start(bf16[128,2560]{1,0:T(8,128)(2,1)S(1)} %slice.98), channel_id=1, source_target_pairs={{0,32},{1,9},{2,34},{3,11},{4,36},{5,13},{6,38},{7,15},{8,40},{9,1... | collective-permute-start | bytes 1966088 | tf_op jit(solution)/shard_map/ppermute | solution.py:69
  141.4 4.5 %near_grad_w_out.1.near_out_ref = bf16[5120,640]{1,0:T(8,128)(2,1)S(1)} custom-call(bf16[512,640]{1,0:T(8,128)(2,1)S(1)} %get-tuple-element.123.rows_ref.c_ref, bf16[128,5120]{1,0:T(8,128)(2,1)S(1)} %pad_maximum_fusion.5.b0_ref, bf16[128,5120]{1,0:T(8,128)(2,1)S(1)} %collective-permute-done.33.b1_ref, bf16[128,5120]{1,0:T(8,128)(2,1)S(1)} %collective-permute-done.32.b3_ref), custom_call_target="tpu_custom_call" | custom-call | flops 327680 | bytes 327680 | tf_op jit(solution)/shard_map/near_grad_w_out/pallas_call | solution.py:248
  146.2 3.2 %far_input_grads.1 = bf16[512,640]{1,0:T(8,128)(2,1)S(1)} custom-call(s32[16]{0:T(128)S(1)} %fusion.12.order_ref, bf16[640,5120]{1,0:T(8,128)(2,1)S(1)} %bitcast.15, bf16[128,2560]{1,0:T(8,128)(2,1)S(1)} %collective-permute-done.30.left_ref.b2_ref, bf16[128,2560]{1,0:T(8,128)(2,1)S(1)} %collective-permute-done.31.right_ref.half_ref, ...), custom_call_target="tpu_custom_call" | custom-call | flops 1677721600 | bytes 11796480 | tf_op jit(solution)/shard_map/far_input_grads/pallas_call | solution.py:211
  149.6 2.7 %far_grad_w_in.1._ = bf16[640,5120]{1,0:T(8,128)(2,1)} custom-call(bf16[512,640]{1,0:T(8,128)(2,1)S(1)} %get-tuple-element.114.rows_ref.x_ref, bf16[128,2560]{1,0:T(8,128)(2,1)S(1)} %collective-permute-done.30.left_ref.b2_ref, bf16[640,5120]{1,0:T(8,128)(2,1)S(1)} %near_grad_w_in.1.near_ref.near_in_ref), custom_call_target="tpu_custom_call" | custom-call | flops 327680 | bytes 327680 | tf_op jit(solution)/shard_map/far_grad_w_in/pallas_call | solution.py:271
  157.4 5.4 %last_grads.1 = (bf16[5120,640]{1,0:T(8,128)(2,1)}, bf16[640,5120]{1,0:T(8,128)(2,1)}) custom-call(bf16[512,640]{1,0:T(8,128)(2,1)S(1)} %get-tuple-element.123.rows_ref.c_ref, bf16[128,2560]{1,0:T(8,128)(2,1)S(1)} %collective-permute-done.35.left_ref, bf16[128,2560]{1,0:T(8,128)(2,1)S(1)} %collective-permute-done.36.right_ref, ...), custom_call_target="tpu_custom_call", output_to_operand_aliasing={{1}: (7, {})} | custom-call | flops 327680 | bytes 327680 | tf_op jit(solution)/shard_map/last_grads/pallas_call | solution.py:307
  (108 shorter events, 33.2 us)
Async XLA Ops:
  0.6 10.3 %collective-permute-start.1 = (bf16[64,640]{1,0:T(8,128)(2,1)}, bf16[64,640]{1,0:T(8,128)(2,1)S(1)}, u32[]{:S(2)}, u32[]{:S(2)}) collective-permute-start(bf16[64,640]{1,0:T(8,128)(2,1)} %param.4), channel_id=1, source_target_pairs={{0,4},{1,5},{2,6},{3,7},{4,0},{5,1},{6,2},{7,3},{8,12},{9,13},{10,... | collective-permute-start | bytes 245768 | tf_op jit(solution)/shard_map/ppermute | solution.py:73
  6.7 13.4 %collective-permute-start.4 = (bf16[64,640]{1,0:T(8,128)(2,1)}, bf16[64,640]{1,0:T(8,128)(2,1)S(1)}, u32[]{:S(2)}, u32[]{:S(2)}) collective-permute-start(bf16[64,640]{1,0:T(8,128)(2,1)} %param.5), channel_id=1, source_target_pairs={{0,2},{1,3},{2,4},{3,5},{4,6},{5,7},{6,0},{7,1},{8,10},{9,11},{10,... | collective-permute-start | bytes 245768 | tf_op jit(solution)/shard_map/ppermute | solution.py:73
  7.7 12.4 %collective-permute-start.5 = (bf16[64,640]{1,0:T(8,128)(2,1)}, bf16[64,640]{1,0:T(8,128)(2,1)S(1)}, u32[]{:S(2)}, u32[]{:S(2)}) collective-permute-start(bf16[64,640]{1,0:T(8,128)(2,1)} %param.5), channel_id=1, source_target_pairs={{0,6},{1,7},{2,0},{3,1},{4,2},{5,3},{6,4},{7,5},{8,14},{9,15},{10,... | collective-permute-start | bytes 245768 | tf_op jit(solution)/shard_map/ppermute | solution.py:73
  20.4 12.5 %collective-permute-start.10 = (bf16[128,2560]{1,0:T(8,128)(2,1)S(1)}, bf16[128,2560]{1,0:T(8,128)(2,1)S(1)}, u32[]{:S(2)}, u32[]{:S(2)}) collective-permute-start(bf16[128,2560]{1,0:T(8,128)(2,1)S(1)} %get-tuple-element.85), channel_id=1, source_target_pairs={{0,32},{1,9},{2,34},{3,11},{4,36},{5,13},{6,38},{7,15},{8,40},{9,1... | collective-permute-start | bytes 1966088 | tf_op jit(solution)/shard_map/ppermute | solution.py:69
  21.9 10.9 %collective-permute-start.11 = (bf16[128,2560]{1,0:T(8,128)(2,1)S(1)}, bf16[128,2560]{1,0:T(8,128)(2,1)S(1)}, u32[]{:S(2)}, u32[]{:S(2)}) collective-permute-start(bf16[128,2560]{1,0:T(8,128)(2,1)S(1)} %get-tuple-element.86), channel_id=1, source_target_pairs={{0,96},{1,25},{2,98},{3,27},{4,100},{5,29},{6,102},{7,31},{8,104},... | collective-permute-start | bytes 1966088 | tf_op jit(solution)/shard_map/ppermute | solution.py:69
  29.5 11.9 %collective-permute-start.8 = (bf16[128,2560]{1,0:T(8,128)(2,1)S(1)}, bf16[128,2560]{1,0:T(8,128)(2,1)S(1)}, u32[]{:S(2)}, u32[]{:S(2)}) collective-permute-start(bf16[128,2560]{1,0:T(8,128)(2,1)S(1)} %get-tuple-element.83), channel_id=1, source_target_pairs={{0,32},{1,9},{2,34},{3,11},{4,36},{5,13},{6,38},{7,15},{8,40},{9,1... | collective-permute-start | bytes 1966088 | tf_op jit(solution)/shard_map/ppermute | solution.py:69
  29.9 11.5 %collective-permute-start.9 = (bf16[128,2560]{1,0:T(8,128)(2,1)S(1)}, bf16[128,2560]{1,0:T(8,128)(2,1)S(1)}, u32[]{:S(2)}, u32[]{:S(2)}) collective-permute-start(bf16[128,2560]{1,0:T(8,128)(2,1)S(1)} %get-tuple-element.84), channel_id=1, source_target_pairs={{0,96},{1,25},{2,98},{3,27},{4,100},{5,29},{6,102},{7,31},{8,104},... | collective-permute-start | bytes 1966088 | tf_op jit(solution)/shard_map/ppermute | solution.py:69
  33.3 21.7 %collective-permute-start.15 = (bf16[128,5120]{1,0:T(8,128)(2,1)S(1)}, bf16[128,5120]{1,0:T(8,128)(2,1)S(1)}, u32[]{:S(2)}, u32[]{:S(2)}) collective-permute-start(bf16[128,5120]{1,0:T(8,128)(2,1)S(1)} %pad_maximum_fusion.1), channel_id=1, source_target_pairs={{0,96},{1,25},{2,98},{3,27},{4,100},{5,29},{6,102},{7,31},{8,104},... | collective-permute-start | bytes 3932168 | tf_op jit(solution)/shard_map/ppermute | solution.py:69
  36.1 19.3 %collective-permute-start.14 = (bf16[128,5120]{1,0:T(8,128)(2,1)S(1)}, bf16[128,5120]{1,0:T(8,128)(2,1)S(1)}, u32[]{:S(2)}, u32[]{:S(2)}) collective-permute-start(bf16[128,5120]{1,0:T(8,128)(2,1)S(1)} %pad_maximum_fusion), channel_id=1, source_target_pairs={{0,32},{1,9},{2,34},{3,11},{4,36},{5,13},{6,38},{7,15},{8,40},{9,1... | collective-permute-start | bytes 3932168 | tf_op jit(solution)/shard_map/ppermute | solution.py:69
  41.7 34.3 %collective-permute-start.13 = (bf16[128,5120]{1,0:T(8,128)(2,1)S(1)}, bf16[128,5120]{1,0:T(8,128)(2,1)S(1)}, u32[]{:S(2)}, u32[]{:S(2)}) collective-permute-start(bf16[128,5120]{1,0:T(8,128)(2,1)S(1)} %pad_maximum_fusion.3), channel_id=1, source_target_pairs={{0,96},{1,25},{2,98},{3,27},{4,100},{5,29},{6,102},{7,31},{8,104},... | collective-permute-start | bytes 3932168 | tf_op jit(solution)/shard_map/ppermute | solution.py:69
  45.3 31.2 %collective-permute-start.12 = (bf16[128,5120]{1,0:T(8,128)(2,1)S(1)}, bf16[128,5120]{1,0:T(8,128)(2,1)S(1)}, u32[]{:S(2)}, u32[]{:S(2)}) collective-permute-start(bf16[128,5120]{1,0:T(8,128)(2,1)S(1)} %pad_maximum_fusion.2), channel_id=1, source_target_pairs={{0,32},{1,9},{2,34},{3,11},{4,36},{5,13},{6,38},{7,15},{8,40},{9,1... | collective-permute-start | bytes 3932168 | tf_op jit(solution)/shard_map/ppermute | solution.py:69
  56.1 25.0 %collective-permute-start.21 = (bf16[32,5120]{1,0:T(8,128)(2,1)S(1)}, bf16[32,5120]{1,0:T(8,128)(2,1)S(1)}, u32[]{:S(2)}, u32[]{:S(2)}) collective-permute-start(bf16[32,5120]{1,0:T(8,128)(2,1)S(1)} %get-tuple-element.134), channel_id=1, source_target_pairs={{0,16},{1,65},{2,18},{3,67},{4,20},{5,69},{6,22},{7,71},{8,24},{9,... | collective-permute-start | bytes 983048 | tf_op jit(solution)/shard_map/ppermute | solution.py:69
  59.4 24.3 %collective-permute-start.20 = (bf16[32,5120]{1,0:T(8,128)(2,1)S(1)}, bf16[32,5120]{1,0:T(8,128)(2,1)S(1)}, u32[]{:S(2)}, u32[]{:S(2)}) collective-permute-start(bf16[32,5120]{1,0:T(8,128)(2,1)S(1)} %get-tuple-element.135), channel_id=1, source_target_pairs={{0,8},{1,33},{2,10},{3,35},{4,12},{5,37},{6,14},{7,39},{8,16},{9,4... | collective-permute-start | bytes 983048 | tf_op jit(solution)/shard_map/ppermute | solution.py:69
  60.0 23.6 %collective-permute-start.19 = (bf16[32,5120]{1,0:T(8,128)(2,1)S(1)}, bf16[32,5120]{1,0:T(8,128)(2,1)S(1)}, u32[]{:S(2)}, u32[]{:S(2)}) collective-permute-start(bf16[32,5120]{1,0:T(8,128)(2,1)S(1)} %get-tuple-element.136), channel_id=1, source_target_pairs={{0,24},{1,97},{2,26},{3,99},{4,28},{5,101},{6,30},{7,103},{8,0},{9... | collective-permute-start | bytes 983048 | tf_op jit(solution)/shard_map/ppermute | solution.py:69
  77.2 8.7 %collective-permute-start.18 = (bf16[32,5120]{1,0:T(8,128)(2,1)S(1)}, bf16[32,5120]{1,0:T(8,128)(2,1)S(1)}, u32[]{:S(2)}, u32[]{:S(2)}) collective-permute-start(bf16[32,5120]{1,0:T(8,128)(2,1)S(1)} %get-tuple-element.131), channel_id=1, source_target_pairs={{0,16},{1,65},{2,18},{3,67},{4,20},{5,69},{6,22},{7,71},{8,24},{9,... | collective-permute-start | bytes 983048 | tf_op jit(solution)/shard_map/ppermute | solution.py:69
  80.4 8.9 %collective-permute-start.17 = (bf16[32,5120]{1,0:T(8,128)(2,1)S(1)}, bf16[32,5120]{1,0:T(8,128)(2,1)S(1)}, u32[]{:S(2)}, u32[]{:S(2)}) collective-permute-start(bf16[32,5120]{1,0:T(8,128)(2,1)S(1)} %get-tuple-element.132), channel_id=1, source_target_pairs={{0,8},{1,33},{2,10},{3,35},{4,12},{5,37},{6,14},{7,39},{8,16},{9,4... | collective-permute-start | bytes 983048 | tf_op jit(solution)/shard_map/ppermute | solution.py:69
  81.1 8.6 %collective-permute-start.16 = (bf16[32,5120]{1,0:T(8,128)(2,1)S(1)}, bf16[32,5120]{1,0:T(8,128)(2,1)S(1)}, u32[]{:S(2)}, u32[]{:S(2)}) collective-permute-start(bf16[32,5120]{1,0:T(8,128)(2,1)S(1)} %get-tuple-element.133), channel_id=1, source_target_pairs={{0,24},{1,97},{2,26},{3,99},{4,28},{5,101},{6,30},{7,103},{8,0},{9... | collective-permute-start | bytes 983048 | tf_op jit(solution)/shard_map/ppermute | solution.py:69
  90.1 8.8 %collective-permute-start.24 = (bf16[32,5120]{1,0:T(8,128)(2,1)S(1)}, bf16[32,5120]{1,0:T(8,128)(2,1)S(1)}, u32[]{:S(2)}, u32[]{:S(2)}) collective-permute-start(bf16[32,5120]{1,0:T(8,128)(2,1)S(1)} %fusion.5), channel_id=1, source_target_pairs={{0,16},{1,65},{2,18},{3,67},{4,20},{5,69},{6,22},{7,71},{8,24},{9,... | collective-permute-start | bytes 983048 | tf_op jit(solution)/shard_map/ppermute | solution.py:69
  92.3 10.0 %collective-permute-start.23 = (bf16[32,5120]{1,0:T(8,128)(2,1)S(1)}, bf16[32,5120]{1,0:T(8,128)(2,1)S(1)}, u32[]{:S(2)}, u32[]{:S(2)}) collective-permute-start(bf16[32,5120]{1,0:T(8,128)(2,1)S(1)} %fusion.5), channel_id=1, source_target_pairs={{0,8},{1,33},{2,10},{3,35},{4,12},{5,37},{6,14},{7,39},{8,16},{9,4... | collective-permute-start | bytes 983048 | tf_op jit(solution)/shard_map/ppermute | solution.py:69
  93.7 8.6 %collective-permute-start.22 = (bf16[32,5120]{1,0:T(8,128)(2,1)S(1)}, bf16[32,5120]{1,0:T(8,128)(2,1)S(1)}, u32[]{:S(2)}, u32[]{:S(2)}) collective-permute-start(bf16[32,5120]{1,0:T(8,128)(2,1)S(1)} %fusion.5), channel_id=1, source_target_pairs={{0,24},{1,97},{2,26},{3,99},{4,28},{5,101},{6,30},{7,103},{8,0},{9... | collective-permute-start | bytes 983048 | tf_op jit(solution)/shard_map/ppermute | solution.py:69
  95.5 11.5 %collective-permute-start.29 = (bf16[32,5120]{1,0:T(8,128)(2,1)S(1)}, bf16[32,5120]{1,0:T(8,128)(2,1)S(1)}, u32[]{:S(2)}, u32[]{:S(2)}) collective-permute-start(bf16[32,5120]{1,0:T(8,128)(2,1)S(1)} %get-tuple-element.129), channel_id=1, source_target_pairs={{0,16},{1,65},{2,18},{3,67},{4,20},{5,69},{6,22},{7,71},{8,24},{9,... | collective-permute-start | bytes 983048 | tf_op jit(solution)/shard_map/ppermute | solution.py:69
  95.8 16.4 %collective-permute-start.28 = (bf16[32,5120]{1,0:T(8,128)(2,1)S(1)}, bf16[32,5120]{1,0:T(8,128)(2,1)S(1)}, u32[]{:S(2)}, u32[]{:S(2)}) collective-permute-start(bf16[32,5120]{1,0:T(8,128)(2,1)S(1)} %get-tuple-element.129), channel_id=1, source_target_pairs={{0,8},{1,33},{2,10},{3,35},{4,12},{5,37},{6,14},{7,39},{8,16},{9,4... | collective-permute-start | bytes 983048 | tf_op jit(solution)/shard_map/ppermute | solution.py:69
  98.9 17.5 %collective-permute-start.27 = (bf16[32,5120]{1,0:T(8,128)(2,1)S(1)}, bf16[32,5120]{1,0:T(8,128)(2,1)S(1)}, u32[]{:S(2)}, u32[]{:S(2)}) collective-permute-start(bf16[32,5120]{1,0:T(8,128)(2,1)S(1)} %get-tuple-element.129), channel_id=1, source_target_pairs={{0,24},{1,97},{2,26},{3,99},{4,28},{5,101},{6,30},{7,103},{8,0},{9... | collective-permute-start | bytes 983048 | tf_op jit(solution)/shard_map/ppermute | solution.py:69
  102.4 19.0 %collective-permute-start.26 = (bf16[128,5120]{1,0:T(8,128)(2,1)S(1)}, bf16[128,5120]{1,0:T(8,128)(2,1)S(1)}, u32[]{:S(2)}, u32[]{:S(2)}) collective-permute-start(bf16[128,5120]{1,0:T(8,128)(2,1)S(1)} %pad_maximum_fusion.4.b0_ref), channel_id=1, source_target_pairs={{0,96},{1,25},{2,98},{3,27},{4,100},{5,29},{6,102},{7,31},{8,104},... | collective-permute-start | bytes 3932168 | tf_op jit(solution)/shard_map/ppermute | solution.py:69
  106.3 18.8 %collective-permute-start.25 = (bf16[128,5120]{1,0:T(8,128)(2,1)S(1)}, bf16[128,5120]{1,0:T(8,128)(2,1)S(1)}, u32[]{:S(2)}, u32[]{:S(2)}) collective-permute-start(bf16[128,5120]{1,0:T(8,128)(2,1)S(1)} %pad_maximum_fusion.4.b0_ref), channel_id=1, source_target_pairs={{0,32},{1,9},{2,34},{3,11},{4,36},{5,13},{6,38},{7,15},{8,40},{9,1... | collective-permute-start | bytes 3932168 | tf_op jit(solution)/shard_map/ppermute | solution.py:69
  116.4 19.7 %collective-permute-start.33 = (bf16[128,5120]{1,0:T(8,128)(2,1)S(1)}, bf16[128,5120]{1,0:T(8,128)(2,1)S(1)}, u32[]{:S(2)}, u32[]{:S(2)}) collective-permute-start(bf16[128,5120]{1,0:T(8,128)(2,1)S(1)} %pad_maximum_fusion.5.b0_ref), channel_id=1, source_target_pairs={{0,96},{1,25},{2,98},{3,27},{4,100},{5,29},{6,102},{7,31},{8,104},... | collective-permute-start | bytes 3932168 | tf_op jit(solution)/shard_map/ppermute | solution.py:69
  120.4 18.8 %collective-permute-start.32 = (bf16[128,5120]{1,0:T(8,128)(2,1)S(1)}, bf16[128,5120]{1,0:T(8,128)(2,1)S(1)}, u32[]{:S(2)}, u32[]{:S(2)}) collective-permute-start(bf16[128,5120]{1,0:T(8,128)(2,1)S(1)} %pad_maximum_fusion.5.b0_ref), channel_id=1, source_target_pairs={{0,32},{1,9},{2,34},{3,11},{4,36},{5,13},{6,38},{7,15},{8,40},{9,1... | collective-permute-start | bytes 3932168 | tf_op jit(solution)/shard_map/ppermute | solution.py:69
  125.2 20.7 %collective-permute-start.31 = (bf16[128,2560]{1,0:T(8,128)(2,1)S(1)}, bf16[128,2560]{1,0:T(8,128)(2,1)S(1)}, u32[]{:S(2)}, u32[]{:S(2)}) collective-permute-start(bf16[128,2560]{1,0:T(8,128)(2,1)S(1)} %slice.97), channel_id=1, source_target_pairs={{0,96},{1,25},{2,98},{3,27},{4,100},{5,29},{6,102},{7,31},{8,104},... | collective-permute-start | bytes 1966088 | tf_op jit(solution)/shard_map/ppermute | solution.py:69
  125.3 20.9 %collective-permute-start.30 = (bf16[128,2560]{1,0:T(8,128)(2,1)S(1)}, bf16[128,2560]{1,0:T(8,128)(2,1)S(1)}, u32[]{:S(2)}, u32[]{:S(2)}) collective-permute-start(bf16[128,2560]{1,0:T(8,128)(2,1)S(1)} %slice.96), channel_id=1, source_target_pairs={{0,32},{1,9},{2,34},{3,11},{4,36},{5,13},{6,38},{7,15},{8,40},{9,1... | collective-permute-start | bytes 1966088 | tf_op jit(solution)/shard_map/ppermute | solution.py:69
  139.3 13.1 %collective-permute-start.36 = (bf16[128,2560]{1,0:T(8,128)(2,1)S(1)}, bf16[128,2560]{1,0:T(8,128)(2,1)S(1)}, u32[]{:S(2)}, u32[]{:S(2)}) collective-permute-start(bf16[128,2560]{1,0:T(8,128)(2,1)S(1)} %slice.99), channel_id=1, source_target_pairs={{0,96},{1,25},{2,98},{3,27},{4,100},{5,29},{6,102},{7,31},{8,104},... | collective-permute-start | bytes 1966088 | tf_op jit(solution)/shard_map/ppermute | solution.py:69
  139.4 13.9 %collective-permute-start.35 = (bf16[128,2560]{1,0:T(8,128)(2,1)S(1)}, bf16[128,2560]{1,0:T(8,128)(2,1)S(1)}, u32[]{:S(2)}, u32[]{:S(2)}) collective-permute-start(bf16[128,2560]{1,0:T(8,128)(2,1)S(1)} %slice.98), channel_id=1, source_target_pairs={{0,32},{1,9},{2,34},{3,11},{4,36},{5,13},{6,38},{7,15},{8,40},{9,1... | collective-permute-start | bytes 1966088 | tf_op jit(solution)/shard_map/ppermute | solution.py:69
  153.3 9.5 %collective-permute-start.39 = (bf16[64,640]{1,0:T(8,128)(2,1)S(1)}, bf16[64,640]{1,0:T(8,128)(2,1)S(1)}, u32[]{:S(2)}, u32[]{:S(2)}) collective-permute-start(bf16[64,640]{1,0:T(8,128)(2,1)S(1)} %get-tuple-element.139), channel_id=1, source_target_pairs={{0,6},{1,7},{2,0},{3,1},{4,2},{5,3},{6,4},{7,5},{8,14},{9,15},{10,... | collective-permute-start | bytes 245768 | tf_op jit(solution)/shard_map/ppermute | solution.py:73
  (13 other events, 71.4 us)
